TPU v7x, 32 devices: a whole 2x2x4 slice. The times are simulated.
32 devices in a mesh: seq: 8 (over z, x), fsdp: 4 (over y, core).
Axes of the slice: x: 2, y: 2, z: 4, core: 2. Of those that a mesh axis runs over, the one named last changes fastest.
Arguments:
- tokens: bfloat16 [8, 1024, 1024], P('fsdp', 'seq'), may hold values from -6 to 6
- resets: int32 [8, 1024], P('fsdp', 'seq'), may hold values 0 or 1
- pre_gain: float32 [1024], replicated, may hold values from 0.5 to 1.5
- query_weight: bfloat16 [1024, 1024], P('fsdp'), may hold values from -0.1875 to 0.1875
- key_weight: bfloat16 [1024, 1024], P('fsdp'), may hold values from -0.1875 to 0.1875
- value_weight: bfloat16 [1024, 1024], P('fsdp'), may hold values from -0.1875 to 0.1875
- forget_weight: bfloat16 [1024, 256], P('fsdp'), may hold values from -0.1875 to 0.1875
- forget_bias: float32 [256], replicated, may hold values from -1 to 9
- outgate_weight: bfloat16 [1024, 1024], P('fsdp'), may hold values from -0.1875 to 0.1875
- output_weight: bfloat16 [1024, 1024], P('fsdp'), may hold values from -0.1875 to 0.1875
- head_gain: float32 [256], replicated, may hold values from 0.5 to 1.5
- post_gain: float32 [1024], replicated, may hold values from 0.5 to 1.5
- gate_weight: bfloat16 [1024, 2816], P('fsdp'), may hold values from -0.1875 to 0.1875
- up_weight: bfloat16 [1024, 2816], P('fsdp'), may hold values from -0.1875 to 0.1875
- down_weight: bfloat16 [2816, 1024], P('fsdp'), may hold values from -0.109375 to 0.109375
- cotangent: bfloat16 [8, 1024, 1024], P('fsdp', 'seq'), may hold values from -6 to 6
Outputs:
- block_output: bfloat16 [8, 1024, 1024], P('fsdp', 'seq')
- input_grad: bfloat16 [8, 1024, 1024], P('fsdp', 'seq')
- pregain_grad: float32 [1024], replicated
- query_grad: float32 [1024, 1024], P(('seq', 'fsdp'))
- key_grad: float32 [1024, 1024], P(('seq', 'fsdp'))
- value_grad: float32 [1024, 1024], P(('seq', 'fsdp'))
- forget_grad: float32 [1024, 256], P(('seq', 'fsdp'))
- bias_grad: float32 [256], replicated
- outgate_grad: float32 [1024, 1024], P(('seq', 'fsdp'))
- output_grad: float32 [1024, 1024], P(('seq', 'fsdp'))
- headgain_grad: float32 [256], replicated
- postgain_grad: float32 [1024], replicated
- gate_grad: float32 [1024, 2816], P(('seq', 'fsdp'))
- up_grad: float32 [1024, 2816], P(('seq', 'fsdp'))
- down_grad: float32 [2816, 1024], P(('seq', 'fsdp'))
Inputs may be any that keep to these rules, and one draw needn't show every extreme that they name: `resets`: 1 marks the first position of a document; documents may cross devices and span many of them.
All inputs are finite; a program needn't handle non-finite values.
Results may differ from a plain program's by a relative error of at most 0.015.
Values may be sent and summed in bfloat16 or wider, within the bound.
A program may use at most 120 MiB of HBM per device.

v0:
```python
import jax
import jax.numpy as jnp
from jax import lax
from jax.sharding import PartitionSpec as P

GROUP = 64


highest = lax.Precision.HIGHEST
norm_eps = 1e-06
gate_scale = 8.0


def entering(x, axis, combine, identity):
    size, place = (lax.axis_size(axis), lax.axis_index(axis))
    everything = jax.tree.map(
        lambda part, kind: lax.all_gather(part.astype(kind), axis),
        x,
        (jnp.bfloat16, jnp.bfloat16, jnp.bfloat16),
    )
    start = jax.tree.map(
        lambda part, zero: jnp.broadcast_to(jnp.asarray(zero, part.dtype), part.shape), x, identity
    )

    def entering_turn(k, before):
        reached = k < place
        new = combine(
            before, jax.tree.map(lambda part, own: part[k].astype(own.dtype), everything, x)
        )
        return jax.tree.map(lambda a, b: jnp.where(reached, a, b), new, before)

    return lax.fori_loop(0, size, entering_turn, start)


def carried_in(x, axis, combine, identity):
    size, place = (lax.axis_size(axis), lax.axis_index(axis))
    everything = jax.tree.map(
        lambda part, kind: lax.all_gather(part.astype(kind), axis),
        x,
        jax.tree.map(lambda a: jnp.bfloat16 if a.dtype == jnp.float32 else a.dtype, x),
    )
    start = jax.tree.map(
        lambda part, zero: jnp.broadcast_to(jnp.asarray(zero, part.dtype), part.shape), x, identity
    )

    def carried_turn(k, before):
        at = size - 1 - k
        reached = at > place
        new = combine(
            before, jax.tree.map(lambda part, own: part[at].astype(own.dtype), everything, x)
        )
        return jax.tree.map(lambda a, b: jnp.where(reached, a, b), new, before)

    return lax.fori_loop(0, size, carried_turn, start)


def rms_norm(values, gain):
    return values * lax.rsqrt(jnp.mean(values * values, axis=-1, keepdims=True) + norm_eps) * gain


def slot_block(carry, block):
    key_state, value_state = carry
    queries, keys_in, values_in, log_gates, flags = block
    scale = queries.shape[-1] ** (-0.5)
    length = queries.shape[0]
    decay_sum = jnp.cumsum(log_gates, axis=0)
    resets_seen = jnp.cumsum(flags)
    places = jnp.arange(length)
    linked = (
        (resets_seen[:, None] == resets_seen[None, :]) & (places[:, None] >= places[None, :])
    ).astype(jnp.float32)
    fresh = (resets_seen == 0).astype(jnp.float32)
    ending = (resets_seen == resets_seen[-1]).astype(jnp.float32)
    growth = jnp.exp(decay_sum)
    shrink = jnp.exp(-decay_sum) * -jnp.expm1(log_gates)
    affinity = (
        jnp.einsum("thd,shd->hts", queries, keys_in, precision=highest) * (scale * linked)[None]
    )
    inner = jnp.einsum("hts,shi->thi", affinity, shrink, precision=highest)
    carried = (
        jnp.einsum("thd,hid->thi", queries, key_state, precision=highest)
        * (scale * fresh)[:, None, None]
    )
    scores = growth * (inner + carried)
    weights = jax.nn.softmax(scores, axis=-1)
    lifted = weights * growth
    mixing = jnp.einsum("thi,shi->hts", lifted, shrink, precision=highest) * linked[None]
    outputs = jnp.einsum("hts,shd->thd", mixing, values_in, precision=highest)
    outputs = (
        outputs
        + jnp.einsum("thi,hid->thd", lifted, value_state, precision=highest) * fresh[:, None, None]
    )
    last_growth = growth[-1][:, :, None]
    kept = shrink * ending[:, None, None]
    key_next = last_growth * (
        fresh[-1] * key_state + jnp.einsum("shi,shd->hid", kept, keys_in, precision=highest)
    )
    value_next = last_growth * (
        fresh[-1] * value_state + jnp.einsum("shi,shd->hid", kept, values_in, precision=highest)
    )
    return ((key_next, value_next), outputs)


def state_block(carry, block):
    key_state, value_state = carry
    keys_in, values_in, log_gates, flags = block
    decay_sum = jnp.cumsum(log_gates, axis=0)
    resets_seen = jnp.cumsum(flags)
    ending = (resets_seen == resets_seen[-1]).astype(jnp.float32)
    kept_last = (resets_seen[-1] == 0).astype(jnp.float32)
    kept = jnp.exp(-decay_sum) * -jnp.expm1(log_gates) * ending[:, None, None]
    last_growth = jnp.exp(decay_sum[-1])[:, :, None]
    key_next = last_growth * (
        kept_last * key_state + jnp.einsum("shi,shd->hid", kept, keys_in, precision=highest)
    )
    value_next = last_growth * (
        kept_last * value_state + jnp.einsum("shi,shd->hid", kept, values_in, precision=highest)
    )
    return ((key_next, value_next), None)


def split_blocks(array):
    count = array.shape[0] // GROUP
    return array.reshape((count, GROUP) + array.shape[1:])


def slot_attention(queries, keys_in, values_in, log_gates, flags, key_state, value_state):
    blocks = (
        split_blocks(queries),
        split_blocks(keys_in),
        split_blocks(values_in),
        split_blocks(log_gates),
        split_blocks(flags),
    )
    final, outputs = lax.scan(jax.checkpoint(slot_block), (key_state, value_state), blocks)
    return (outputs.reshape(queries.shape), final)


def local_state(keys_in, values_in, log_gates, flags):
    zeros = jnp.zeros((keys_in.shape[1], log_gates.shape[2], keys_in.shape[2]), jnp.float32)
    blocks = (
        split_blocks(keys_in),
        split_blocks(values_in),
        split_blocks(log_gates),
        split_blocks(flags),
    )
    final, unused = lax.scan(jax.checkpoint(state_block), (zeros, zeros), blocks)
    passing = jnp.exp(jnp.sum(log_gates, axis=0)) * (jnp.sum(flags) == 0).astype(jnp.float32)
    return (passing, final[0], final[1])


def chain_join(earlier, later):
    factor = later[0][:, :, None]
    return (earlier[0] * later[0], factor * earlier[1] + later[1], factor * earlier[2] + later[2])


def fore_dot(left, right):
    return jnp.dot(left, right, preferred_element_type=jnp.float32)


def trans_dot(left, right):
    return lax.dot_general(
        left, right, (((0,), (0,)), ((), ())), preferred_element_type=jnp.float32
    )


def back_dot(left, right):
    return lax.dot_general(
        left, right, (((1,), (1,)), ((), ())), preferred_element_type=jnp.float32
    )


def gate_logs(forget_pre, forget_bias):
    return jax.nn.log_sigmoid(forget_pre + forget_bias) / gate_scale


def gated_unit(gate_vals, up_vals):
    return jax.nn.silu(gate_vals) * up_vals


def micro_step(weights, tokens, flags, cotan, pre_gain, forget_bias, head_gain, post_gain):
    (
        query_weight,
        key_weight,
        value_weight,
        forget_weight,
        outgate_weight,
        output_weight,
        gate_weight,
        up_weight,
        down_weight,
    ) = weights
    length, width = tokens.shape
    head_width = head_gain.shape[0]
    heads = width // head_width
    slots = forget_bias.shape[0] // heads
    inputs = tokens.astype(jnp.float32)
    normed_full, norm_back = jax.vjp(rms_norm, inputs, pre_gain)
    normed = normed_full.astype(jnp.bfloat16)
    queries = fore_dot(normed, query_weight).astype(jnp.bfloat16)
    keys_low = fore_dot(normed, key_weight).astype(jnp.bfloat16)
    values_low = fore_dot(normed, value_weight).astype(jnp.bfloat16)
    forget_pre = fore_dot(normed, forget_weight)
    gate_logits = fore_dot(normed, outgate_weight)
    log_gates, logs_back = jax.vjp(gate_logs, forget_pre, forget_bias)
    shaped = (length, heads, head_width)
    query_heads = queries.astype(jnp.float32).reshape(shaped)
    key_heads = keys_low.astype(jnp.float32).reshape(shaped)
    value_heads = values_low.astype(jnp.float32).reshape(shaped)
    gate_heads = log_gates.reshape(length, heads, slots)

    def bound_state(key_in, value_in, gates_in):
        return local_state(key_in, value_in, gates_in, flags)

    (passing, key_end, value_end), state_back = jax.vjp(
        bound_state, key_heads, value_heads, gate_heads
    )
    identity = (jnp.ones_like(passing), jnp.zeros_like(key_end), jnp.zeros_like(value_end))
    prefix = entering((passing, key_end, value_end), "seq", chain_join, identity)
    key_start, value_start = (prefix[1], prefix[2])

    def attend(query_in, key_in, value_in, gates_in, key_init, value_init):
        return slot_attention(query_in, key_in, value_in, gates_in, flags, key_init, value_init)[0]

    mixed, attend_back = jax.vjp(
        attend, query_heads, key_heads, value_heads, gate_heads, key_start, value_start
    )

    def merge_heads(mixed_in, logits_in, gain_in):
        return rms_norm(mixed_in, gain_in).reshape(length, width) * jax.nn.silu(logits_in)

    merged_full, merge_back = jax.vjp(merge_heads, mixed, gate_logits, head_gain)
    merged = merged_full.astype(jnp.bfloat16)
    hidden_one = inputs + fore_dot(merged, output_weight)
    normed_second, second_back = jax.vjp(rms_norm, hidden_one, post_gain)
    normed_two = normed_second.astype(jnp.bfloat16)
    gate_vals = fore_dot(normed_two, gate_weight)
    up_vals = fore_dot(normed_two, up_weight)
    hidden_full, unit_back = jax.vjp(gated_unit, gate_vals, up_vals)
    hidden = hidden_full.astype(jnp.bfloat16)
    block_output = (hidden_one + fore_dot(hidden, down_weight)).astype(jnp.bfloat16)
    down_grad = trans_dot(hidden, cotan)
    hidden_delta = back_dot(cotan, down_weight)
    gate_full, up_full = unit_back(hidden_delta)
    gate_delta = gate_full.astype(jnp.bfloat16)
    up_delta = up_full.astype(jnp.bfloat16)
    gate_grad = trans_dot(normed_two, gate_delta)
    up_grad = trans_dot(normed_two, up_delta)
    second_delta = back_dot(gate_delta, gate_weight) + back_dot(up_delta, up_weight)
    through_norm, postgain_grad = second_back(second_delta)
    first_delta = cotan.astype(jnp.float32) + through_norm
    attn_delta = first_delta.astype(jnp.bfloat16)
    output_grad = trans_dot(merged, attn_delta)
    merged_delta = back_dot(attn_delta, output_weight)
    mixed_delta, logits_delta, headgain_grad = merge_back(merged_delta)
    query_delta, keys_delta, values_delta, gates_delta, carry_key, carry_value = attend_back(
        mixed_delta
    )
    later_grads = carried_in((passing, carry_key, carry_value), "seq", chain_join, identity)
    end_key, end_value = (later_grads[1], later_grads[2])
    passing_delta = jnp.sum(end_key * key_start, axis=-1) + jnp.sum(
        end_value * value_start, axis=-1
    )
    keys_extra, values_extra, gates_extra = state_back((passing_delta, end_key, end_value))
    query_low = query_delta.reshape(length, width).astype(jnp.bfloat16)
    keys_back = (keys_delta + keys_extra).reshape(length, width).astype(jnp.bfloat16)
    values_back = (values_delta + values_extra).reshape(length, width).astype(jnp.bfloat16)
    gates_total = (gates_delta + gates_extra).reshape(length, heads * slots)
    forget_delta, bias_grad = logs_back(gates_total)
    forget_low = forget_delta.astype(jnp.bfloat16)
    logits_low = logits_delta.astype(jnp.bfloat16)
    query_grad = trans_dot(normed, query_low)
    key_grad = trans_dot(normed, keys_back)
    value_grad = trans_dot(normed, values_back)
    forget_grad = trans_dot(normed, forget_low)
    outgate_grad = trans_dot(normed, logits_low)
    normed_delta = back_dot(query_low, query_weight) + back_dot(keys_back, key_weight)
    normed_delta = (
        normed_delta + back_dot(values_back, value_weight) + back_dot(forget_low, forget_weight)
    )
    normed_delta = normed_delta + back_dot(logits_low, outgate_weight)
    input_delta, pregain_grad = norm_back(normed_delta)
    input_grad = (first_delta + input_delta).astype(jnp.bfloat16)
    matrices = (
        query_grad,
        key_grad,
        value_grad,
        forget_grad,
        outgate_grad,
        output_grad,
        gate_grad,
        up_grad,
        down_grad,
    )
    vectors = (pregain_grad, bias_grad, headgain_grad, postgain_grad)
    return (block_output, input_grad, matrices, vectors)


def body(
    tokens,
    resets,
    pre_gain,
    query_weight,
    key_weight,
    value_weight,
    forget_weight,
    forget_bias,
    outgate_weight,
    output_weight,
    head_gain,
    post_gain,
    gate_weight,
    up_weight,
    down_weight,
    cotangent,
):
    shards = (
        query_weight,
        key_weight,
        value_weight,
        forget_weight,
        outgate_weight,
        output_weight,
        gate_weight,
        up_weight,
        down_weight,
    )
    output_list = []
    grad_list = []
    matrix_total = None
    vector_total = None
    for micro_index in range(tokens.shape[0]):
        whole = (
            lax.all_gather(shards[0], "fsdp", axis=0, tiled=True),
            lax.all_gather(shards[1], "fsdp", axis=0, tiled=True),
            lax.all_gather(shards[2], "fsdp", axis=0, tiled=True),
            lax.all_gather(shards[3], "fsdp", axis=0, tiled=True),
            lax.all_gather(shards[4], "fsdp", axis=0, tiled=True),
            lax.all_gather(shards[5], "fsdp", axis=0, tiled=True),
            lax.all_gather(shards[6], "fsdp", axis=0, tiled=True),
            lax.all_gather(shards[7], "fsdp", axis=0, tiled=True),
            lax.all_gather(shards[8], "fsdp", axis=0, tiled=True),
        )
        block_output, input_grad, matrices, vectors = micro_step(
            whole,
            tokens[micro_index],
            resets[micro_index],
            cotangent[micro_index],
            pre_gain,
            forget_bias,
            head_gain,
            post_gain,
        )
        output_list.append(block_output)
        grad_list.append(input_grad)
        matrices = (
            lax.psum_scatter(matrices[0], ("seq", "fsdp"), scatter_dimension=0, tiled=True),
            lax.psum_scatter(matrices[1], ("seq", "fsdp"), scatter_dimension=0, tiled=True),
            lax.psum_scatter(matrices[2], ("seq", "fsdp"), scatter_dimension=0, tiled=True),
            lax.psum_scatter(matrices[3], ("seq", "fsdp"), scatter_dimension=0, tiled=True),
            lax.psum_scatter(matrices[4], ("seq", "fsdp"), scatter_dimension=0, tiled=True),
            lax.psum_scatter(matrices[5], ("seq", "fsdp"), scatter_dimension=0, tiled=True),
            lax.psum_scatter(matrices[6], ("seq", "fsdp"), scatter_dimension=0, tiled=True),
            lax.psum_scatter(matrices[7], ("seq", "fsdp"), scatter_dimension=0, tiled=True),
            lax.psum_scatter(matrices[8], ("seq", "fsdp"), scatter_dimension=0, tiled=True),
        )
        vectors = lax.psum((vectors[0], vectors[1], vectors[2], vectors[3]), ("seq", "fsdp"))
        if micro_index == 0:
            matrix_total, vector_total = (matrices, vectors)
        else:
            matrix_total = jax.tree.map(jnp.add, matrix_total, matrices)
            vector_total = jax.tree.map(jnp.add, vector_total, vectors)
    return (
        jnp.stack(output_list),
        jnp.stack(grad_list),
        vector_total[0],
        matrix_total[0],
        matrix_total[1],
        matrix_total[2],
        matrix_total[3],
        vector_total[1],
        matrix_total[4],
        matrix_total[5],
        vector_total[2],
        vector_total[3],
        matrix_total[6],
        matrix_total[7],
        matrix_total[8],
    )


def solution(mesh):
    placed = (
        P("fsdp", "seq", None),
        P("fsdp", "seq"),
        P(),
        P("fsdp", None),
        P("fsdp", None),
        P("fsdp", None),
        P("fsdp", None),
        P(),
        P("fsdp", None),
        P("fsdp", None),
        P(),
        P(),
        P("fsdp", None),
        P("fsdp", None),
        P("fsdp", None),
        P("fsdp", "seq", None),
    )
    return jax.shard_map(
        body,
        mesh=mesh,
        in_specs=placed,
        out_specs=(
            P("fsdp", "seq", None),
            P("fsdp", "seq", None),
            P(),
            P(("seq", "fsdp"), None),
            P(("seq", "fsdp"), None),
            P(("seq", "fsdp"), None),
            P(("seq", "fsdp"), None),
            P(),
            P(("seq", "fsdp"), None),
            P(("seq", "fsdp"), None),
            P(),
            P(),
            P(("seq", "fsdp"), None),
            P(("seq", "fsdp"), None),
            P(("seq", "fsdp"), None),
        ),
        check_vma=False,
    )
```

profile of v0, /device:TPU:0, one launch (start us, length us, event | category | flops | bytes accessed | tf_op | source)
XLA Modules:
  0.0 2076.7 jit_solution(12100343184358292224)
XLA Ops:
  23.3 11.6 all-gather.25.cloned.1.call-done
  37.4 21.7 %all-gather.27.cloned.1.call-done = bf16[1024,1024]{1,0:T(8,128)(2,1)} async-done(((bf16[256,1024]{1,0:T(8,128)(2,1)}), bf16[1024,1024]{1,0:T(8,128)(2,1)}) %all-gather.27.cloned.1.call-update) | async-done | bytes 2097168 | tf_op jit(solution)/shard_map/all_gather | solution.py:336
  61.7 9.8 while.238
  88.0 13.5 while.240
  108.7 20.4 all_gather.97
  130.4 17.4 all_gather.110
  161.6 30.1 %all-gather.43.cloned.1.call-done = bf16[32,64,256]{2,1,0:T(8,128)(2,1)} async-done(((bf16[4,64,256]{2,1,0:T(8,128)(2,1)}), bf16[32,64,256]{2,1,0:T(8,128)(2,1)}) %all-gather.43.cloned.1.call-update) | async-done | bytes 1048592 | tf_op jit(solution)/shard_map/all_gather | solution.py:17
  203.4 23.8 %while.236 = (s32[]{:T(128)}, f32[4,64,256]{2,1,0:T(8,128)S(1)}, f32[4,64,256]{2,1,0:T(8,128)S(1)}, f32[2,64,4,256]{3,1,2,0:T(8,128)S(1)}, f32[2,4,64,256]{3,2,1...) while((s32[]{:T(128)}, f32[4,64,256]{2,1,0:T(8,128)S(1)}, ...), condition=%wide.region_14.16_spmd.clone, body=%wide.region_9.15_spmd.clone.sunk | while | flops 328995200 | bytes 7308229 | solution.py:135
  233.4 41.1 %all-gather.47.cloned.1.call-done = bf16[32,64,256]{2,1,0:T(8,128)(2,1)} async-done(((bf16[4,64,256]{2,1,0:T(8,128)(2,1)}), bf16[32,64,256]{2,1,0:T(8,128)(2,1)}) %all-gather.47.cloned.1.call-update) | async-done | bytes 1048592 | tf_op jit(solution)/shard_map/all_gather | solution.py:17
  274.5 14.3 while.241
  291.5 31.2 %while.237 = (s32[]{:T(128)}, f32[4,64,256]{2,1,0:T(8,128)S(1)}, f32[4,64,256]{2,1,0:T(8,128)S(1)}, f32[2,64,4,256]{3,1,2,0:T(8,128)}, f32[2,4,64,256]{3,2,1,0:T...) while((s32[]{:T(128)}, f32[4,64,256]{2,1,0:T(8,128)S(1)}, ...), condition=%wide.region_31.33_spmd.clone, body=%wide.region_26.32_spmd.clone.sunk | while | flops 328995200 | bytes 6961853 | solution.py:135
  347.0 40.3 %all-gather.37.cloned.1.call-done = bf16[1024,2816]{1,0:T(8,128)(2,1)} async-done(((bf16[256,2816]{1,0:T(8,128)(2,1)}), bf16[1024,2816]{1,0:T(8,128)(2,1)}) %all-gather.37.cloned.1.call-update) | async-done | bytes 5767184 | tf_op jit(solution)/shard_map/all_gather | solution.py:341
  392.0 40.2 %all-gather.39.cloned.1.call-done = bf16[2816,1024]{1,0:T(8,128)(2,1)} async-done(((bf16[704,1024]{1,0:T(8,128)(2,1)}), bf16[2816,1024]{1,0:T(8,128)(2,1)}) %all-gather.39.cloned.1.call-update) | async-done | bytes 5767184 | tf_op jit(solution)/shard_map/all_gather | solution.py:342
  472.5 53.8 %while.242 = (s32[]{:T(128)}, f32[4,64,256]{2,1,0:T(8,128)}, f32[4,64,256]{2,1,0:T(8,128)}, bf16[2,64,4,256]{3,1,2,0:T(8,128)(2,1)}, f32[2,64,4,256]{3,1,2,0:T(8...) while((s32[]{:T(128)}, f32[4,64,256]{2,1,0:T(8,128)}, ...), condition=%wide.region_45.47_spmd.clone, body=%wide.region_36.46_spmd.clone.sunk | while | flops 885575744 | bytes 36841472 | solution.py:135
  532.0 57.2 %while.244 = (s32[]{:T(128)}, f32[4,64,256]{2,1,0:T(8,128)}, f32[4,64,256]{2,1,0:T(8,128)}, bf16[2,64,4,256]{3,1,2,0:T(8,128)(2,1)}, f32[2,64,4,256]{3,1,2,0:T(8...) while((s32[]{:T(128)}, f32[4,64,256]{2,1,0:T(8,128)}, ...), condition=%wide.region_69.71_spmd.clone, body=%wide.region_60.70_spmd.clone.sunk | while | flops 885575744 | bytes 34744296 | solution.py:135
  596.3 12.9 all-gather.51.cloned.1.call-done
  609.2 14.7 while.243
  624.7 26.0 %all-gather.53.cloned.1.call-done = bf16[32,64,256]{2,1,0:T(8,128)(2,1)} async-done(((bf16[4,64,256]{2,1,0:T(8,128)(2,1)}), bf16[32,64,256]{2,1,0:T(8,128)(2,1)}) %all-gather.53.cloned.1.call-update) | async-done | bytes 1048592 | tf_op jit(solution)/shard_map/all_gather | solution.py:38
  650.7 41.5 %all-gather.55.cloned.1.call-done = bf16[32,64,256]{2,1,0:T(8,128)(2,1)} async-done(((bf16[4,64,256]{2,1,0:T(8,128)(2,1)}), bf16[32,64,256]{2,1,0:T(8,128)(2,1)}) %all-gather.55.cloned.1.call-update) | async-done | bytes 1048592 | tf_op jit(solution)/shard_map/all_gather | solution.py:38
  692.2 14.4 while.245
  710.4 25.6 %while.235 = (s32[]{:T(128)}, f32[4,64,256]{2,1,0:T(8,128)S(1)}, f32[4,64,256]{2,1,0:T(8,128)S(1)}, f32[2,64,4,256]{3,1,2,0:T(8,128)}, f32[2,64,4,256]{3,1,2,0:T...) while((s32[]{:T(128)}, f32[4,64,256]{2,1,0:T(8,128)S(1)}, ...), condition=%wide.region_78.80_spmd, body=%wide.region_72.79_spmd.sunk | while | flops 305418304 | bytes 18828936 | solution.py:147
  738.5 23.2 %while.234 = (s32[]{:T(128)}, f32[4,64,256]{2,1,0:T(8,128)S(1)}, f32[4,64,256]{2,1,0:T(8,128)S(1)}, f32[2,64,4,256]{3,1,2,0:T(8,128)}, f32[2,64,4,256]{3,1,2,0:T...) while((s32[]{:T(128)}, f32[4,64,256]{2,1,0:T(8,128)S(1)}, ...), condition=%wide.region_54.56_spmd, body=%wide.region_48.55_spmd.sunk | while | flops 305418304 | bytes 18828936 | solution.py:147
  844.1 38.6 %all-reduce.4 = (f32[1024]{0:T(1024)}, f32[256]{0:T(256)}, f32[256]{0:T(256)}, f32[1024]{0:T(1024)}) all-reduce(f32[1024]{0:T(1024)S(1)} %add.736, f32[256]{0:T(256)S(1)} %negate_add_fusion, f32[256]{0:T(256)S(1)} %add.744, f32[1024]{0:T(1024)S(1)} %add.745), channel_id=1, replica_groups=mesh['seq'=8,'fsdp'=4] {'seq','fsdp'}, use_global_device_ids=true, to_apply=%region_83.85 | all-reduce | flops 2560 | bytes 20480 | tf_op jit(solution)/shard_map/psum | solution.py:367
  884.0 20.7 reduce-scatter.16.cloned.1.call-done
  904.6 139.9 %reduce-scatter.10.cloned.1.call-done = f32[32,1024]{1,0:T(8,128)} async-done(((f32[1024,1024]{1,0:T(8,128)}), f32[32,1024]{1,0:T(8,128)}) %reduce-scatter.10.cloned.1.call-update) | async-done | bytes 131088 | tf_op jit(solution)/shard_map/reduce_scatter | solution.py:357
  1044.6 140.1 %reduce-scatter.18.cloned.1.call-done = f32[32,1024]{1,0:T(8,128)} async-done(((f32[1024,1024]{1,0:T(8,128)}), f32[32,1024]{1,0:T(8,128)}) %reduce-scatter.18.cloned.1.call-update) | async-done | bytes 131088 | tf_op jit(solution)/shard_map/reduce_scatter | solution.py:361
  1184.7 139.6 %reduce-scatter.20.cloned.1.call-done = f32[32,1024]{1,0:T(8,128)} async-done(((f32[1024,1024]{1,0:T(8,128)}), f32[32,1024]{1,0:T(8,128)}) %reduce-scatter.20.cloned.1.call-update) | async-done | bytes 131088 | tf_op jit(solution)/shard_map/reduce_scatter | solution.py:362
  1324.2 140.2 %reduce-scatter.12.cloned.1.call-done = f32[32,1024]{1,0:T(8,128)} async-done(((f32[1024,1024]{1,0:T(8,128)}), f32[32,1024]{1,0:T(8,128)}) %reduce-scatter.12.cloned.1.call-update) | async-done | bytes 131088 | tf_op jit(solution)/shard_map/reduce_scatter | solution.py:358
  1464.4 140.5 %reduce-scatter.14.cloned.1.call-done = f32[32,1024]{1,0:T(8,128)} async-done(((f32[1024,1024]{1,0:T(8,128)}), f32[32,1024]{1,0:T(8,128)}) %reduce-scatter.14.cloned.1.call-update) | async-done | bytes 131088 | tf_op jit(solution)/shard_map/reduce_scatter | solution.py:359
  1604.9 153.5 %reduce-scatter.22.cloned.1.call-done = f32[32,2816]{1,0:T(8,128)} async-done(((f32[1024,2816]{1,0:T(8,128)}), f32[32,2816]{1,0:T(8,128)}) %reduce-scatter.22.cloned.1.call-update) | async-done | bytes 360464 | tf_op jit(solution)/shard_map/reduce_scatter | solution.py:363
  1758.5 155.6 %reduce-scatter.24.cloned.1.call-done = f32[32,2816]{1,0:T(8,128)} async-done(((f32[1024,2816]{1,0:T(8,128)}), f32[32,2816]{1,0:T(8,128)}) %reduce-scatter.24.cloned.1.call-update) | async-done | bytes 360464 | tf_op jit(solution)/shard_map/reduce_scatter | solution.py:364
  1914.1 155.9 %reduce-scatter.26.cloned.1.call-done = f32[88,1024]{1,0:T(8,128)} async-done(((f32[2816,1024]{1,0:T(8,128)}), f32[88,1024]{1,0:T(8,128)}) %reduce-scatter.26.cloned.1.call-update) | async-done | bytes 360464 | tf_op jit(solution)/shard_map/reduce_scatter | solution.py:365
  (1175 shorter events, 530.7 us)
Async XLA Ops:
  7.2 27.7 %all-gather.25.cloned.1.call-start = ((), (), s32[]{:S(2)}) async-start(), calls=%async_computation.9 | async-start | bytes 2621440 | tf_op jit(solution)/shard_map/all_gather | solution.py:335
  8.0 51.2 %all-gather.27.cloned.1.call-start = ((), (), s32[]{:S(2)}) async-start(), calls=%async_computation.10 | async-start | bytes 2621440 | tf_op jit(solution)/shard_map/all_gather | solution.py:336
  8.7 139.8 %all-gather.29.cloned.1.call-start = ((), (), s32[]{:S(2)}) async-start(), calls=%async_computation.11 | async-start | bytes 2621440 | tf_op jit(solution)/shard_map/all_gather | solution.py:334
  9.5 149.2 %all-gather.31.cloned.1.call-start = ((), (), s32[]{:S(2)}) async-start(), calls=%async_computation.12 | async-start | bytes 2621440 | tf_op jit(solution)/shard_map/all_gather | solution.py:338
  10.0 151.6 %all-gather.41.cloned.1.call-start = ((), (), s32[]{:S(2)}) async-start(), calls=%async_computation.17 | async-start | bytes 1179648 | tf_op jit(solution)/shard_map/all_gather | solution.py:17
  19.5 129.0 %copy-start.130 = (f32[128]{0:T(128)}, f32[128]{0:T(128)S(1)}, u32[]{:S(2)}) copy-start(f32[128]{0:T(128)S(1)} %fusion.411) | copy-start | bytes 1540
  72.2 119.5 %all-gather.43.cloned.1.call-start = ((), (), s32[]{:S(2)}) async-start(), calls=%async_computation.18 | async-start | bytes 1179648 | tf_op jit(solution)/shard_map/all_gather | solution.py:17
  72.9 85.7 %copy-start.128 = (f32[128]{0:T(128)}, f32[128]{0:T(128)S(1)}, u32[]{:S(2)}) copy-start(f32[128]{0:T(128)S(1)} %fusion.413) | copy-start | bytes 1540
  87.9 145.6 %all-gather.45.cloned.1.call-start = ((), (), s32[]{:S(2)}) async-start(), calls=%async_computation.19 | async-start | bytes 1179648 | tf_op jit(solution)/shard_map/all_gather | solution.py:17
  102.3 172.2 %all-gather.47.cloned.1.call-start = ((), (), s32[]{:S(2)}) async-start(), calls=%async_computation.20 | async-start | bytes 1179648 | tf_op jit(solution)/shard_map/all_gather | solution.py:17
  103.1 226.7 %all-gather.33.cloned.1.call-start = ((), (), s32[]{:S(2)}) async-start(), calls=%async_computation.13 | async-start | bytes 2621440 | tf_op jit(solution)/shard_map/all_gather | solution.py:339
  103.8 238.5 %all-gather.35.cloned.1.call-start = ((), (), s32[]{:S(2)}) async-start(), calls=%async_computation.14 | async-start | bytes 7208960 | tf_op jit(solution)/shard_map/all_gather | solution.py:340
  104.4 282.9 %all-gather.37.cloned.1.call-start = ((), (), s32[]{:S(2)}) async-start(), calls=%async_computation.15 | async-start | bytes 7208960 | tf_op jit(solution)/shard_map/all_gather | solution.py:341
  105.2 327.0 %all-gather.39.cloned.1.call-start = ((), (), s32[]{:S(2)}) async-start(), calls=%async_computation.16 | async-start | bytes 7208960 | tf_op jit(solution)/shard_map/all_gather | solution.py:342
  105.7 490.5 %all-gather.49.cloned.1.call-start = ((), (), s32[]{:S(2)}) async-start(), calls=%async_computation.21 | async-start | bytes 1179648 | tf_op jit(solution)/shard_map/all_gather | solution.py:38
  105.8 45.8 %copy-start.63 = (bf16[2,64,4,256]{3,1,2,0:T(8,128)(2,1)}, bf16[2,64,4,256]{3,1,2,0:T(8,128)(2,1)S(1)}, u32[]{:S(2)}) copy-start(bf16[2,64,4,256]{3,1,2,0:T(8,128)(2,1)S(1)} %fusion.455) | copy-start | bytes 786436
  227.2 47.3 %copy-start.31 = (f32[4,64,256]{2,1,0:T(8,128)S(1)}, f32[4,64,256]{2,1,0:T(8,128)}, u32[]{:S(2)}) copy-start(f32[4,64,256]{2,1,0:T(8,128)} %custom-call.7) | copy-start | bytes 786436
  332.2 126.0 %copy-start.23 = (f32[128,1024]{1,0:T(8,128)}, f32[128,1024]{1,0:T(8,128)S(1)}, u32[]{:S(2)}) copy-start(f32[128,1024]{1,0:T(8,128)S(1)} %get-tuple-element.3188) | copy-start | bytes 1572868
  332.8 125.4 %copy-start.25 = (f32[128,1024]{1,0:T(8,128)}, f32[128,1024]{1,0:T(8,128)S(1)}, u32[]{:S(2)}) copy-start(f32[128,1024]{1,0:T(8,128)S(1)} %get-tuple-element.3190) | copy-start | bytes 1572868
  333.0 54.3 %copy-start.38 = (bf16[128,1024]{1,0:T(8,128)(2,1)}, bf16[128,1024]{1,0:T(8,128)(2,1)S(1)}, u32[]{:S(2)}) copy-start(bf16[128,1024]{1,0:T(8,128)(2,1)S(1)} %multiply_convert_fusion.6) | copy-start | bytes 786436
  527.9 81.3 %all-gather.51.cloned.1.call-start = ((), (), s32[]{:S(2)}) async-start(), calls=%async_computation.22 | async-start | bytes 1179648 | tf_op jit(solution)/shard_map/all_gather | solution.py:38
  529.6 121.2 %all-gather.53.cloned.1.call-start = ((), (), s32[]{:S(2)}) async-start(), calls=%async_computation.23 | async-start | bytes 1179648 | tf_op jit(solution)/shard_map/all_gather | solution.py:38
  590.8 101.4 %all-gather.55.cloned.1.call-start = ((), (), s32[]{:S(2)}) async-start(), calls=%async_computation.24 | async-start | bytes 1179648 | tf_op jit(solution)/shard_map/all_gather | solution.py:38
  596.2 308.5 %reduce-scatter.16.cloned.1.call-start = ((), (), s32[]{:S(2)}) async-start(), calls=%async_computation.28 | async-start | bytes 1081344 | tf_op jit(solution)/shard_map/reduce_scatter | solution.py:360
  770.8 273.8 %reduce-scatter.10.cloned.1.call-start = ((), (), s32[]{:S(2)}) async-start(), calls=%async_computation.25 | async-start | bytes 4325376 | tf_op jit(solution)/shard_map/reduce_scatter | solution.py:357
  775.0 409.7 %reduce-scatter.18.cloned.1.call-start = ((), (), s32[]{:S(2)}) async-start(), calls=%async_computation.29 | async-start | bytes 4325376 | tf_op jit(solution)/shard_map/reduce_scatter | solution.py:361
  779.8 544.5 %reduce-scatter.20.cloned.1.call-start = ((), (), s32[]{:S(2)}) async-start(), calls=%async_computation.30 | async-start | bytes 4325376 | tf_op jit(solution)/shard_map/reduce_scatter | solution.py:362
  784.3 680.1 %reduce-scatter.12.cloned.1.call-start = ((), (), s32[]{:S(2)}) async-start(), calls=%async_computation.26 | async-start | bytes 4325376 | tf_op jit(solution)/shard_map/reduce_scatter | solution.py:358
  791.2 813.7 %reduce-scatter.14.cloned.1.call-start = ((), (), s32[]{:S(2)}) async-start(), calls=%async_computation.27 | async-start | bytes 4325376 | tf_op jit(solution)/shard_map/reduce_scatter | solution.py:359
  796.1 962.4 %reduce-scatter.22.cloned.1.call-start = ((), (), s32[]{:S(2)}) async-start(), calls=%async_computation.31 | async-start | bytes 11894784 | tf_op jit(solution)/shard_map/reduce_scatter | solution.py:363
  805.9 1108.2 %reduce-scatter.24.cloned.1.call-start = ((), (), s32[]{:S(2)}) async-start(), calls=%async_computation.32 | async-start | bytes 11894784 | tf_op jit(solution)/shard_map/reduce_scatter | solution.py:364
  814.8 1255.2 %reduce-scatter.26.cloned.1.call-start = ((), (), s32[]{:S(2)}) async-start(), calls=%async_computation.33 | async-start | bytes 11894784 | tf_op jit(solution)/shard_map/reduce_scatter | solution.py:365
  (192 other events, 800.5 us)
Sparse Core Ops, SparseCore 0:
  9.6 25.2 all-gather.24
  36.5 22.5 all-gather.26
  60.7 22.5 all-gather.28
  84.8 22.5 all-gather.30
  109.9 40.2 all-gather.40
  152.7 38.9 all-gather.42
  194.4 38.9 all-gather.44
  235.5 38.8 all-gather.46
  276.0 21.3 all-gather.32
  298.8 43.4 all-gather.34
  343.9 43.3 all-gather.36
  388.7 43.3 all-gather.38
  528.0 40.1 all-gather.48
  570.1 38.9 all-gather.50
  611.7 38.9 all-gather.52
  653.3 38.8 all-gather.54
  770.9 133.6 reduce-scatter.15
  907.4 137.0 reduce-scatter.9
  1047.5 137.1 reduce-scatter.17
  1187.5 136.7 reduce-scatter.19
  1327.2 137.1 reduce-scatter.11
  1467.4 137.5 reduce-scatter.13
  1607.9 150.4 reduce-scatter.21
  1761.3 152.7 reduce-scatter.23
  1917.1 152.8 reduce-scatter.25
where the time goes:
time: 2090 us; the launch traced here: 2080 us
  waiting for transfers between devices  1470 us (70%)
  matrix products  240 us (11%)
  local copies, waits for them, and re-layouts  136 us (7%)
  other arithmetic  117 us (6%)
  blocking collectives  85.2 us (4%)
    reduce_scatter x1, waiting for transfers between devices, body(): lax.psum_scatter(matrices[8], ('seq', 'fsdp'), scatter_dimension=0, tiled...  156 us
    reduce_scatter x1, waiting for transfers between devices, body(): lax.psum_scatter(matrices[7], ('seq', 'fsdp'), scatter_dimension=0, tiled...  156 us
    reduce_scatter x1, waiting for transfers between devices, body(): lax.psum_scatter(matrices[6], ('seq', 'fsdp'), scatter_dimension=0, tiled...  154 us
    reduce_scatter x1, waiting for transfers between devices, body(): lax.psum_scatter(matrices[2], ('seq', 'fsdp'), scatter_dimension=0, tiled...  140 us
    reduce_scatter x1, waiting for transfers between devices, body(): lax.psum_scatter(matrices[1], ('seq', 'fsdp'), scatter_dimension=0, tiled...  140 us
    reduce_scatter x1, waiting for transfers between devices, body(): lax.psum_scatter(matrices[4], ('seq', 'fsdp'), scatter_dimension=0, tiled...  140 us
    reduce_scatter x1, waiting for transfers between devices, body(): lax.psum_scatter(matrices[0], ('seq', 'fsdp'), scatter_dimension=0, tiled...  140 us
    reduce_scatter x1, waiting for transfers between devices, body(): lax.psum_scatter(matrices[5], ('seq', 'fsdp'), scatter_dimension=0, tiled...  140 us
  transfers between devices with their start and end apart: 25, of which 20 were waited for; matrix products, arithmetic and copies ran while one was open for 15% of the time, Pallas kernels for 0%

commit v1 on v0

v1 whole, which is shorter than its diff:
```python
import functools

import jax
import jax.numpy as jnp
from jax import lax
from jax.experimental import pallas as pl
from jax.experimental.pallas import tpu as pltpu
from jax.sharding import PartitionSpec as P

BLOCK = 64
norm_eps = 1e-06
f32, bf16 = jnp.float32, jnp.bfloat16
MESH = pl.DeviceIdType.MESH
VMEM = pltpu.VMEM
ANY = pl.ANY
LIMIT = 60 * 2**20


def in_vmem():
    return pl.BlockSpec(memory_space=VMEM)


def in_place():
    return pl.BlockSpec(memory_space=ANY)


def greet(partners):
    barrier = pltpu.get_barrier_semaphore()
    for partner in partners:
        pl.semaphore_signal(barrier, inc=1, device_id=partner, device_id_type=MESH)
    pl.semaphore_wait(barrier, len(partners))


def remote(src, dst, sems, index, partner):
    return pltpu.make_async_remote_copy(
        src_ref=src,
        dst_ref=dst,
        send_sem=sems[0].at[index],
        recv_sem=sems[1].at[index],
        device_id=partner,
        device_id_type=MESH,
    )


def gather_kernel(count, *refs):
    shards, wholes = refs[:count], refs[count : 2 * count]
    local, *sems = refs[2 * count :]
    s, f = lax.axis_index("seq"), lax.axis_index("fsdp")
    q = lax.rem(s, 4)
    sib, far, nx, nz = (s, f ^ 1), (s, f ^ 2), (s ^ 1, f), (s ^ 2, f)
    fy = f ^ 2
    greet((sib, far, nx, nz))
    started = []

    def go(copy):
        copy.start()
        started.append(copy)

    def piece(m, owner, which, half=None):
        rows = shards[m].shape[0]
        quarter = rows // 4
        first = (quarter // 2 + 15) // 16 * 16
        start, size = (0, quarter) if half is None else ((0, first), (first, quarter - first))[half]
        return wholes[m].at[owner, pl.ds(pl.multiple_of(which * quarter + start, 16), size)]

    def send(kind, m, part, partner):
        go(remote(part, part, sems, (kind, m), partner))

    def arrived(kind, m, part):
        remote(part, part, sems, (kind, m), sib).wait_recv()

    for m in range(count):
        rows = shards[m].shape[0]
        quarter = rows // 4
        src = shards[m].at[pl.ds(pl.multiple_of(q * quarter, 16), quarter)]
        go(remote(src, piece(m, f, q), sems, (1, m), far))
    own = []
    for m in range(count):
        go(remote(shards[m], wholes[m].at[f], sems, (0, m), sib))
        copy = pltpu.make_async_copy(shards[m], wholes[m].at[f], local.at[m])
        copy.start()
        own.append(copy)
    for step in range(count + 2):
        if step < count:
            m = step
            mine = piece(m, fy, q)
            arrived(1, m, mine)
            send(2, m, mine, nx)
            send(3, m, mine, nz)
            send(6, m, mine, sib)
        if 0 <= step - 1 < count:
            m = step - 1
            from_x, from_z = piece(m, fy, q ^ 1), piece(m, fy, q ^ 2)
            arrived(2, m, from_x)
            send(4, m, piece(m, fy, q ^ 1, 0), nz)
            send(7, m, from_x, sib)
            arrived(3, m, from_z)
            send(5, m, piece(m, fy, q ^ 2, 1), nx)
            send(8, m, from_z, sib)
        if 0 <= step - 2 < count:
            m = step - 2
            for kind, half in ((4, 0), (5, 1)):
                part = piece(m, fy, q ^ 3, half)
                arrived(kind, m, part)
                send(kind + 5, m, part, sib)
    fs = fy ^ 1
    for m in range(count):
        arrived(0, m, wholes[m].at[f ^ 1])
        arrived(6, m, piece(m, fs, q))
        arrived(7, m, piece(m, fs, q ^ 1))
        arrived(8, m, piece(m, fs, q ^ 2))
        arrived(9, m, piece(m, fs, q ^ 3, 0))
        arrived(10, m, piece(m, fs, q ^ 3, 1))
        own[m].wait()
    for copy in started:
        copy.wait_send()


def gather(shards):
    count = len(shards)
    wholes = pl.pallas_call(
        functools.partial(gather_kernel, count),
        name="gather",
        out_shape=[jax.ShapeDtypeStruct((4,) + w.shape, w.dtype) for w in shards],
        in_specs=[in_place()] * count,
        out_specs=[in_place()] * count,
        scratch_shapes=[
            pltpu.SemaphoreType.DMA((count,)),
            pltpu.SemaphoreType.DMA((11, count)),
            pltpu.SemaphoreType.DMA((11, count)),
        ],
        compiler_params=pltpu.CompilerParams(collective_id=1, has_side_effects=True),
    )(*shards)
    return [w.reshape((-1, w.shape[-1])) for w in wholes]


def parts_of(a, count):
    if a.dtype == bf16:
        return [a]
    out = []
    for i in range(count):
        part = a.astype(bf16)
        out.append(part)
        if i + 1 < count:
            a = a - part.astype(f32)
    return out


def dot(a, b, ca=1, cb=0, count=1):
    total = None
    for right in reversed(parts_of(b, count)):
        term = lax.dot_general(
            a.astype(bf16), right, (((ca,), (cb,)), ((), ())), preferred_element_type=f32
        )
        total = term if total is None else total + term
    return total


def to_col(row):
    n = row.shape[1]
    i = lax.broadcasted_iota(jnp.int32, (n, n), 0)
    j = lax.broadcasted_iota(jnp.int32, (n, n), 1)
    return jnp.sum(jnp.where(i == j, jnp.broadcast_to(row, (n, n)), 0.0), axis=1, keepdims=True)


def mask_set(flags_col, flags_row):
    n = flags_col.shape[0]
    i = lax.broadcasted_iota(jnp.int32, (n, n), 0)
    j = lax.broadcasted_iota(jnp.int32, (n, n), 1)
    same = (i // BLOCK) == (j // BLOCK)
    lower = jnp.where(same & (i >= j), 1.0, 0.0)
    block = jnp.where(same, 1.0, 0.0)
    seen_col = dot(lower, flags_col)[:, :1]
    all_col = dot(block, flags_col)[:, :1]
    seen_row = dot(flags_row, lower, 1, 1)[:1, :]
    linked = jnp.where(seen_col == seen_row, lower, 0.0)
    fresh = jnp.where(seen_col == 0.0, 1.0, 0.0)
    ending = jnp.where(seen_col == all_col, 1.0, 0.0)
    unbroken = jnp.where(all_col == 0.0, 1.0, 0.0)
    return lower, linked, fresh, ending, unbroken


def gate_set(pre, bias, lower, ending):
    z = pre + bias
    u = jnp.exp(-jnp.abs(z))
    lp = jnp.where(
        u < 0.02, u * (1.0 - u * (0.5 - u * (1.0 / 3.0 - 0.25 * u))), jnp.log(1.0 + u)
    )
    g = (jnp.minimum(z, 0.0) - lp) * 0.125
    series = 1.0 + g * (1.0 / 7.0)
    for order in (6, 5, 4, 3, 2):
        series = 1.0 + g * (1.0 / order) * series
    oma = jnp.where(g > -0.35, -g * series, 1.0 - jnp.exp(g))
    a = dot(lower, g, count=3)
    n, lanes = a.shape
    last = jnp.concatenate(
        [
            jnp.broadcast_to(a[b * BLOCK + BLOCK - 1 : b * BLOCK + BLOCK], (BLOCK, lanes))
            for b in range(n // BLOCK)
        ],
        axis=0,
    )
    tail = jnp.exp(last - a) * ending
    return z, u, oma, jnp.exp(a), jnp.exp(-a), tail


def rows_of(b):
    return slice(b * BLOCK, (b + 1) * BLOCK)


def passing(growth, unbroken, b, hs):
    last = b * BLOCK + BLOCK - 1
    return to_col(growth[last : last + 1, hs] * unbroken[last : last + 1])


def attend_kernel(
    size, heads, q_ref, k_ref, v_ref, pre_ref, bias_ref, fcol_ref, frow_ref, logit_ref, gain_ref,
    merged_ref, mixed_ref, aff_ref, mixing_ref, weight_ref, inner_ref, state_ref, pass_ref,
    ends, came, going, send_sem, recv_sem,
):
    s, f = lax.axis_index("seq"), lax.axis_index("fsdp")
    right, left = (lax.rem(s + 1, size), f), (lax.rem(s + size - 1, size), f)
    greet((left, right))
    n, width = q_ref.shape
    head = width // heads
    slots = pre_ref.shape[1] // heads
    blocks = n // BLOCK
    streams = 2
    per = blocks // streams
    scale = head ** (-0.5)
    lower, linked, fresh, ending, unbroken = mask_set(fcol_ref[...], frow_ref[...])
    z, u, oma, growth, inverse, tail = gate_set(pre_ref[...], bias_ref[...], lower, ending)
    shrink, kept = inverse * oma, tail * oma

    @pl.when(s == 0)
    def _():
        came[...] = jnp.zeros_like(came)

    for h in range(heads):
        hs, hd = slice(h * slots, (h + 1) * slots), slice(h * head, (h + 1) * head)
        for b in range(blocks):
            part = kept[rows_of(b), hs]
            at = (h * streams + b // per) * per + b % per
            ends[at, :, :head] = dot(part, k_ref[rows_of(b), hd], 0, 0)
            ends[at, :, head:] = dot(part, v_ref[rows_of(b), hd], 0, 0)
            pass_ref[at] = jnp.broadcast_to(passing(growth, unbroken, b, hs), pass_ref.shape[1:])
    sends = []
    for pair in range(heads * streams):
        copy = remote(going.at[pair], came.at[pair], (send_sem, recv_sem), pair, right)

        @pl.when(s > 0)
        def _(copy=copy):
            copy.wait_recv()

        state = came[pair].astype(f32)
        for b in range(per):
            at = pair * per + b
            state_ref[pair, b] = state.astype(bf16)
            state = pass_ref[at][:, :1] * state + ends[at]
        state_ref[pair, per] = state.astype(bf16)
        going[pair] = state.astype(bf16)

        @pl.when(s < size - 1)
        def _(copy=copy):
            copy.start()

        sends.append(copy)
    for h in range(heads):
        hs, hd = slice(h * slots, (h + 1) * slots), slice(h * head, (h + 1) * head)
        gr, sh = growth[:, hs], shrink[:, hs]
        qh, vh = q_ref[:, hd], v_ref[:, hd]
        aff = (dot(qh, k_ref[:, hd], 1, 1) * (linked * scale)).astype(bf16)
        aff_ref[h] = aff
        carried = jnp.concatenate(
            [
                dot(qh[rows_of(b)], state_ref[h * streams + b // per, b % per, :, :head], 1, 1)
                for b in range(blocks)
            ],
            axis=0,
        )
        inner = dot(aff, sh) + carried * (scale * fresh)
        scores = gr * inner
        e = jnp.exp(scores - jnp.max(scores, axis=1, keepdims=True))
        weights = e / jnp.sum(e, axis=1, keepdims=True)
        weight_ref[:, hs] = weights
        inner_ref[:, hs] = inner
        lifted = weights * gr
        mixing = (dot(lifted, sh.astype(bf16), 1, 1) * linked).astype(bf16)
        mixing_ref[h] = mixing
        brought = jnp.concatenate(
            [
                dot(lifted[rows_of(b)], state_ref[h * streams + b // per, b % per, :, head:])
                for b in range(blocks)
            ],
            axis=0,
        )
        mixed = dot(mixing, vh) + brought * fresh
        mixed_ref[:, hd] = mixed
        r = lax.rsqrt(jnp.mean(mixed * mixed, axis=1, keepdims=True) + norm_eps)
        logits = logit_ref[:, hd]
        merged_ref[:, hd] = (
            mixed * r * gain_ref[...] * (logits / (1.0 + jnp.exp(-logits)))
        ).astype(bf16)
    for copy in sends:

        @pl.when(s < size - 1)
        def _(copy=copy):
            copy.wait_send()


def attend(size, heads, q, k, v, pre, bias, fcol, frow, logits, gain):
    n, width = q.shape
    head, slots = width // heads, pre.shape[1] // heads
    pairs, per = heads * 2, n // BLOCK // 2
    return pl.pallas_call(
        functools.partial(attend_kernel, size, heads),
        name="attend",
        out_shape=[
            jax.ShapeDtypeStruct((n, width), bf16),
            jax.ShapeDtypeStruct((n, width), f32),
            jax.ShapeDtypeStruct((heads, n, n), bf16),
            jax.ShapeDtypeStruct((heads, n, n), bf16),
            jax.ShapeDtypeStruct(pre.shape, f32),
            jax.ShapeDtypeStruct(pre.shape, f32),
            jax.ShapeDtypeStruct((pairs, per + 1, slots, 2 * head), bf16),
            jax.ShapeDtypeStruct((pairs * per, slots, 128), f32),
        ],
        in_specs=[in_vmem()] * 9,
        out_specs=[in_vmem()] * 8,
        scratch_shapes=[
            VMEM((pairs * per, slots, 2 * head), f32),
            VMEM((pairs, slots, 2 * head), bf16),
            VMEM((pairs, slots, 2 * head), bf16),
            pltpu.SemaphoreType.DMA((pairs,)),
            pltpu.SemaphoreType.DMA((pairs,)),
        ],
        compiler_params=pltpu.CompilerParams(
            collective_id=2, has_side_effects=True, vmem_limit_bytes=LIMIT
        ),
    )(q, k, v, pre, bias, fcol, frow, logits, gain)


def return_kernel(
    size, heads, q_ref, k_ref, v_ref, pre_ref, bias_ref, fcol_ref, frow_ref, logit_ref, gain_ref,
    mixed_ref, aff_ref, mixing_ref, weight_ref, inner_ref, state_ref, pass_ref, delta_ref,
    q_low, k_low, v_low, forget_low, logit_low, bias_grad, gain_grad,
    owed, came, going, k_acc, v_acc, dmix, da_acc, doma_acc, send_sem, recv_sem,
):
    s, f = lax.axis_index("seq"), lax.axis_index("fsdp")
    right, left = (lax.rem(s + 1, size), f), (lax.rem(s + size - 1, size), f)
    greet((left, right))
    n, width = q_ref.shape
    head = width // heads
    slots = pre_ref.shape[1] // heads
    blocks = n // BLOCK
    streams = 2
    per = blocks // streams
    scale = head ** (-0.5)
    lower, linked, fresh, ending, unbroken = mask_set(fcol_ref[...], frow_ref[...])
    z, u, oma, growth, inverse, tail = gate_set(pre_ref[...], bias_ref[...], lower, ending)
    shrink, kept = inverse * oma, tail * oma

    @pl.when(s == size - 1)
    def _():
        came[...] = jnp.zeros_like(came)

    gain_total = jnp.zeros((1, head), f32)
    for h in range(heads):
        hs, hd = slice(h * slots, (h + 1) * slots), slice(h * head, (h + 1) * head)
        mixed, logits, delta = mixed_ref[:, hd], logit_ref[:, hd], delta_ref[:, hd]
        r = lax.rsqrt(jnp.mean(mixed * mixed, axis=1, keepdims=True) + norm_eps)
        sig = 1.0 / (1.0 + jnp.exp(-logits))
        silu = logits * sig
        unit = mixed * r
        dy = delta * silu
        logit_low[:, hd] = (delta * unit * gain_ref[...] * (sig + silu * (1.0 - sig))).astype(bf16)
        gain_total = gain_total + jnp.sum(dy * unit, axis=0, keepdims=True)
        dy = dy * gain_ref[...]
        dmixed = r * (dy - unit * jnp.mean(unit * dy, axis=1, keepdims=True))
        gr, sh = growth[:, hs], shrink[:, hs].astype(bf16)
        weights, inner = weight_ref[:, hs], inner_ref[:, hs]
        aff, mixing = aff_ref[h], mixing_ref[h]
        qh, kh, vh = q_ref[:, hd], k_ref[:, hd], v_ref[:, hd]
        do = dmixed.astype(bf16)
        lifted = (weights * gr).astype(bf16)
        dm = (dot(do, vh, 1, 1) * linked).astype(bf16)
        v_acc[:, hd] = dot(mixing, do, 0, 0)
        fdo = (dmixed * fresh).astype(bf16)

        def states(b, h=h):
            return state_ref.at[h * streams + b // per, b % per]

        dlift = dot(dm, sh) + jnp.concatenate(
            [dot(fdo[rows_of(b)], states(b)[:, head:], 1, 1) for b in range(blocks)], axis=0
        )
        dsh = dot(dm, lifted, 0, 0)
        dw = dlift * gr
        dsc = weights * (dw - jnp.sum(weights * dw, axis=1, keepdims=True))
        du = dsc * gr
        du_low = du.astype(bf16)
        da = (dot(du_low, sh, 1, 1) * (linked * scale)).astype(bf16)
        dsh = dsh + dot(aff, du_low, 0, 0)
        fdu = (du * (fresh * scale)).astype(bf16)
        q_low[:, hd] = (
            dot(da, kh)
            + jnp.concatenate(
                [dot(fdu[rows_of(b)], states(b)[:, :head]) for b in range(blocks)], axis=0
            )
        ).astype(bf16)
        k_acc[:, hd] = dot(da, qh, 0, 0)
        for b in range(blocks):
            at = (h * streams + b // per) * per + b % per
            owed[at, :, :head] = dot(fdu[rows_of(b)], qh[rows_of(b)], 0, 0)
            owed[at, :, head:] = dot(lifted[rows_of(b)], fdo[rows_of(b)], 0, 0)
        da_acc[:, hs] = lifted.astype(f32) * dlift + du_low.astype(f32) * inner - dsh * sh.astype(f32)
        doma_acc[:, hs] = dsh * inverse[:, hs]
    gain_grad[...] = gain_total
    sends = []
    for pair in range(heads * streams):
        copy = remote(going.at[pair], came.at[pair], (send_sem, recv_sem), pair, left)

        @pl.when(s < size - 1)
        def _(copy=copy):
            copy.wait_recv()

        state = came[pair].astype(f32)
        for b in reversed(range(per)):
            at = pair * per + b
            before = owed[at] + pass_ref[at][:, :1] * state
            owed[at] = state
            state = before
        going[pair] = state.astype(bf16)

        @pl.when(s > 0)
        def _(copy=copy):
            copy.start()

        sends.append(copy)
    row = lax.broadcasted_iota(jnp.int32, (BLOCK, 1), 0)
    for h in range(heads):
        hs, hd = slice(h * slots, (h + 1) * slots), slice(h * head, (h + 1) * head)
        for b in range(blocks):
            rb = rows_of(b)
            pair = h * streams + b // per
            at = pair * per + b % per
            leaving = owed[at]
            low = leaving.astype(bf16)
            part = kept[rb, hs].astype(bf16)
            dkept = dot(k_ref[rb, hd], low[:, :head], 1, 1) + dot(v_ref[rb, hd], low[:, head:], 1, 1)
            k_low[rb, hd] = (k_acc[rb, hd] + dot(part, low[:, :head])).astype(bf16)
            v_low[rb, hd] = (v_acc[rb, hd] + dot(part, low[:, head:])).astype(bf16)
            held = jnp.sum(low.astype(f32) * state_ref[pair, b % per + 1].astype(f32), axis=1, keepdims=True)
            held_row = to_row(held)
            da_acc[rb, hs] = (
                da_acc[rb, hs] - dkept * part.astype(f32) + jnp.where(row == BLOCK - 1, held_row, 0.0)
            )
            doma_acc[rb, hs] = doma_acc[rb, hs] + dkept * tail[rb, hs]
    dg = dot(lower, da_acc[...], 0, 0, count=3) - doma_acc[...] * (1.0 - oma)
    sig = jnp.where(z >= 0.0, u / (1.0 + u), 1.0 / (1.0 + u))
    dpre = dg * sig * 0.125
    forget_low[...] = dpre.astype(bf16)
    bias_grad[...] = jnp.sum(dpre, axis=0, keepdims=True)
    for copy in sends:

        @pl.when(s > 0)
        def _(copy=copy):
            copy.wait_send()


def to_row(col):
    n = col.shape[0]
    i = lax.broadcasted_iota(jnp.int32, (n, n), 0)
    j = lax.broadcasted_iota(jnp.int32, (n, n), 1)
    return jnp.sum(jnp.where(i == j, jnp.broadcast_to(col, (n, n)), 0.0), axis=0, keepdims=True)


def go_back(size, heads, q, k, v, pre, bias, fcol, frow, logits, gain, kept, delta):
    n, width = q.shape
    head, slots = width // heads, pre.shape[1] // heads
    pairs, per = heads * 2, n // BLOCK // 2
    return pl.pallas_call(
        functools.partial(return_kernel, size, heads),
        name="go_back",
        out_shape=[
            jax.ShapeDtypeStruct((n, width), bf16),
            jax.ShapeDtypeStruct((n, width), bf16),
            jax.ShapeDtypeStruct((n, width), bf16),
            jax.ShapeDtypeStruct(pre.shape, bf16),
            jax.ShapeDtypeStruct((n, width), bf16),
            jax.ShapeDtypeStruct((1, pre.shape[1]), f32),
            jax.ShapeDtypeStruct((1, head), f32),
        ],
        in_specs=[in_vmem()] * 17,
        out_specs=[in_vmem()] * 7,
        scratch_shapes=[
            VMEM((pairs * per, slots, 2 * head), f32),
            VMEM((pairs, slots, 2 * head), bf16),
            VMEM((pairs, slots, 2 * head), bf16),
            VMEM((n, width), f32),
            VMEM((n, width), f32),
            VMEM((8, 128), f32),
            VMEM(pre.shape, f32),
            VMEM(pre.shape, f32),
            pltpu.SemaphoreType.DMA((pairs,)),
            pltpu.SemaphoreType.DMA((pairs,)),
        ],
        compiler_params=pltpu.CompilerParams(
            collective_id=3, has_side_effects=True, vmem_limit_bytes=LIMIT
        ),
    )(q, k, v, pre, bias, fcol, frow, logits, gain, *kept, delta)


TILE = 256


def cut(columns, flip):
    tiles = columns // TILE
    if tiles <= 1:
        half = columns // 2
        return [(0, half, flip), (half, half, 1 - flip)]
    pieces = 2 if tiles <= 4 else 4
    out, start = [], 0
    for i in range(pieces):
        count = tiles // pieces + (1 if i < tiles % pieces else 0)
        out.append((start, count * TILE, (i + flip) % 2))
        start += count * TILE
    return out


def sum_kernel(lo, plan, n_left, n_right, *refs):
    zs = lo // 2
    lefts, refs = refs[:n_left], refs[n_left:]
    rights, refs = refs[:n_right], refs[n_right:]
    vec_in, refs = refs[0], refs[1:]
    outs, refs = refs[: len(plan)], refs[len(plan) :]
    vec_out, refs = refs[0], refs[1:]
    left_all, refs = refs[:n_left], refs[n_left:]
    right_all, refs = refs[:n_right], refs[n_right:]
    chunks = [(g,) + c for g, p in enumerate(plan) for c in p[5]]
    nc = len(chunks)
    sums, refs = refs[:nc], refs[nc:]
    first, refs = refs[:nc], refs[nc:]
    second, refs = refs[:nc], refs[nc:]
    third, refs = refs[:nc], refs[nc:]
    vec_acc, vec_got, local, in_send, in_recv, st_send, st_recv, z_send, z_recv, v_send, v_recv = refs
    s, f = lax.axis_index("seq"), lax.axis_index("fsdp")
    core, y = lax.rem(f, 2), f // 2
    low = lax.rem(s, lo)
    base = s - low
    x, z = lax.rem(low, 2), low // 2
    sib, far, nx = (s, f ^ 1), (s, f ^ 2), (s ^ 1, f)
    nz = [(base + lax.rem(z + d, zs) * 2 + x, f) for d in range(1, zs)]
    greet([sib, far, nx] + nz)
    started, own = [], []

    def go(copy):
        copy.start()
        started.append(copy)

    tokens = rights[0].shape[0]
    waiting = {}

    def exchange(kind, i):
        index = i if kind == 0 else n_left + i
        if (kind, i) in waiting:
            return
        if kind == 0:
            src_own, src_far = lefts[i].at[core], lefts[i].at[1 - core]
            dst_own, dst_far = left_all[i].at[:, pl.ds(0, tokens)], left_all[i].at[:, pl.ds(tokens, tokens)]
        else:
            src_own = src_far = rights[i]
            dst_own, dst_far = right_all[i].at[pl.ds(0, tokens)], right_all[i].at[pl.ds(tokens, tokens)]
        keep = pltpu.make_async_copy(src_own, dst_own, local.at[index])
        keep.start()
        copy = remote(src_far, dst_far, (in_send, in_recv), index, sib)
        go(copy)
        waiting[kind, i] = [keep, copy]

    def have(kind, i):
        pair = waiting[kind, i]
        if pair:
            pair[0].wait()
            pair[1].wait_recv()
            waiting[kind, i] = None

    for left, right, *_ in plan:
        exchange(0, left)
        exchange(1, right)

    def stage_copy(c, stage):
        order = chunks[c][3]
        ours, theirs = (y, 1 - y), (x, 1 - x)
        if stage == 0:
            other = (theirs if order else ours)[1]
            return remote(sums[c].at[other], first[c], (st_send, st_recv), (0, c), nx if order else far)
        if order:
            src = sums[c].at[x, 1 - y]
        else:
            src = sums[c].at[y, 1 - x]
        return remote(src, second[c], (st_send, st_recv), (1, c), far if order else nx)

    def z_copy(c, d):
        order = chunks[c][3]
        a, b = (x, y) if order else (y, x)
        src = sums[c].at[a, b, lax.rem(z + d, zs)]
        return remote(src, third[c].at[d - 1], (z_send, z_recv), (d - 1, c), nz[d - 1])

    def produce(c):
        g, start, width, order = chunks[c]
        left, right, columns, rows, kept, _ = plan[g]
        have(0, left)
        have(1, right)
        tile = min(TILE, width)

        def body(i, carry):
            at = pl.multiple_of(start + i * tile, 128)
            to = pl.multiple_of(i * tile, 128)
            got = jnp.dot(
                left_all[left][...], right_all[right][:, pl.ds(at, tile)], preferred_element_type=f32
            ).astype(bf16)
            for zz in range(zs):
                for xx in range(2):
                    for yy in range(2):
                        group = (zz * 2 + xx) * 2 + yy
                        a, b = (xx, yy) if order else (yy, xx)
                        sums[c][a, b, zz, :, pl.ds(to, tile)] = got[group * rows : (group + 1) * rows]
            return carry

        lax.fori_loop(0, width // tile, body, 0)
        go(stage_copy(c, 0))

    def after_first(c):
        order = chunks[c][3]
        stage_copy(c, 0).wait_recv()
        a = x if order else y
        for b in range(2):
            for zz in range(zs):
                sums[c][a, b, zz] = (
                    sums[c][a, b, zz].astype(f32) + first[c][b, zz].astype(f32)
                ).astype(bf16)
        go(stage_copy(c, 1))

    def after_second(c):
        order = chunks[c][3]
        stage_copy(c, 1).wait_recv()
        a, b = (x, y) if order else (y, x)
        for zz in range(zs):
            sums[c][a, b, zz] = (
                sums[c][a, b, zz].astype(f32) + second[c][zz].astype(f32)
            ).astype(bf16)
        for d in range(1, zs):
            go(z_copy(c, d))

    def after_third(c):
        g, start, width, order = chunks[c]
        kept = plan[g][4]
        a, b = (x, y) if order else (y, x)
        total = sums[c][a, b, z].astype(f32)
        for d in range(1, zs):
            z_copy(c, d).wait_recv()
            total = total + third[c][d - 1].astype(f32)
        outs[g][:, start : start + width] = total[:kept]

    def vector(step):
        if step == 0:
            vec_acc[0] = vec_in[...]
        elif step <= 3:
            v_copy(step - 1).wait_recv()
            vec_acc[step] = vec_acc[step - 1] + vec_got[step - 1]
        else:
            total = vec_acc[3]
            for d in range(1, zs):
                v_copy(2 + d).wait_recv()
                total = total + vec_got[2 + d]
            vec_out[...] = total
        if step < 3:
            go(v_copy(step))
        elif step == 3:
            for d in range(1, zs):
                go(v_copy(2 + d))

    def v_copy(i):
        partner = (sib, far, nx)[i] if i < 3 else nz[i - 3]
        return remote(vec_acc.at[min(i, 3)], vec_got.at[i], (v_send, v_recv), i, partner)

    lag = 2
    steps = nc + 3 * lag
    for t in range(steps):
        if t < nc:
            produce(t)
        if 0 <= t - lag < nc:
            after_first(t - lag)
        if 0 <= t - 2 * lag < nc:
            after_second(t - 2 * lag)
        if 0 <= t - 3 * lag < nc:
            after_third(t - 3 * lag)
        if steps - 7 <= t < steps - 2:
            vector(t - (steps - 7))
    for copy in started:
        copy.wait_send()


def sum_grads(lo, plan, lefts, rights, vectors):
    zs = lo // 2
    tokens = rights[0].shape[0]
    chunks = [(p[3],) + c for p in plan for c in p[5]]
    nc = len(chunks)
    dma = pltpu.SemaphoreType.DMA
    n_in = len(lefts) + len(rights)
    scratch = [VMEM((a.shape[1], 2 * tokens), bf16) for a in lefts]
    scratch += [VMEM((2 * tokens, b.shape[1]), bf16) for b in rights]
    scratch += [VMEM((2, 2, zs, r, w), bf16) for r, _, w, _ in chunks]
    scratch += [VMEM((2, zs, r, w), bf16) for r, _, w, _ in chunks]
    scratch += [VMEM((zs, r, w), bf16) for r, _, w, _ in chunks]
    scratch += [VMEM((zs - 1, r, w), bf16) for r, _, w, _ in chunks]
    scratch += [
        VMEM((4,) + vectors.shape, f32),
        VMEM((2 + zs,) + vectors.shape, f32),
        dma((n_in,)),
        dma((n_in,)),
        dma((n_in,)),
        dma((2, nc)),
        dma((2, nc)),
        dma((zs - 1, nc)),
        dma((zs - 1, nc)),
        dma((2 + zs,)),
        dma((2 + zs,)),
    ]
    out = pl.pallas_call(
        functools.partial(sum_kernel, lo, plan, len(lefts), len(rights)),
        name="sum_grads",
        out_shape=[jax.ShapeDtypeStruct((p[4], p[2]), f32) for p in plan]
        + [jax.ShapeDtypeStruct(vectors.shape, f32)],
        in_specs=[in_place()] * n_in + [in_vmem()],
        out_specs=[in_vmem()] * (len(plan) + 1),
        scratch_shapes=scratch,
        compiler_params=pltpu.CompilerParams(
            collective_id=4, has_side_effects=True, vmem_limit_bytes=LIMIT
        ),
    )(*lefts, *rights, vectors)
    return out[:-1], out[-1]


def rms_norm(values, gain):
    return values * lax.rsqrt(jnp.mean(values * values, axis=-1, keepdims=True) + norm_eps) * gain


def fore_dot(left, right):
    return jnp.dot(left, right, preferred_element_type=f32)


def back_dot(left, right):
    return lax.dot_general(left, right, (((1,), (1,)), ((), ())), preferred_element_type=f32)


def gated_unit(gate_vals, up_vals):
    return jax.nn.silu(gate_vals) * up_vals


def by_owner(a, hi, lo):
    tokens, features = a.shape
    r = features // (hi * lo * 4)
    t = a.reshape(tokens, hi, lo, 2, 2, r).transpose(4, 2, 3, 1, 5, 0).reshape(2, lo * 2, hi * r, tokens)
    pad = -(hi * r) % 16
    if pad:
        t = jnp.pad(t, ((0, 0), (0, 0), (0, pad), (0, 0)))
    return t.reshape(2, -1, tokens)


def body(
    size, tokens, resets, pre_gain, query_weight, key_weight, value_weight, forget_weight, forget_bias,
    outgate_weight, output_weight, head_gain, post_gain, gate_weight, up_weight, down_weight, cotangent,
):
    lo = 8 if size % 8 == 0 else size
    hi = size // lo
    streams, length, width = tokens.shape
    n = streams * length
    head = head_gain.shape[0]
    heads = width // head
    (wq, wk, wv, wf, wg, wo, w_gate, w_up, w_down) = gather(
        (
            query_weight, key_weight, value_weight, forget_weight, outgate_weight, output_weight,
            gate_weight, up_weight, down_weight,
        )
    )
    inputs = tokens.reshape(n, width).astype(f32)
    cotan = cotangent.reshape(n, width)
    flags = resets.reshape(n).astype(f32)
    fcol = jnp.broadcast_to(flags[:, None], (n, 128))
    frow = jnp.broadcast_to(flags[None], (8, n))
    bias, gain = forget_bias[None], head_gain[None]
    normed_full, norm_back = jax.vjp(rms_norm, inputs, pre_gain)
    normed = normed_full.astype(bf16)
    q = fore_dot(normed, wq).astype(bf16)
    k = fore_dot(normed, wk).astype(bf16)
    v = fore_dot(normed, wv).astype(bf16)
    pre = fore_dot(normed, wf)
    logits = fore_dot(normed, wg)
    merged, *kept = attend(size, heads, q, k, v, pre, bias, fcol, frow, logits, gain)
    hidden_one = inputs + fore_dot(merged, wo)
    normed_second, second_back = jax.vjp(rms_norm, hidden_one, post_gain)
    normed_two = normed_second.astype(bf16)
    gate_vals = fore_dot(normed_two, w_gate)
    up_vals = fore_dot(normed_two, w_up)
    hidden_full, unit_back = jax.vjp(gated_unit, gate_vals, up_vals)
    hidden = hidden_full.astype(bf16)
    block_output = (hidden_one + fore_dot(hidden, w_down)).astype(bf16)
    hidden_delta = back_dot(cotan, w_down)
    gate_full, up_full = unit_back(hidden_delta)
    gate_delta = gate_full.astype(bf16)
    up_delta = up_full.astype(bf16)
    second_delta = back_dot(gate_delta, w_gate) + back_dot(up_delta, w_up)
    through_norm, postgain_grad = second_back(second_delta)
    first_delta = cotan.astype(f32) + through_norm
    attn_delta = first_delta.astype(bf16)
    merged_delta = back_dot(attn_delta, wo)
    q_low, k_low, v_low, forget_low, logit_low, bias_grad, headgain_grad = go_back(
        size, heads, q, k, v, pre, bias, fcol, frow, logits, gain, kept, merged_delta
    )
    normed_delta = (
        back_dot(q_low, wq)
        + back_dot(k_low, wk)
        + back_dot(v_low, wv)
        + back_dot(forget_low, wf)
        + back_dot(logit_low, wg)
    )
    input_delta, pregain_grad = norm_back(normed_delta)
    input_grad = (first_delta + input_delta).astype(bf16)

    order = functools.partial(by_owner, hi=hi, lo=lo)
    lefts = [order(hidden), order(normed_two), order(merged), order(normed)]
    rights = [cotan, gate_delta, up_delta, attn_delta, logit_low, q_low, k_low, v_low, forget_low]
    which = (0, 1, 1, 2, 3, 3, 3, 3, 3)
    features = (hidden.shape[1],) + (width,) * 8
    plan = []
    for i, (left, right) in enumerate(zip(which, rights)):
        kept_rows = features[i] // (lo * 4)
        columns = right.shape[1]
        plan.append((left, i, columns, -(-kept_rows // 16) * 16, kept_rows, tuple(cut(columns, i % 2))))
    sizes = (width, bias.shape[1], head, width)
    vectors = jnp.concatenate([pregain_grad, bias_grad[0], headgain_grad[0], postgain_grad])
    total = vectors.shape[0]
    vectors = jnp.pad(vectors, (0, -total % 1024)).reshape(8, -1)
    grads, vectors = sum_grads(lo, tuple(plan), lefts, rights, vectors)
    if hi > 1:
        alike = [[a * lo + b for a in range(hi)] for b in range(lo)]
        grads = [
            lax.psum_scatter(g, "seq", scatter_dimension=0, axis_index_groups=alike, tiled=True)
            for g in grads
        ]
        vectors = lax.psum(vectors, "seq", axis_index_groups=alike)
    down_grad, gate_grad, up_grad, output_grad, outgate_grad, query_grad, key_grad, value_grad, forget_grad = grads
    vectors = vectors.reshape(-1)
    ends = [sum(sizes[: i + 1]) for i in range(4)]
    pregain, bias_total, headgain, postgain = [vectors[e - w : e] for e, w in zip(ends, sizes)]
    shape = tokens.shape
    return (
        block_output.reshape(shape), input_grad.reshape(shape), pregain, query_grad, key_grad, value_grad,
        forget_grad, bias_total, outgate_grad, output_grad, headgain, postgain, gate_grad, up_grad, down_grad,
    )


def solution(mesh):
    rows, whole, both = P("fsdp", None), P(), P(("seq", "fsdp"), None)
    return jax.shard_map(
        functools.partial(body, mesh.shape["seq"]),
        mesh=mesh,
        in_specs=(
            P("fsdp", "seq", None), P("fsdp", "seq"), whole, rows, rows, rows, rows, whole, rows, rows,
            whole, whole, rows, rows, rows, P("fsdp", "seq", None),
        ),
        out_specs=(
            P("fsdp", "seq", None), P("fsdp", "seq", None), whole, both, both, both, both, whole, both,
            both, whole, whole, both, both, both,
        ),
        check_vma=False,
    )
```

time: 2090 us -> 530 us (0.25)
  waiting for transfers between devices: 1470 us -> 0 us
  Pallas kernels: 0 us -> 457 us
  matrix products: 240 us -> 39.7 us
  other arithmetic: 117 us -> 3.9 us
  local copies, waits for them, and re-layouts: 136 us -> 23.3 us
  blocking collectives: 85.2 us -> 0 us
    reduce_scatter x9 -> x0, waiting for transfers between devices: 1190 us -> none  [the longest x1 156 us: body(): lax.psum_scatter(matrices[8], ('seq', 'fsdp'), scatter_dimension=0, tiled...]
    pallas_call x0 -> x4, Pallas kernels: none -> 457 us  [the longest x1 221 us: gather(): pl.pallas_call(functools.partial(gather_kernel, count), name='gather', ou...]
    all_gather x16 -> x0, waiting for transfers between devices: 278 us -> none  [the longest x4 80.4 us: carried_in(): lax.all_gather(part.astype(kind), axis)]
    dot_general x188 -> x9, matrix products: 204 us -> 23 us  [fore_dot(): return jnp.dot(left, right, preferred_element_type=f32)]
    all_gather x3 -> x0, blocking collectives: 46.5 us -> none  [the longest x2 37.9 us: entering(): lax.all_gather(part.astype(kind), axis)]
    psum x1 -> x0, blocking collectives: 38.6 us -> none  [body(): lax.psum((vectors[0], vectors[1], vectors[2], vectors[3]), ('seq', 'fsdp'))]
    convert_element_type x69 -> x6, other arithmetic: 40.9 us -> 3.47 us  [the longest x1 2.68 us: body(): input_grad = (first_delta + input_delta).astype(bf16)]
    select_n x32 -> x0, other arithmetic: 35.5 us -> none  [the longest x16 17.8 us: entering_turn(): return jax.tree.map(lambda a, b: jnp.where(reached, a, b), new, before)]
  transfers between devices with their start and end apart: 25 -> 0, of which waited for: 20 -> 0; matrix products, arithmetic and copies ran while one was open for 15% -> 0% of each run, Pallas kernels for 0% -> 0%
where the time goes in v1:
time: 530 us; the launch traced here: 525 us
  Pallas kernels  457 us (86%)
  matrix products  39.7 us (7%)
  local copies, waits for them, and re-layouts  23.3 us (4%)
    pallas_call x1, Pallas kernels, gather(): pl.pallas_call(functools.partial(gather_kernel, count), name='gather', ou...  221 us
    pallas_call x1, Pallas kernels, sum_grads(): pl.pallas_call(functools.partial(sum_kernel, lo, plan, len(lefts), len(ri...  145 us
    pallas_call x1, Pallas kernels, go_back(): pl.pallas_call(functools.partial(return_kernel, size, heads), name='go_ba...  69.3 us
    dot_general x9, matrix products, fore_dot(): return jnp.dot(left, right, preferred_element_type=f32)  23 us
    pallas_call x1, Pallas kernels, attend(): pl.pallas_call(functools.partial(attend_kernel, size, heads), name='atten...  22.3 us
    dot_general x9, matrix products, back_dot(): lax.dot_general(left, right, (((1,), (1,)), ((), ())), preferred_element_...  16.8 us

profile of v1, /device:TPU:0, one launch (start us, length us, event | category | flops | bytes accessed | tf_op | source)
XLA Modules:
  0.0 525.4 jit_solution(12333561348593230278)
XLA Ops:
  0.7 220.6 %gather.1 = (bf16[4,256,1024]{2,1,0:T(8,128)(2,1)}, bf16[4,256,1024]{2,1,0:T(8,128)(2,1)}, bf16[4,256,1024]{2,1,0:T(8,128)(2,1)}, bf16[4,256,256]{2,1,0:T(8,128)...) custom-call(bf16[256,1024]{1,0:T(8,128)(2,1)} %refs_0_.1, ...), custom_call_target="tpu_custom_call" | custom-call | tf_op jit(solution)/shard_map/gather/pallas_call | solution.py:121
  221.7 3.4 fusion.22.logit_ref
  225.1 1.5 convolution_convert_fusion.v_ref
  226.7 1.5 convolution_convert_fusion.1.k_ref
  228.3 1.5 convolution_convert_fusion.2.q_ref
  229.8 1.0 fusion.21.pre_ref
  230.8 0.8 broadcast_in_dim.13.fcol_ref
  232.2 22.3 %attend.1 = (bf16[256,1024]{1,0:T(8,128)(2,1)}, f32[256,1024]{1,0:T(8,128)}, bf16[4,256,256]{2,1,0:T(8,128)(2,1)}, bf16[4,256,256]{2,1,0:T(8,128)(2,1)}, f32[256...) custom-call(bf16[256,1024]{1,0:T(8,128)(2,1)} %convolution_convert_fusion.2.q_ref, ...), custom_call_target="tpu_custom_call" | custom-call | tf_op jit(solution)/shard_map/attend/pallas_call | solution.py:315
  254.6 2.6 multiply_reduce_fusion.2
  257.3 4.4 fusion.24
  261.8 1.7 fusion.23
  263.6 4.3 multiply_convert_fusion
  268.0 1.7 fusion.25
  269.7 1.9 multiply_reduce_fusion
  272.0 1.6 copy-done.2
  273.6 1.8 fusion.26.delta_ref
  275.4 69.3 %go_back.1 = (bf16[256,1024]{1,0:T(8,128)(2,1)}, bf16[256,1024]{1,0:T(8,128)(2,1)}, bf16[256,1024]{1,0:T(8,128)(2,1)}, bf16[256,256]{1,0:T(8,128)(2,1)}, bf16[25...) custom-call(bf16[256,1024]{1,0:T(8,128)(2,1)} %convolution_convert_fusion.2.q_ref, ...), custom_call_target="tpu_custom_call" | custom-call | tf_op jit(solution)/shard_map/go_back/pallas_call | solution.py:481
  344.7 2.6 fusion.27
  347.4 0.7 convolution_add_fusion.2
  349.2 0.7 convolution_add_fusion.1
  349.9 0.8 copy-done.1
  351.6 2.2 fusion.14
  354.4 1.4 copy.43
  355.9 2.1 reshape.255
  358.2 0.8 copy.44
  359.1 1.7 copy.37
  360.9 1.4 pad.8
  362.4 0.8 copy.40
  363.5 0.8 copy.42
  364.3 144.7 %sum_grads.1 = (f32[88,1024]{1,0:T(8,128)}, f32[32,2816]{1,0:T(8,128)}, f32[32,2816]{1,0:T(8,128)}, f32[32,1024]{1,0:T(8,128)}, f32[32,1024]{1,0:T(8,128)}, /*in...) custom-call(bf16[2,1536,256]{2,1,0:T(8,128)(2,1)} %bitcast.104, ...), custom_call_target="tpu_custom_call" | custom-call | tf_op jit(solution)/shard_map/sum_grads/pallas_call | solution.py:729
  511.0 2.7 fusion.8
  513.7 5.3 %fusion.5 = bf16[256,1024]{1,0:T(8,128)(2,1)} fusion(f32[256,1024]{1,0:T(8,128)S(1)} %get-tuple-element.95, bf16[256,2816]{1,0:T(8,128)(2,1)S(1)} %copy-done.20, bf16[2816,1024]{1,0:T(8,128)(2,1)} %bitcast.134), kind=kOutput, calls=%fused_computation.18 | convolution fusion | flops 1476919296 | bytes 8781824 | tf_op jit(solution)/shard_map/dot_general | solution.py:749
  (126 shorter events, 13.1 us)
Async XLA Ops:
  0.7 220.6 %copy-start = (bf16[2,128,1024]{2,1,0:T(8,128)(2,1)S(1)}, bf16[2,128,1024]{2,1,0:T(8,128)(2,1)}, u32[]{:S(2)}) copy-start(bf16[2,128,1024]{2,1,0:T(8,128)(2,1)} %param.16) | copy-start | bytes 1572868
  0.7 220.8 %copy-start.30 = (f32[1024]{0:T(1024)S(1)}, f32[1024]{0:T(1024)}, u32[]{:S(2)}) copy-start(f32[1024]{0:T(1024)} %param.18) | copy-start | bytes 12292
  221.7 3.4 copy-start.13
  228.3 2.5 copy-start.40
  254.5 2.6 copy-start.31
  257.2 4.6 slice-start.4
  257.3 4.5 slice-start.5
  257.3 6.2 %slice-start = ((s8[5767168]{0:T(1024)(128)(4,1)}), s8[4194304]{0:T(1024)(128)(4,1)S(1)}, s32[]{:S(2)}) async-start(s8[5767168]{0:T(1024)(128)(4,1)} %bitcast.135), calls=%async_computation | async-start | bytes 8388608
  261.8 7.8 %slice-start.2 = ((s8[5767168]{0:T(1024)(128)(4,1)}), s8[4194304]{0:T(1024)(128)(4,1)S(1)}, s32[]{:S(2)}) async-start(s8[5767168]{0:T(1024)(128)(4,1)} %bitcast.139), calls=%async_computation.2 | async-start | bytes 8388608
  263.6 6.1 %slice-start.3 = ((s8[5767168]{0:T(1024)(128)(4,1)}), s8[1572864]{0:T(1024)(128)(4,1)S(1)}, s32[]{:S(2)}) async-start(s8[5767168]{0:T(1024)(128)(4,1)} %bitcast.139), calls=%async_computation.3 | async-start | bytes 3145728
  271.6 3.8 copy-start.6
  271.7 3.7 copy-start.35
  271.7 86.3 %copy-start.33 = (f32[256]{0:T(256)}, f32[256]{0:T(256)S(1)}, u32[]{:S(2)}) copy-start(f32[256]{0:T(256)S(1)} %get-tuple-element.98) | copy-start | bytes 3076
  273.6 71.1 %copy-start.3 = (bf16[256,1024]{1,0:T(8,128)(2,1)}, bf16[256,1024]{1,0:T(8,128)(2,1)S(1)}, u32[]{:S(2)}) copy-start(bf16[256,1024]{1,0:T(8,128)(2,1)S(1)} %fusion.18.refs_7_) | copy-start | bytes 1572868
  344.7 2.7 copy-start.8
  344.7 2.7 copy-start.16
  360.8 2.4 copy-start.12
  364.3 146.6 %copy-start.37 = (f32[256]{0:T(256)S(1)}, f32[256]{0:T(256)}, u32[]{:S(2)}) copy-start(f32[256]{0:T(256)} %get-tuple-element.86) | copy-start | bytes 3076
  364.3 146.6 %copy-start.5 = (bf16[2,128,1024]{2,1,0:T(8,128)(2,1)S(1)}, bf16[2,128,1024]{2,1,0:T(8,128)(2,1)}, u32[]{:S(2)}) copy-start(bf16[2,128,1024]{2,1,0:T(8,128)(2,1)} %param.31) | copy-start | bytes 1572868
  364.3 146.6 %copy-start.7 = (f32[256,1024]{1,0:T(8,128)S(1)}, f32[256,1024]{1,0:T(8,128)}, u32[]{:S(2)}) copy-start(f32[256,1024]{1,0:T(8,128)} %copy-done.6) | copy-start | bytes 3145732
  364.3 146.6 %copy-start.34 = (f32[256]{0:T(256)S(1)}, f32[256]{0:T(256)}, u32[]{:S(2)}) copy-start(f32[256]{0:T(256)} %copy-done.33) | copy-start | bytes 3076
  364.3 146.6 %copy-start.36 = (f32[256]{0:T(256)S(1)}, f32[256]{0:T(256)}, u32[]{:S(2)}) copy-start(f32[256]{0:T(256)} %copy-done.35) | copy-start | bytes 3076
  510.9 2.7 copy-start.20
  513.6 5.3 %copy-start.29 = (f32[32,1024]{1,0:T(8,128)S(1)}, f32[32,1024]{1,0:T(8,128)}, u32[]{:S(2)}) copy-start(f32[32,1024]{1,0:T(8,128)} %get-tuple-element.118) | copy-start | bytes 393220
  513.6 6.0 %copy-start.28 = (f32[32,1024]{1,0:T(8,128)S(1)}, f32[32,1024]{1,0:T(8,128)}, u32[]{:S(2)}) copy-start(f32[32,1024]{1,0:T(8,128)} %get-tuple-element.119) | copy-start | bytes 393220
  513.7 6.6 %copy-start.27 = (f32[32,1024]{1,0:T(8,128)S(1)}, f32[32,1024]{1,0:T(8,128)}, u32[]{:S(2)}) copy-start(f32[32,1024]{1,0:T(8,128)} %get-tuple-element.120) | copy-start | bytes 393220
  513.7 7.3 %copy-start.32 = (f32[32,256]{1,0:T(8,128)S(1)}, f32[32,256]{1,0:T(8,128)}, u32[]{:S(2)}) copy-start(f32[32,256]{1,0:T(8,128)} %get-tuple-element.121) | copy-start | bytes 98308
  513.7 7.9 %copy-start.26 = (f32[32,1024]{1,0:T(8,128)S(1)}, f32[32,1024]{1,0:T(8,128)}, u32[]{:S(2)}) copy-start(f32[32,1024]{1,0:T(8,128)} %get-tuple-element.123) | copy-start | bytes 393220
  513.7 8.6 %copy-start.25 = (f32[32,1024]{1,0:T(8,128)S(1)}, f32[32,1024]{1,0:T(8,128)}, u32[]{:S(2)}) copy-start(f32[32,1024]{1,0:T(8,128)} %get-tuple-element.124) | copy-start | bytes 393220
  513.7 9.2 %copy-start.24 = (f32[32,2816]{1,0:T(8,128)S(1)}, f32[32,2816]{1,0:T(8,128)}, u32[]{:S(2)}) copy-start(f32[32,2816]{1,0:T(8,128)} %get-tuple-element.127) | copy-start | bytes 1081348
  519.0 4.7 copy-start.23
  519.0 5.4 %copy-start.22 = (f32[88,1024]{1,0:T(8,128)S(1)}, f32[88,1024]{1,0:T(8,128)}, u32[]{:S(2)}) copy-start(f32[88,1024]{1,0:T(8,128)} %get-tuple-element.129) | copy-start | bytes 1081348
  (15 other events, 25.8 us)

commit v2 on v1

--- a/solution.py
+++ b/solution.py
@@ -43,8 +43,8 @@
 
 
 def gather_kernel(count, *refs):
-    shards, wholes = refs[:count], refs[count : 2 * count]
-    local, *sems = refs[2 * count :]
+    shards, wholes, held = refs[:count], refs[count : 2 * count], refs[2 * count : 3 * count]
+    local, *sems = refs[3 * count :]
     s, f = lax.axis_index("seq"), lax.axis_index("fsdp")
     q = lax.rem(s, 4)
     sib, far, nx, nz = (s, f ^ 1), (s, f ^ 2), (s ^ 1, f), (s ^ 2, f)
@@ -77,9 +77,13 @@
     own = []
     for m in range(count):
         go(remote(shards[m], wholes[m].at[f], sems, (0, m), sib))
-        copy = pltpu.make_async_copy(shards[m], wholes[m].at[f], local.at[m])
+        copy = pltpu.make_async_copy(shards[m], held[m], local.at[0, m])
         copy.start()
         own.append(copy)
+    for m in range(count):
+        own[m].wait()
+        own[m] = pltpu.make_async_copy(held[m], wholes[m].at[f], local.at[1, m])
+        own[m].start()
     for step in range(count + 2):
         if step < count:
             m = step
@@ -124,12 +128,15 @@
         out_shape=[jax.ShapeDtypeStruct((4,) + w.shape, w.dtype) for w in shards],
         in_specs=[in_place()] * count,
         out_specs=[in_place()] * count,
-        scratch_shapes=[
-            pltpu.SemaphoreType.DMA((count,)),
+        scratch_shapes=[VMEM(w.shape, w.dtype) for w in shards]
+        + [
+            pltpu.SemaphoreType.DMA((2, count)),
             pltpu.SemaphoreType.DMA((11, count)),
             pltpu.SemaphoreType.DMA((11, count)),
         ],
-        compiler_params=pltpu.CompilerParams(collective_id=1, has_side_effects=True),
+        compiler_params=pltpu.CompilerParams(
+            collective_id=1, has_side_effects=True, vmem_limit_bytes=LIMIT
+        ),
     )(*shards)
     return [w.reshape((-1, w.shape[-1])) for w in wholes]
 

time: 530 us -> 384 us (0.72)
  Pallas kernels: 457 us -> 311 us
    pallas_call x1, Pallas kernels: 221 us -> 72 us  [gather(): pl.pallas_call(functools.partial(gather_kernel, count), name='gather', ou...]
where the time goes in v2:
time: 384 us; the launch traced here: 379 us
  Pallas kernels  311 us (81%)
  matrix products  39.7 us (10%)
  local copies, waits for them, and re-layouts  23.3 us (6%)
  other arithmetic  3.9 us (1%)
    pallas_call x1, Pallas kernels, sum_grads(): pl.pallas_call(functools.partial(sum_kernel, lo, plan, len(lefts), len(ri...  145 us
    pallas_call x1, Pallas kernels, gather(): pl.pallas_call(functools.partial(gather_kernel, count), name='gather', ou...  72 us
    pallas_call x1, Pallas kernels, go_back(): pl.pallas_call(functools.partial(return_kernel, size, heads), name='go_ba...  71.2 us
    dot_general x9, matrix products, fore_dot(): return jnp.dot(left, right, preferred_element_type=f32)  23 us
    pallas_call x1, Pallas kernels, attend(): pl.pallas_call(functools.partial(attend_kernel, size, heads), name='atten...  22.3 us
    dot_general x9, matrix products, back_dot(): lax.dot_general(left, right, (((1,), (1,)), ((), ())), preferred_element_...  16.8 us
    unnamed x103, local copies, waits for them, and re-layouts  9.87 us

profile of v2, /device:TPU:0, one launch (start us, length us, event | category | flops | bytes accessed | tf_op | source)
XLA Modules:
  0.0 379.2 jit_solution(2430040930865382192)
XLA Ops:
  0.7 72.0 %gather.1 = (bf16[4,256,1024]{2,1,0:T(8,128)(2,1)}, bf16[4,256,1024]{2,1,0:T(8,128)(2,1)}, bf16[4,256,1024]{2,1,0:T(8,128)(2,1)}, bf16[4,256,256]{2,1,0:T(8,128)...) custom-call(bf16[256,1024]{1,0:T(8,128)(2,1)} %refs_0_.1, ...), custom_call_target="tpu_custom_call" | custom-call | tf_op jit(solution)/shard_map/gather/pallas_call | solution.py:125
  73.1 3.4 fusion.22.logit_ref
  76.5 1.5 convolution_convert_fusion.v_ref
  78.1 1.5 convolution_convert_fusion.1.k_ref
  79.7 1.5 convolution_convert_fusion.2.q_ref
  81.2 1.0 fusion.21.pre_ref
  82.2 0.8 broadcast_in_dim.13.fcol_ref
  83.5 22.3 %attend.1 = (bf16[256,1024]{1,0:T(8,128)(2,1)}, f32[256,1024]{1,0:T(8,128)}, bf16[4,256,256]{2,1,0:T(8,128)(2,1)}, bf16[4,256,256]{2,1,0:T(8,128)(2,1)}, f32[256...) custom-call(bf16[256,1024]{1,0:T(8,128)(2,1)} %convolution_convert_fusion.2.q_ref, ...), custom_call_target="tpu_custom_call" | custom-call | tf_op jit(solution)/shard_map/attend/pallas_call | solution.py:322
  106.0 2.6 multiply_reduce_fusion.2
  108.7 4.4 %fusion.24 = f32[256,2816]{1,0:T(8,128)S(1)} fusion(bf16[256,1024]{1,0:T(8,128)(2,1)S(1)} %multiply_convert_fusion.3, bf16[1024,2816]{1,0:T(8,128)(2,1)} %bitcast.138), kind=kOutput, calls=%fused_computation.61 | convolution fusion | flops 1476395008 | bytes 9175040 | tf_op jit(solution)/shard_map/dot_general | solution.py:756
  113.2 1.7 fusion.23
  115.0 4.3 %multiply_convert_fusion = (bf16[256,2816]{1,0:T(8,128)(2,1)S(1)}, bf16[256,2816]{1,0:T(8,128)(2,1)S(1)}, bf16[256,2816]{1,0:T(8,128)(2,1)}) fusion(f32[256,2816]{1,0:T(8,128)S(1)} %fusion.23, f32[256,2816]{1,0:T(8,128)S(1)} %fusion.24, bf16[2816,1024]{1,0:T(8,128)(2,1)S(1)} %bitcast.137, bf16[256,1024]{1,0:T(8,128)(2,1)S(1)} %bitcast.112), kind=kOutput, calls=%fused_computation.5 | convolution fusion | flops 1487929344 | bytes 16384000 | tf_op jit(solution)/shard_map/dot_general | solution.py:760
  119.4 1.7 fusion.25
  121.1 1.9 multiply_reduce_fusion
  123.4 1.6 copy-done.2
  125.0 1.8 fusion.26.delta_ref
  126.8 71.2 %go_back.1 = (bf16[256,1024]{1,0:T(8,128)(2,1)}, bf16[256,1024]{1,0:T(8,128)(2,1)}, bf16[256,1024]{1,0:T(8,128)(2,1)}, bf16[256,256]{1,0:T(8,128)(2,1)}, bf16[25...) custom-call(bf16[256,1024]{1,0:T(8,128)(2,1)} %convolution_convert_fusion.2.q_ref, ...), custom_call_target="tpu_custom_call" | custom-call | tf_op jit(solution)/shard_map/go_back/pallas_call | solution.py:488
  198.0 2.6 fusion.27
  200.7 0.7 convolution_add_fusion.2
  202.4 0.7 convolution_add_fusion.1
  203.2 0.8 copy-done.1
  204.9 2.2 fusion.14
  207.7 1.4 copy.43
  209.1 2.1 reshape.255
  211.5 0.8 copy.44
  212.3 1.7 copy.37
  214.1 1.4 pad.8
  215.7 0.8 copy.40
  216.7 0.8 copy.42
  217.6 145.2 %sum_grads.1 = (f32[88,1024]{1,0:T(8,128)}, f32[32,2816]{1,0:T(8,128)}, f32[32,2816]{1,0:T(8,128)}, f32[32,1024]{1,0:T(8,128)}, f32[32,1024]{1,0:T(8,128)}, /*in...) custom-call(bf16[2,1536,256]{2,1,0:T(8,128)(2,1)} %bitcast.104, ...), custom_call_target="tpu_custom_call" | custom-call | tf_op jit(solution)/shard_map/sum_grads/pallas_call | solution.py:736
  364.7 2.7 fusion.8
  367.5 5.3 %fusion.5 = bf16[256,1024]{1,0:T(8,128)(2,1)} fusion(f32[256,1024]{1,0:T(8,128)S(1)} %get-tuple-element.95, bf16[256,2816]{1,0:T(8,128)(2,1)S(1)} %copy-done.20, bf16[2816,1024]{1,0:T(8,128)(2,1)} %bitcast.134), kind=kOutput, calls=%fused_computation.18 | convolution fusion | flops 1476919296 | bytes 8781824 | tf_op jit(solution)/shard_map/dot_general | solution.py:756
  (126 shorter events, 13.1 us)
Async XLA Ops:
  0.7 72.0 %copy-start = (bf16[2,128,1024]{2,1,0:T(8,128)(2,1)S(1)}, bf16[2,128,1024]{2,1,0:T(8,128)(2,1)}, u32[]{:S(2)}) copy-start(bf16[2,128,1024]{2,1,0:T(8,128)(2,1)} %param.16) | copy-start | bytes 1572868
  0.7 72.2 %copy-start.30 = (f32[1024]{0:T(1024)S(1)}, f32[1024]{0:T(1024)}, u32[]{:S(2)}) copy-start(f32[1024]{0:T(1024)} %param.18) | copy-start | bytes 12292
  73.1 3.4 copy-start.13
  79.7 2.5 copy-start.40
  105.9 2.6 copy-start.31
  108.5 4.6 %slice-start.4 = ((s8[5767168]{0:T(1024)(128)(4,1)}), s8[4194304]{0:T(1024)(128)(4,1)S(1)}, s32[]{:S(2)}) async-start(s8[5767168]{0:T(1024)(128)(4,1)} %bitcast.142), calls=%async_computation.4 | async-start | bytes 8388608
  108.7 4.5 %slice-start.5 = ((s8[5767168]{0:T(1024)(128)(4,1)}), s8[1572864]{0:T(1024)(128)(4,1)S(1)}, s32[]{:S(2)}) async-start(s8[5767168]{0:T(1024)(128)(4,1)} %bitcast.142), calls=%async_computation.5 | async-start | bytes 3145728
  108.7 6.2 %slice-start = ((s8[5767168]{0:T(1024)(128)(4,1)}), s8[4194304]{0:T(1024)(128)(4,1)S(1)}, s32[]{:S(2)}) async-start(s8[5767168]{0:T(1024)(128)(4,1)} %bitcast.135), calls=%async_computation | async-start | bytes 8388608
  113.2 7.8 %slice-start.2 = ((s8[5767168]{0:T(1024)(128)(4,1)}), s8[4194304]{0:T(1024)(128)(4,1)S(1)}, s32[]{:S(2)}) async-start(s8[5767168]{0:T(1024)(128)(4,1)} %bitcast.139), calls=%async_computation.2 | async-start | bytes 8388608
  115.0 6.1 %slice-start.3 = ((s8[5767168]{0:T(1024)(128)(4,1)}), s8[1572864]{0:T(1024)(128)(4,1)S(1)}, s32[]{:S(2)}) async-start(s8[5767168]{0:T(1024)(128)(4,1)} %bitcast.139), calls=%async_computation.3 | async-start | bytes 3145728
  123.0 3.8 copy-start.6
  123.1 3.7 copy-start.35
  123.1 88.2 %copy-start.33 = (f32[256]{0:T(256)}, f32[256]{0:T(256)S(1)}, u32[]{:S(2)}) copy-start(f32[256]{0:T(256)S(1)} %get-tuple-element.98) | copy-start | bytes 3076
  125.0 73.0 %copy-start.3 = (bf16[256,1024]{1,0:T(8,128)(2,1)}, bf16[256,1024]{1,0:T(8,128)(2,1)S(1)}, u32[]{:S(2)}) copy-start(bf16[256,1024]{1,0:T(8,128)(2,1)S(1)} %fusion.18.refs_7_) | copy-start | bytes 1572868
  198.0 2.7 copy-start.8
  198.0 2.7 copy-start.16
  214.1 2.4 copy-start.12
  217.6 147.1 %copy-start.37 = (f32[256]{0:T(256)S(1)}, f32[256]{0:T(256)}, u32[]{:S(2)}) copy-start(f32[256]{0:T(256)} %get-tuple-element.86) | copy-start | bytes 3076
  217.6 147.1 %copy-start.5 = (bf16[2,128,1024]{2,1,0:T(8,128)(2,1)S(1)}, bf16[2,128,1024]{2,1,0:T(8,128)(2,1)}, u32[]{:S(2)}) copy-start(bf16[2,128,1024]{2,1,0:T(8,128)(2,1)} %param.31) | copy-start | bytes 1572868
  217.6 147.1 %copy-start.7 = (f32[256,1024]{1,0:T(8,128)S(1)}, f32[256,1024]{1,0:T(8,128)}, u32[]{:S(2)}) copy-start(f32[256,1024]{1,0:T(8,128)} %copy-done.6) | copy-start | bytes 3145732
  217.6 147.1 %copy-start.34 = (f32[256]{0:T(256)S(1)}, f32[256]{0:T(256)}, u32[]{:S(2)}) copy-start(f32[256]{0:T(256)} %copy-done.33) | copy-start | bytes 3076
  217.6 147.1 %copy-start.36 = (f32[256]{0:T(256)S(1)}, f32[256]{0:T(256)}, u32[]{:S(2)}) copy-start(f32[256]{0:T(256)} %copy-done.35) | copy-start | bytes 3076
  364.7 2.7 copy-start.20
  367.4 5.3 %copy-start.29 = (f32[32,1024]{1,0:T(8,128)S(1)}, f32[32,1024]{1,0:T(8,128)}, u32[]{:S(2)}) copy-start(f32[32,1024]{1,0:T(8,128)} %get-tuple-element.118) | copy-start | bytes 393220
  367.4 6.0 %copy-start.28 = (f32[32,1024]{1,0:T(8,128)S(1)}, f32[32,1024]{1,0:T(8,128)}, u32[]{:S(2)}) copy-start(f32[32,1024]{1,0:T(8,128)} %get-tuple-element.119) | copy-start | bytes 393220
  367.4 6.7 %copy-start.27 = (f32[32,1024]{1,0:T(8,128)S(1)}, f32[32,1024]{1,0:T(8,128)}, u32[]{:S(2)}) copy-start(f32[32,1024]{1,0:T(8,128)} %get-tuple-element.120) | copy-start | bytes 393220
  367.4 7.3 %copy-start.32 = (f32[32,256]{1,0:T(8,128)S(1)}, f32[32,256]{1,0:T(8,128)}, u32[]{:S(2)}) copy-start(f32[32,256]{1,0:T(8,128)} %get-tuple-element.121) | copy-start | bytes 98308
  367.4 7.9 %copy-start.26 = (f32[32,1024]{1,0:T(8,128)S(1)}, f32[32,1024]{1,0:T(8,128)}, u32[]{:S(2)}) copy-start(f32[32,1024]{1,0:T(8,128)} %get-tuple-element.123) | copy-start | bytes 393220
  367.4 8.6 %copy-start.25 = (f32[32,1024]{1,0:T(8,128)S(1)}, f32[32,1024]{1,0:T(8,128)}, u32[]{:S(2)}) copy-start(f32[32,1024]{1,0:T(8,128)} %get-tuple-element.124) | copy-start | bytes 393220
  367.4 9.2 %copy-start.24 = (f32[32,2816]{1,0:T(8,128)S(1)}, f32[32,2816]{1,0:T(8,128)}, u32[]{:S(2)}) copy-start(f32[32,2816]{1,0:T(8,128)} %get-tuple-element.127) | copy-start | bytes 1081348
  372.7 4.7 %copy-start.23 = (f32[32,2816]{1,0:T(8,128)S(1)}, f32[32,2816]{1,0:T(8,128)}, u32[]{:S(2)}) copy-start(f32[32,2816]{1,0:T(8,128)} %get-tuple-element.128) | copy-start | bytes 1081348
  372.7 5.4 %copy-start.22 = (f32[88,1024]{1,0:T(8,128)S(1)}, f32[88,1024]{1,0:T(8,128)}, u32[]{:S(2)}) copy-start(f32[88,1024]{1,0:T(8,128)} %get-tuple-element.129) | copy-start | bytes 1081348
  (15 other events, 25.8 us)

commit v3 on v1

v3 whole, which is shorter than its diff:
```python
import functools

import jax
import jax.numpy as jnp
from jax import lax
from jax.experimental import pallas as pl
from jax.experimental.pallas import tpu as pltpu
from jax.sharding import PartitionSpec as P

BLOCK = 64
TILE = 256
norm_eps = 1e-06
f32, bf16 = jnp.float32, jnp.bfloat16
MESH = pl.DeviceIdType.MESH
VMEM = pltpu.VMEM
ANY = pl.ANY
LIMIT = 60 * 2**20


def in_vmem():
    return pl.BlockSpec(memory_space=VMEM)


def in_place():
    return pl.BlockSpec(memory_space=ANY)


def greet(partners):
    barrier = pltpu.get_barrier_semaphore()
    for partner in partners:
        pl.semaphore_signal(barrier, inc=1, device_id=partner, device_id_type=MESH)
    pl.semaphore_wait(barrier, len(partners))


def remote(src, dst, sems, index, partner):
    return pltpu.make_async_remote_copy(
        src_ref=src,
        dst_ref=dst,
        send_sem=sems[0].at[index],
        recv_sem=sems[1].at[index],
        device_id=partner,
        device_id_type=MESH,
    )


def parts_of(a, count):
    if a.dtype == bf16:
        return [a]
    out = []
    for i in range(count):
        part = a.astype(bf16)
        out.append(part)
        if i + 1 < count:
            a = a - part.astype(f32)
    return out


def dot(a, b, ca=1, cb=0, count=1):
    total = None
    for right in reversed(parts_of(b, count)):
        term = lax.dot_general(
            a.astype(bf16), right, (((ca,), (cb,)), ((), ())), preferred_element_type=f32
        )
        total = term if total is None else total + term
    return total


def to_col(row):
    n = row.shape[1]
    i = lax.broadcasted_iota(jnp.int32, (n, n), 0)
    j = lax.broadcasted_iota(jnp.int32, (n, n), 1)
    return jnp.sum(jnp.where(i == j, jnp.broadcast_to(row, (n, n)), 0.0), axis=1, keepdims=True)


def mask_set(flags_col, flags_row):
    n = flags_col.shape[0]
    i = lax.broadcasted_iota(jnp.int32, (n, n), 0)
    j = lax.broadcasted_iota(jnp.int32, (n, n), 1)
    same = (i // BLOCK) == (j // BLOCK)
    lower = jnp.where(same & (i >= j), 1.0, 0.0)
    block = jnp.where(same, 1.0, 0.0)
    seen_col = dot(lower, flags_col)[:, :1]
    all_col = dot(block, flags_col)[:, :1]
    seen_row = dot(flags_row, lower, 1, 1)[:1, :]
    linked = jnp.where(seen_col == seen_row, lower, 0.0)
    fresh = jnp.where(seen_col == 0.0, 1.0, 0.0)
    ending = jnp.where(seen_col == all_col, 1.0, 0.0)
    unbroken = jnp.where(all_col == 0.0, 1.0, 0.0)
    return lower, linked, fresh, ending, unbroken


def gate_set(pre, bias, lower, ending):
    z = pre + bias
    u = jnp.exp(-jnp.abs(z))
    lp = jnp.where(
        u < 0.02, u * (1.0 - u * (0.5 - u * (1.0 / 3.0 - 0.25 * u))), jnp.log(1.0 + u)
    )
    g = (jnp.minimum(z, 0.0) - lp) * 0.125
    series = 1.0 + g * (1.0 / 7.0)
    for order in (6, 5, 4, 3, 2):
        series = 1.0 + g * (1.0 / order) * series
    oma = jnp.where(g > -0.35, -g * series, 1.0 - jnp.exp(g))
    a = dot(lower, g, count=3)
    n, lanes = a.shape
    last = jnp.concatenate(
        [
            jnp.broadcast_to(a[b * BLOCK + BLOCK - 1 : b * BLOCK + BLOCK], (BLOCK, lanes))
            for b in range(n // BLOCK)
        ],
        axis=0,
    )
    tail = jnp.exp(last - a) * ending
    return z, u, oma, jnp.exp(a), jnp.exp(-a), tail


def rows_of(b):
    return slice(b * BLOCK, (b + 1) * BLOCK)


def passing(growth, unbroken, b, hs):
    last = b * BLOCK + BLOCK - 1
    return to_col(growth[last : last + 1, hs] * unbroken[last : last + 1])


def sigmoid(v):
    return 1.0 / (1.0 + jnp.exp(-v))


WEIGHTS = ("key", "value", "forget", "query", "outgate", "output", "gate", "up", "down")
TWICE = ("gate", "up")


def front_kernel(size, heads, grouped, *refs):
    count = len(WEIGHTS)
    shards, refs = dict(zip(WEIGHTS, refs[:count])), refs[count:]
    (tok_ref, cot_ref, pre_gain, post_gain, head_gain, bias_ref, fcol_ref, frow_ref), refs = refs[:8], refs[8:]
    (
        out_ref, first_ref, attn_ref, mdelta_ref, postgain_grad,
        normed_t, merged_t, second_t, hidden_t, gate_delta, up_delta,
        q_ref, k_ref, v_ref, pre_ref, logit_ref,
        mixed_ref, aff_ref, mixing_ref, weight_ref, inner_ref, state_ref, pass_ref,
    ), refs = refs[:23], refs[23:]
    passed, refs = dict(zip(WEIGHTS[:5], refs[:5])), refs[5:]
    whole, refs = dict(zip(WEIGHTS, refs[:count])), refs[count:]
    (
        normed, merged, one_ref, second, block_acc, delta_acc, flat_t,
        ends, going, gathered, prefix, came,
        local, send_sem, recv_sem, away, st_send, st_recv,
    ) = refs
    sems = (send_sem, recv_sem)
    s, f = lax.axis_index("seq"), lax.axis_index("fsdp")
    q = lax.rem(s, 4)
    kind_bit = lax.rem(q + q // 2, 2)
    sib, far, nx, nz = (s, f ^ 1), (s, f ^ 2), (s ^ 1, f), (s ^ 2, f)
    fy, fs = f ^ 2, f ^ 3
    others = [(lax.rem(s + d, size), f) for d in range(1, size)]
    greet([sib, far] + others)
    started = []

    def go(copy):
        copy.start()
        started.append(copy)

    def piece(m, owner, start, length):
        rows = shards[m].shape[0]
        return whole[m].at[pl.ds(pl.multiple_of(owner * rows + start, 16), length)]

    def quarter(m, owner, which, half=None):
        rows = shards[m].shape[0] // 4
        first = (rows // 2 + 15) // 16 * 16
        start, length = (0, rows) if half is None else ((0, first), (first, rows - first))[half]
        return piece(m, owner, which * rows + start, length)

    def eighth(m, owner, bit, half):
        rows = shards[m].shape[0] // 2
        return piece(m, owner, bit * rows + half * (rows // 2), rows // 2)

    def mine(m, owner):
        if m in TWICE:
            rows = shards[m].shape[0] // 2
            return piece(m, owner, kind_bit * rows, rows)
        return quarter(m, owner, q)

    def from_x(m, owner):
        return eighth(m, owner, 1 - kind_bit, 0) if m in TWICE else quarter(m, owner, q ^ 1)

    def from_z(m, owner):
        return eighth(m, owner, 1 - kind_bit, 1) if m in TWICE else quarter(m, owner, q ^ 2)

    def send(kind, m, part, partner):
        go(remote(part, part, sems, (kind, WEIGHTS.index(m)), partner))

    def arrived(kind, m, part):
        remote(part, part, sems, (kind, WEIGHTS.index(m)), sib).wait_recv()

    own = {}
    for i, m in enumerate(WEIGHTS):
        rows = shards[m].shape[0]
        if m in TWICE:
            src = shards[m].at[pl.ds(pl.multiple_of(kind_bit * (rows // 2), 16), rows // 2)]
        else:
            src = shards[m].at[pl.ds(pl.multiple_of(q * (rows // 4), 16), rows // 4)]
        go(remote(src, mine(m, f), sems, (1, i), far))
    for i, m in enumerate(WEIGHTS):
        rows = shards[m].shape[0]
        go(remote(shards[m], piece(m, f, 0, rows), sems, (0, i), sib))
        own[m] = pltpu.make_async_copy(shards[m], piece(m, f, 0, rows), local.at[i])
        own[m].start()

    def pump(step):
        if step < count:
            m = WEIGHTS[step]
            part = mine(m, fy)
            arrived(1, m, part)
            if m in TWICE:
                send(2, m, eighth(m, fy, kind_bit, 0), nx)
                send(3, m, eighth(m, fy, kind_bit, 1), nz)
            else:
                send(2, m, part, nx)
                send(3, m, part, nz)
            send(6, m, part, sib)
        if 0 <= step - 1 < count:
            m = WEIGHTS[step - 1]
            arrived(2, m, from_x(m, fy))
            if m not in TWICE:
                send(4, m, quarter(m, fy, q ^ 1, 0), nz)
            send(7, m, from_x(m, fy), sib)
            arrived(3, m, from_z(m, fy))
            if m not in TWICE:
                send(5, m, quarter(m, fy, q ^ 2, 1), nx)
            send(8, m, from_z(m, fy), sib)
        if 0 <= step - 2 < count:
            m = WEIGHTS[step - 2]
            if m not in TWICE:
                for kind in (4, 5):
                    part = quarter(m, fy, q ^ 3, kind - 4)
                    arrived(kind, m, part)
                    send(kind + 5, m, part, sib)

    def ready(m):
        own[m].wait()
        arrived(0, m, piece(m, f ^ 1, 0, shards[m].shape[0]))
        arrived(6, m, mine(m, fs))
        arrived(7, m, from_x(m, fs))
        arrived(8, m, from_z(m, fs))
        if m not in TWICE:
            arrived(9, m, quarter(m, fs, q ^ 3, 0))
            arrived(10, m, quarter(m, fs, q ^ 3, 1))

    n, width = tok_ref.shape
    head = width // heads
    slots = bias_ref.shape[1] // heads
    blocks = n // BLOCK
    streams = 2
    per = blocks // streams
    pairs = heads * streams
    scale = head ** (-0.5)

    def across(columns, step):
        def turn(i, carry):
            step(pl.ds(pl.multiple_of(i * TILE, TILE), TILE))
            return carry

        lax.fori_loop(0, columns // TILE, turn, 0)

    def project(m, to_ref):
        def step(at):
            to_ref[:, at] = dot(normed[...], whole[m][:, at]).astype(to_ref.dtype)

        across(whole[m].shape[1], step)

    def turn_over(source, to_ref, rows, padded):
        if not grouped:
            to_ref[...] = source[...].astype(bf16)
            return
        for group in range(16):
            for core in range(2):
                at = (group * 2 + core) * rows
                to_ref[core, group * padded : group * padded + rows] = source[at : at + rows].astype(bf16)

    inputs = tok_ref[...].astype(f32)
    unit = inputs * lax.rsqrt(jnp.mean(inputs * inputs, axis=1, keepdims=True) + norm_eps)
    scaled = unit * pre_gain[...]
    normed[...] = scaled.astype(bf16)
    turn_over(scaled.T, normed_t, width // 32, width // 32)
    for step in range(5):
        pump(step)
    for m, to_ref in (("key", k_ref), ("value", v_ref), ("forget", pre_ref)):
        ready(m)
        project(m, to_ref)
    lower, linked, fresh, ending, unbroken = mask_set(fcol_ref[...], frow_ref[...])
    z, u, oma, growth, inverse, tail = gate_set(pre_ref[...], bias_ref[...], lower, ending)
    shrink, kept = inverse * oma, tail * oma
    for h in range(heads):
        hs, hd = slice(h * slots, (h + 1) * slots), slice(h * head, (h + 1) * head)
        for stream in range(streams):
            pair = h * streams + stream
            total, through = None, None
            for b in range(stream * per, (stream + 1) * per):
                part = kept[rows_of(b), hs].astype(bf16)
                at = pair * per + b % per
                end_k = dot(part, k_ref[rows_of(b), hd], 0, 0)
                end_v = dot(part, v_ref[rows_of(b), hd], 0, 0)
                ends[at, :, :head] = end_k
                ends[at, :, head:] = end_v
                factor = passing(growth, unbroken, b, hs)
                pass_ref[at] = jnp.broadcast_to(factor, pass_ref.shape[1:])
                if total is None:
                    total, through = (end_k, end_v), factor
                else:
                    total = (factor * total[0] + end_k, factor * total[1] + end_v)
                    through = through * factor
            at = slice(pair * slots, (pair + 1) * slots)
            going[at, :head] = total[0].astype(bf16)
            going[at, head : 2 * head] = total[1].astype(bf16)
            going[at, 2 * head :] = jnp.broadcast_to(through, (slots, going.shape[1] - 2 * head)).astype(bf16)

    share = pairs * slots // size

    def rows_for(place):
        return pl.ds(pl.multiple_of(place * share, 16), share)

    first_hop, second_hop = [], []
    for d in range(1, size):
        to = others[d - 1]
        copy = remote(going.at[rows_for(to[0])], gathered.at[s], (st_send, st_recv), (0, d - 1), to)
        go(copy)
        first_hop.append(lax.rem(s + size - d, size))
    gathered[s] = going[rows_for(s)]
    pump(5)
    pump(6)
    for m, to_ref in (("query", q_ref), ("outgate", logit_ref)):
        ready(m)
        project(m, to_ref)
    for i, m in enumerate(WEIGHTS[:5]):
        copy = pltpu.make_async_copy(whole[m], passed[m], away.at[i])
        copy.start()
        own[m] = copy
    for d in range(1, size):
        source = first_hop[d - 1]
        remote(gathered.at[source], gathered.at[source], (st_send, st_recv), (0, d - 1), sib).wait_recv()
    state = jnp.zeros((share, 2 * head), f32)
    for place in range(size):
        prefix[place] = state.astype(bf16)
        entry = gathered[place].astype(f32)
        state = entry[:, 2 * head : 2 * head + 1] * state + entry[:, : 2 * head]
    for d in range(1, size):
        to = others[d - 1]
        go(remote(prefix.at[to[0]], came.at[rows_for(s)], (st_send, st_recv), (1, d - 1), to))
    came[rows_for(s)] = prefix[s]
    pump(7)
    for h in range(heads):
        hd = slice(h * head, (h + 1) * head)
        aff_ref[h] = (dot(q_ref[:, hd], k_ref[:, hd], 1, 1) * (linked * scale)).astype(bf16)
    for d in range(1, size):
        part = came.at[rows_for(first_hop[d - 1])]
        remote(part, part, (st_send, st_recv), (1, d - 1), sib).wait_recv()
    pump(8)
    for h in range(heads):
        hs, hd = slice(h * slots, (h + 1) * slots), slice(h * head, (h + 1) * head)
        for stream in range(streams):
            pair = h * streams + stream
            state = came[pair * slots : (pair + 1) * slots].astype(f32)
            for b in range(per):
                at = pair * per + b
                state_ref[pair, b] = state.astype(bf16)
                state = pass_ref[at][:, :1] * state + ends[at]
            state_ref[pair, per] = state.astype(bf16)
        gr, sh = growth[:, hs], shrink[:, hs]
        qh, vh = q_ref[:, hd], v_ref[:, hd]
        carried = jnp.concatenate(
            [
                dot(qh[rows_of(b)], state_ref[h * streams + b // per, b % per, :, :head], 1, 1)
                for b in range(blocks)
            ],
            axis=0,
        )
        inner = dot(aff_ref[h], sh) + carried * (scale * fresh)
        scores = gr * inner
        e = jnp.exp(scores - jnp.max(scores, axis=1, keepdims=True))
        weights = e / jnp.sum(e, axis=1, keepdims=True)
        weight_ref[:, hs] = weights
        inner_ref[:, hs] = inner
        lifted = weights * gr
        mixing = (dot(lifted, sh.astype(bf16), 1, 1) * linked).astype(bf16)
        mixing_ref[h] = mixing
        brought = jnp.concatenate(
            [
                dot(lifted[rows_of(b)], state_ref[h * streams + b // per, b % per, :, head:])
                for b in range(blocks)
            ],
            axis=0,
        )
        mixed = dot(mixing, vh) + brought * fresh
        mixed_ref[:, hd] = mixed
        r = lax.rsqrt(jnp.mean(mixed * mixed, axis=1, keepdims=True) + norm_eps)
        logits = logit_ref[:, hd]
        delta_acc[:, hd] = mixed * r * head_gain[...] * (logits * sigmoid(logits))
        merged[:, hd] = delta_acc[:, hd].astype(bf16)
    ready("output")

    def join(at):
        one_ref[:, at] = tok_ref[:, at].astype(f32) + dot(merged[...], whole["output"][:, at])

    across(width, join)
    turn_over(delta_acc[...].T, merged_t, width // 32, width // 32)
    one = one_ref[...]
    scaled = one * lax.rsqrt(jnp.mean(one * one, axis=1, keepdims=True) + norm_eps) * post_gain[...]
    second[...] = scaled.astype(bf16)
    turn_over(scaled.T, second_t, width // 32, width // 32)
    pump(9)
    pump(10)
    ready("gate")
    ready("up")
    ready("down")
    block_acc[...] = one
    delta_acc[...] = jnp.zeros_like(delta_acc)

    def unit_tile(i, carry):
        at = pl.ds(pl.multiple_of(i * TILE, TILE), TILE)
        w_gate, w_up, w_down = whole["gate"][:, at], whole["up"][:, at], whole["down"][at]
        gate_vals, up_vals = dot(second[...], w_gate), dot(second[...], w_up)
        sig = sigmoid(gate_vals)
        silu = gate_vals * sig
        full = silu * up_vals
        flat_t[at] = full.T
        hidden_delta = dot(cot_ref[...], w_down, 1, 1)
        d_up = (hidden_delta * silu).astype(bf16)
        d_gate = (hidden_delta * up_vals * (sig + silu * (1.0 - sig))).astype(bf16)
        gate_delta[:, at] = d_gate
        up_delta[:, at] = d_up
        block_acc[...] += dot(full, w_down)
        delta_acc[...] += dot(d_gate, w_gate, 1, 1) + dot(d_up, w_up, 1, 1)
        return carry

    ff = whole["down"].shape[0]
    lax.fori_loop(0, ff // TILE, unit_tile, 0)
    out_ref[...] = block_acc[...].astype(bf16)
    turn_over(flat_t, hidden_t, ff // 32, -(-(ff // 32) // 16) * 16)
    one = one_ref[...]
    r = lax.rsqrt(jnp.mean(one * one, axis=1, keepdims=True) + norm_eps)
    unit = one * r
    delta = delta_acc[...]
    postgain_grad[...] = jnp.sum(delta * unit, axis=0, keepdims=True)
    delta = delta * post_gain[...]
    first = cot_ref[...].astype(f32) + r * (delta - unit * jnp.mean(unit * delta, axis=1, keepdims=True))
    first_ref[...] = first
    attn_ref[...] = first.astype(bf16)

    def split(at):
        mdelta_ref[:, at] = dot(attn_ref[...], whole["output"][at], 1, 1)

    across(width, split)
    for m in WEIGHTS[:5]:
        own[m].wait()
    for copy in started:
        copy.wait_send()


def front(size, heads, grouped, shards, tokens, cotan, pre_gain, post_gain, head_gain, bias, fcol, frow):
    n, width = tokens.shape
    head, slots = width // heads, bias.shape[1] // heads
    pairs, per = heads * 2, n // BLOCK // 2
    ff = shards["gate"].shape[1]
    shards = [shards[m] for m in WEIGHTS]
    count = len(shards)
    padded = -(-(ff // 32) // 16) * 512

    def turned(rows, grouped_rows):
        shape = (2, grouped_rows // 2, n) if grouped else (rows, n)
        return jax.ShapeDtypeStruct(shape, bf16)

    def low(*shape):
        return jax.ShapeDtypeStruct(shape, bf16)

    def full(*shape):
        return jax.ShapeDtypeStruct(shape, f32)

    outs = [
        low(n, width), full(n, width), low(n, width), full(n, width), full(1, width),
        turned(width, width), turned(width, width), turned(width, width), turned(ff, padded),
        low(n, ff), low(n, ff),
        low(n, width), low(n, width), low(n, width), full(n, heads * slots), full(n, width),
        full(n, width), low(heads, n, n), low(heads, n, n), full(n, heads * slots), full(n, heads * slots),
        low(pairs, per + 1, slots, 2 * head), full(pairs * per, slots, 128),
    ]
    wholes = [low(4 * w.shape[0], w.shape[1]) for w in shards]
    share = pairs * slots // size
    dma = pltpu.SemaphoreType.DMA
    got = pl.pallas_call(
        functools.partial(front_kernel, size, heads, grouped),
        name="front",
        out_shape=outs + wholes[:5],
        in_specs=[in_place()] * count + [in_vmem()] * 8,
        out_specs=[in_vmem()] * len(outs) + [in_place()] * 5,
        scratch_shapes=[VMEM(w.shape, bf16) for w in wholes]
        + [
            VMEM((n, width), bf16),
            VMEM((n, width), bf16),
            VMEM((n, width), f32),
            VMEM((n, width), bf16),
            VMEM((n, width), f32),
            VMEM((n, width), f32),
            VMEM((ff, n), f32),
            VMEM((pairs * per, slots, 2 * head), f32),
            VMEM((pairs * slots, 2 * head + 128), bf16),
            VMEM((size, share, 2 * head + 128), bf16),
            VMEM((size, share, 2 * head), bf16),
            VMEM((pairs * slots, 2 * head), bf16),
            dma((count,)),
            dma((11, count)),
            dma((11, count)),
            dma((5,)),
            dma((2, size - 1)),
            dma((2, size - 1)),
        ],
        compiler_params=pltpu.CompilerParams(
            collective_id=1, has_side_effects=True, vmem_limit_bytes=LIMIT
        ),
    )(*shards, tokens, cotan, pre_gain, post_gain, head_gain, bias, fcol, frow)
    return got


def return_kernel(
    size, heads, q_ref, k_ref, v_ref, pre_ref, bias_ref, fcol_ref, frow_ref, logit_ref, gain_ref,
    mixed_ref, aff_ref, mixing_ref, weight_ref, inner_ref, state_ref, pass_ref, delta_ref,
    q_low, k_low, v_low, forget_low, logit_low, bias_grad, gain_grad,
    owed, came, going, k_acc, v_acc, dmix, da_acc, doma_acc, send_sem, recv_sem,
):
    s, f = lax.axis_index("seq"), lax.axis_index("fsdp")
    right, left = (lax.rem(s + 1, size), f), (lax.rem(s + size - 1, size), f)
    greet((left, right))
    n, width = q_ref.shape
    head = width // heads
    slots = pre_ref.shape[1] // heads
    blocks = n // BLOCK
    streams = 2
    per = blocks // streams
    scale = head ** (-0.5)
    lower, linked, fresh, ending, unbroken = mask_set(fcol_ref[...], frow_ref[...])
    z, u, oma, growth, inverse, tail = gate_set(pre_ref[...], bias_ref[...], lower, ending)
    shrink, kept = inverse * oma, tail * oma

    @pl.when(s == size - 1)
    def _():
        came[...] = jnp.zeros_like(came)

    gain_total = jnp.zeros((1, head), f32)
    for h in range(heads):
        hs, hd = slice(h * slots, (h + 1) * slots), slice(h * head, (h + 1) * head)
        mixed, logits, delta = mixed_ref[:, hd], logit_ref[:, hd], delta_ref[:, hd]
        r = lax.rsqrt(jnp.mean(mixed * mixed, axis=1, keepdims=True) + norm_eps)
        sig = 1.0 / (1.0 + jnp.exp(-logits))
        silu = logits * sig
        unit = mixed * r
        dy = delta * silu
        logit_low[:, hd] = (delta * unit * gain_ref[...] * (sig + silu * (1.0 - sig))).astype(bf16)
        gain_total = gain_total + jnp.sum(dy * unit, axis=0, keepdims=True)
        dy = dy * gain_ref[...]
        dmixed = r * (dy - unit * jnp.mean(unit * dy, axis=1, keepdims=True))
        gr, sh = growth[:, hs], shrink[:, hs].astype(bf16)
        weights, inner = weight_ref[:, hs], inner_ref[:, hs]
        aff, mixing = aff_ref[h], mixing_ref[h]
        qh, kh, vh = q_ref[:, hd], k_ref[:, hd], v_ref[:, hd]
        do = dmixed.astype(bf16)
        lifted = (weights * gr).astype(bf16)
        dm = (dot(do, vh, 1, 1) * linked).astype(bf16)
        v_acc[:, hd] = dot(mixing, do, 0, 0)
        fdo = (dmixed * fresh).astype(bf16)

        def states(b, h=h):
            return state_ref.at[h * streams + b // per, b % per]

        dlift = dot(dm, sh) + jnp.concatenate(
            [dot(fdo[rows_of(b)], states(b)[:, head:], 1, 1) for b in range(blocks)], axis=0
        )
        dsh = dot(dm, lifted, 0, 0)
        dw = dlift * gr
        dsc = weights * (dw - jnp.sum(weights * dw, axis=1, keepdims=True))
        du = dsc * gr
        du_low = du.astype(bf16)
        da = (dot(du_low, sh, 1, 1) * (linked * scale)).astype(bf16)
        dsh = dsh + dot(aff, du_low, 0, 0)
        fdu = (du * (fresh * scale)).astype(bf16)
        q_low[:, hd] = (
            dot(da, kh)
            + jnp.concatenate(
                [dot(fdu[rows_of(b)], states(b)[:, :head]) for b in range(blocks)], axis=0
            )
        ).astype(bf16)
        k_acc[:, hd] = dot(da, qh, 0, 0)
        for b in range(blocks):
            at = (h * streams + b // per) * per + b % per
            owed[at, :, :head] = dot(fdu[rows_of(b)], qh[rows_of(b)], 0, 0)
            owed[at, :, head:] = dot(lifted[rows_of(b)], fdo[rows_of(b)], 0, 0)
        da_acc[:, hs] = lifted.astype(f32) * dlift + du_low.astype(f32) * inner - dsh * sh.astype(f32)
        doma_acc[:, hs] = dsh * inverse[:, hs]
    gain_grad[...] = gain_total
    sends = []
    for pair in range(heads * streams):
        copy = remote(going.at[pair], came.at[pair], (send_sem, recv_sem), pair, left)

        @pl.when(s < size - 1)
        def _(copy=copy):
            copy.wait_recv()

        state = came[pair].astype(f32)
        for b in reversed(range(per)):
            at = pair * per + b
            before = owed[at] + pass_ref[at][:, :1] * state
            owed[at] = state
            state = before
        going[pair] = state.astype(bf16)

        @pl.when(s > 0)
        def _(copy=copy):
            copy.start()

        sends.append(copy)
    row = lax.broadcasted_iota(jnp.int32, (BLOCK, 1), 0)
    for h in range(heads):
        hs, hd = slice(h * slots, (h + 1) * slots), slice(h * head, (h + 1) * head)
        for b in range(blocks):
            rb = rows_of(b)
            pair = h * streams + b // per
            at = pair * per + b % per
            leaving = owed[at]
            low = leaving.astype(bf16)
            part = kept[rb, hs].astype(bf16)
            dkept = dot(k_ref[rb, hd], low[:, :head], 1, 1) + dot(v_ref[rb, hd], low[:, head:], 1, 1)
            k_low[rb, hd] = (k_acc[rb, hd] + dot(part, low[:, :head])).astype(bf16)
            v_low[rb, hd] = (v_acc[rb, hd] + dot(part, low[:, head:])).astype(bf16)
            held = jnp.sum(low.astype(f32) * state_ref[pair, b % per + 1].astype(f32), axis=1, keepdims=True)
            held_row = to_row(held)
            da_acc[rb, hs] = (
                da_acc[rb, hs] - dkept * part.astype(f32) + jnp.where(row == BLOCK - 1, held_row, 0.0)
            )
            doma_acc[rb, hs] = doma_acc[rb, hs] + dkept * tail[rb, hs]
    dg = dot(lower, da_acc[...], 0, 0, count=3) - doma_acc[...] * (1.0 - oma)
    sig = jnp.where(z >= 0.0, u / (1.0 + u), 1.0 / (1.0 + u))
    dpre = dg * sig * 0.125
    forget_low[...] = dpre.astype(bf16)
    bias_grad[...] = jnp.sum(dpre, axis=0, keepdims=True)
    for copy in sends:

        @pl.when(s > 0)
        def _(copy=copy):
            copy.wait_send()


def to_row(col):
    n = col.shape[0]
    i = lax.broadcasted_iota(jnp.int32, (n, n), 0)
    j = lax.broadcasted_iota(jnp.int32, (n, n), 1)
    return jnp.sum(jnp.where(i == j, jnp.broadcast_to(col, (n, n)), 0.0), axis=0, keepdims=True)


def go_back(size, heads, q, k, v, pre, bias, fcol, frow, logits, gain, kept, delta):
    n, width = q.shape
    head, slots = width // heads, pre.shape[1] // heads
    pairs, per = heads * 2, n // BLOCK // 2
    return pl.pallas_call(
        functools.partial(return_kernel, size, heads),
        name="go_back",
        out_shape=[
            jax.ShapeDtypeStruct((n, width), bf16),
            jax.ShapeDtypeStruct((n, width), bf16),
            jax.ShapeDtypeStruct((n, width), bf16),
            jax.ShapeDtypeStruct(pre.shape, bf16),
            jax.ShapeDtypeStruct((n, width), bf16),
            jax.ShapeDtypeStruct((1, pre.shape[1]), f32),
            jax.ShapeDtypeStruct((1, head), f32),
        ],
        in_specs=[in_vmem()] * 17,
        out_specs=[in_vmem()] * 7,
        scratch_shapes=[
            VMEM((pairs * per, slots, 2 * head), f32),
            VMEM((pairs, slots, 2 * head), bf16),
            VMEM((pairs, slots, 2 * head), bf16),
            VMEM((n, width), f32),
            VMEM((n, width), f32),
            VMEM((8, 128), f32),
            VMEM(pre.shape, f32),
            VMEM(pre.shape, f32),
            pltpu.SemaphoreType.DMA((pairs,)),
            pltpu.SemaphoreType.DMA((pairs,)),
        ],
        compiler_params=pltpu.CompilerParams(
            collective_id=3, has_side_effects=True, vmem_limit_bytes=LIMIT
        ),
    )(q, k, v, pre, bias, fcol, frow, logits, gain, *kept, delta)


def cut(columns, flip):
    tiles = columns // TILE
    if tiles <= 1:
        half = columns // 2
        return [(0, half, flip), (half, half, 1 - flip)]
    pieces = 4 if tiles <= 4 else 6
    out, start = [], 0
    for i in range(pieces):
        count = tiles // pieces + (1 if i < tiles % pieces else 0)
        out.append((start, count * TILE, (i + flip) % 2))
        start += count * TILE
    return out


def sum_kernel(plan, n_left, n_right, *refs):
    lefts, refs = refs[:n_left], refs[n_left:]
    rights, refs = refs[:n_right], refs[n_right:]
    vec_in, refs = refs[0], refs[1:]
    outs, refs = refs[: len(plan)], refs[len(plan) :]
    vec_out, refs = refs[0], refs[1:]
    left_all, refs = refs[:n_left], refs[n_left:]
    right_all, refs = refs[:n_right], refs[n_right:]
    chunks = [(g,) + c for g, p in enumerate(plan) for c in p[5]]
    nc = len(chunks)
    sums, refs = refs[:nc], refs[nc:]
    landed = []
    for _ in range(4):
        landed.append(refs[:nc])
        refs = refs[nc:]
    vec_acc, vec_got, local, in_send, in_recv, st_send, st_recv, v_send, v_recv = refs
    s, f = lax.axis_index("seq"), lax.axis_index("fsdp")
    core, y = lax.rem(f, 2), f // 2
    x, z_low, z_high = lax.rem(s, 2), lax.rem(s // 2, 2), lax.rem(s // 4, 2)
    sib, far, nx, nz, nzz = (s, f ^ 1), (s, f ^ 2), (s ^ 1, f), (s ^ 2, f), (s ^ 4, f)
    greet([sib, far, nx, nz, nzz])
    started = []

    def go(copy):
        copy.start()
        started.append(copy)

    tokens = rights[0].shape[0]
    waiting = {}

    def exchange(kind, i):
        index = i if kind == 0 else n_left + i
        if (kind, i) in waiting:
            return
        if kind == 0:
            src_own, src_far = lefts[i].at[core], lefts[i].at[1 - core]
            dst_own, dst_far = left_all[i].at[:, pl.ds(0, tokens)], left_all[i].at[:, pl.ds(tokens, tokens)]
        else:
            src_own = src_far = rights[i]
            dst_own, dst_far = right_all[i].at[pl.ds(0, tokens)], right_all[i].at[pl.ds(tokens, tokens)]
        keep = pltpu.make_async_copy(src_own, dst_own, local.at[index])
        keep.start()
        copy = remote(src_far, dst_far, (in_send, in_recv), index, sib)
        go(copy)
        waiting[kind, i] = [keep, copy]

    def have(kind, i):
        pair = waiting[kind, i]
        if pair:
            pair[0].wait()
            pair[1].wait_recv()
            waiting[kind, i] = None

    for left, right, *_ in plan[:2]:
        exchange(0, left)
        exchange(1, right)

    def route(c):
        if chunks[c][3]:
            return (x, z_low, y, z_high), (nx, nz, far, nzz)
        return (y, z_low, x, z_high), (far, nz, nx, nzz)

    def stage_copy(c, stage):
        bits, partners = route(c)
        at = bits[:stage] + (1 - bits[stage],)
        return remote(sums[c].at[at], landed[stage][c], (st_send, st_recv), (stage, c), partners[stage])

    def produce(c):
        g, start, width, order = chunks[c]
        left, right, columns, rows, kept, _ = plan[g]
        have(0, left)
        have(1, right)
        for after in plan[g + 1 : g + 3]:
            exchange(0, after[0])
            exchange(1, after[1])
        tile = min(TILE, width)

        def body(i, carry):
            at = pl.multiple_of(start + i * tile, 128)
            to = pl.multiple_of(i * tile, 128)
            got = jnp.dot(
                left_all[left][...], right_all[right][:, pl.ds(at, tile)], preferred_element_type=f32
            ).astype(bf16)
            for group in range(16):
                zh, zl, xx, yy = (group >> 3) & 1, (group >> 2) & 1, (group >> 1) & 1, group & 1
                place = (xx, zl, yy, zh) if order else (yy, zl, xx, zh)
                sums[c][*place, :, pl.ds(to, tile)] = got[group * rows : (group + 1) * rows]
            return carry

        lax.fori_loop(0, width // tile, body, 0)
        go(stage_copy(c, 0))

    def advance(c, stage):
        stage_copy(c, stage).wait_recv()
        bits, _ = route(c)
        if stage == 3:
            g, start, width, _ = chunks[c]
            kept = plan[g][4]
            total = sums[c][bits].astype(f32) + landed[3][c][...].astype(f32)
            outs[g][:, start : start + width] = total[:kept]
            return
        for rest in range(1 << (3 - stage)):
            tail = tuple((rest >> k) & 1 for k in reversed(range(3 - stage)))
            at = bits[: stage + 1] + tail
            sums[c][at] = (sums[c][at].astype(f32) + landed[stage][c][tail].astype(f32)).astype(bf16)
        go(stage_copy(c, stage + 1))

    def v_copy(i):
        return remote(vec_acc.at[i], vec_got.at[i], (v_send, v_recv), i, (sib, far, nx, nz, nzz)[i])

    def vector(step):
        if step == 0:
            vec_acc[0] = vec_in[...]
        else:
            v_copy(step - 1).wait_recv()
            total = vec_acc[step - 1] + vec_got[step - 1]
            if step == 5:
                vec_out[...] = total
                return
            vec_acc[step] = total
        go(v_copy(step))

    lag = 3
    steps = nc + 4 * lag
    for t in range(steps):
        if t < nc:
            produce(t)
        for stage in range(4):
            c = t - (stage + 1) * lag
            if 0 <= c < nc:
                advance(c, stage)
        if steps - 7 <= t < steps - 1:
            vector(t - (steps - 7))
    for copy in started:
        copy.wait_send()


def sum_grads(plan, lefts, rights, vectors):
    tokens = rights[0].shape[0]
    chunks = [(p[3],) + c for p in plan for c in p[5]]
    nc = len(chunks)
    dma = pltpu.SemaphoreType.DMA
    n_in = len(lefts) + len(rights)
    scratch = [VMEM((a.shape[1], 2 * tokens), bf16) for a in lefts]
    scratch += [VMEM((2 * tokens, b.shape[1]), bf16) for b in rights]
    for lead in ((2, 2, 2, 2), (2, 2, 2), (2, 2), (2,), ()):
        scratch += [VMEM(lead + (r, w), bf16) for r, _, w, _ in chunks]
    scratch += [VMEM((5,) + vectors.shape, f32)] * 2
    scratch += [dma((n_in,))] * 3 + [dma((4, nc))] * 2 + [dma((5,))] * 2
    out = pl.pallas_call(
        functools.partial(sum_kernel, plan, len(lefts), len(rights)),
        name="sum_grads",
        out_shape=[jax.ShapeDtypeStruct((p[4], p[2]), f32) for p in plan]
        + [jax.ShapeDtypeStruct(vectors.shape, f32)],
        in_specs=[in_place()] * n_in + [in_vmem()],
        out_specs=[in_vmem()] * (len(plan) + 1),
        scratch_shapes=scratch,
        compiler_params=pltpu.CompilerParams(
            collective_id=4, has_side_effects=True, vmem_limit_bytes=LIMIT
        ),
    )(*lefts, *rights, vectors)
    return out[:-1], out[-1]


def rms_norm(values, gain):
    return values * lax.rsqrt(jnp.mean(values * values, axis=-1, keepdims=True) + norm_eps) * gain


def back_dot(left, right):
    return lax.dot_general(left, right, (((1,), (1,)), ((), ())), preferred_element_type=f32)


def by_owner(a, hi, lo):
    features, tokens = a.shape
    r = features // (hi * lo * 4)
    t = a.reshape(hi, lo, 2, 2, r, tokens).transpose(3, 1, 2, 0, 4, 5).reshape(2, lo * 2, hi * r, tokens)
    pad = -(hi * r) % 16
    if pad:
        t = jnp.pad(t, ((0, 0), (0, 0), (0, pad), (0, 0)))
    return t.reshape(2, -1, tokens)


def body(
    size, tokens, resets, pre_gain, query_weight, key_weight, value_weight, forget_weight, forget_bias,
    outgate_weight, output_weight, head_gain, post_gain, gate_weight, up_weight, down_weight, cotangent,
):
    lo = 8
    hi = size // lo
    streams, length, width = tokens.shape
    n = streams * length
    head = head_gain.shape[0]
    heads = width // head
    shards = {
        "query": query_weight, "key": key_weight, "value": value_weight, "forget": forget_weight,
        "outgate": outgate_weight, "output": output_weight, "gate": gate_weight, "up": up_weight, "down": down_weight,
    }
    cotan = cotangent.reshape(n, width)
    flags = resets.reshape(n).astype(f32)
    fcol = jnp.broadcast_to(flags[:, None], (n, 128))
    frow = jnp.broadcast_to(flags[None], (8, n))
    bias, gain = forget_bias[None], head_gain[None]
    (
        block_output, first_delta, attn_delta, merged_delta, postgain_grad,
        normed_t, merged_t, second_t, hidden_t, gate_delta, up_delta,
        q, k, v, pre, logits, *kept, wk, wv, wf, wq, wg,
    ) = front(
        size, heads, hi == 1, shards, tokens.reshape(n, width), cotan, pre_gain[None], post_gain[None],
        gain, bias, fcol, frow,
    )
    q_low, k_low, v_low, forget_low, logit_low, bias_grad, headgain_grad = go_back(
        size, heads, q, k, v, pre, bias, fcol, frow, logits, gain, kept, merged_delta
    )
    normed_delta = (
        back_dot(q_low, wq)
        + back_dot(k_low, wk)
        + back_dot(v_low, wv)
        + back_dot(forget_low, wf)
        + back_dot(logit_low, wg)
    )
    inputs = tokens.reshape(n, width).astype(f32)
    normed_full, norm_back = jax.vjp(rms_norm, inputs, pre_gain)
    input_delta, pregain_grad = norm_back(normed_delta)
    input_grad = (first_delta + input_delta).astype(bf16)

    lefts = [hidden_t, second_t, merged_t, normed_t]
    if hi > 1:
        lefts = [by_owner(a, hi, lo) for a in lefts]
    rights = [cotan, gate_delta, up_delta, attn_delta, logit_low, q_low, k_low, v_low, forget_low]
    which = (0, 1, 1, 2, 3, 3, 3, 3, 3)
    features = (gate_delta.shape[1],) + (width,) * 8
    plan = []
    for i, (left, right) in enumerate(zip(which, rights)):
        kept_rows = features[i] // (lo * 4)
        columns = right.shape[1]
        plan.append((left, i, columns, -(-kept_rows // 16) * 16, kept_rows, tuple(cut(columns, i % 2))))
    sizes = (width, bias.shape[1], head, width)
    vectors = jnp.concatenate([pregain_grad, bias_grad[0], headgain_grad[0], postgain_grad[0]])
    total = vectors.shape[0]
    vectors = jnp.pad(vectors, (0, -total % 1024)).reshape(8, -1)
    grads, vectors = sum_grads(tuple(plan), lefts, rights, vectors)
    if hi > 1:
        alike = [[a * lo + b for a in range(hi)] for b in range(lo)]
        grads = [
            lax.psum_scatter(g, "seq", scatter_dimension=0, axis_index_groups=alike, tiled=True)
            for g in grads
        ]
        vectors = lax.psum(vectors, "seq", axis_index_groups=alike)
    down_grad, gate_grad, up_grad, output_grad, outgate_grad, query_grad, key_grad, value_grad, forget_grad = grads
    vectors = vectors.reshape(-1)
    ends = [sum(sizes[: i + 1]) for i in range(4)]
    pregain, bias_total, headgain, postgain = [vectors[e - w : e] for e, w in zip(ends, sizes)]
    shape = tokens.shape
    return (
        block_output.reshape(shape), input_grad.reshape(shape), pregain, query_grad, key_grad, value_grad,
        forget_grad, bias_total, outgate_grad, output_grad, headgain, postgain, gate_grad, up_grad, down_grad,
    )


def solution(mesh):
    rows, whole, both = P("fsdp", None), P(), P(("seq", "fsdp"), None)
    return jax.shard_map(
        functools.partial(body, mesh.shape["seq"]),
        mesh=mesh,
        in_specs=(
            P("fsdp", "seq", None), P("fsdp", "seq"), whole, rows, rows, rows, rows, whole, rows, rows,
            whole, whole, rows, rows, rows, P("fsdp", "seq", None),
        ),
        out_specs=(
            P("fsdp", "seq", None), P("fsdp", "seq", None), whole, both, both, both, both, whole, both,
            both, whole, whole, both, both, both,
        ),
        check_vma=False,
    )
```

time: 530 us -> 310 us (0.58)
  Pallas kernels: 457 us -> 288 us
  matrix products: 39.7 us -> 4.99 us
  local copies, waits for them, and re-layouts: 23.3 us -> 12.9 us
    pallas_call x3 -> x2, Pallas kernels: 388 us -> 237 us  [the longest x1 128 us: sum_grads(): pl.pallas_call(functools.partial(sum_kernel, plan, len(lefts), len(rights...]
    dot_general x9 -> x0, matrix products: 23 us -> none  [fore_dot(): return jnp.dot(left, right, preferred_element_type=f32)]
    pallas_call x1, Pallas kernels: 69.3 us -> 50.9 us  [go_back(): pl.pallas_call(functools.partial(return_kernel, size, heads), name='go_ba...]
    dot_general x9 -> x5, matrix products: 16.8 us -> 4.99 us  [back_dot(): lax.dot_general(left, right, (((1,), (1,)), ((), ())), preferred_element_...]
    convert_element_type x4 -> x0, local copies, waits for them, and re-layouts: 5.37 us -> none  [the longest x2 3.49 us: body(): inputs = tokens.reshape(n, width).astype(f32)]
where the time goes in v3:
time: 310 us; the launch traced here: 309 us
  Pallas kernels  288 us (93%)
  local copies, waits for them, and re-layouts  12.9 us (4%)
  matrix products  4.99 us (2%)
    pallas_call x1, Pallas kernels, sum_grads(): pl.pallas_call(functools.partial(sum_kernel, plan, len(lefts), len(rights...  128 us
    pallas_call x1, Pallas kernels, front(): pl.pallas_call(functools.partial(front_kernel, size, heads, grouped), nam...  109 us
    pallas_call x1, Pallas kernels, go_back(): pl.pallas_call(functools.partial(return_kernel, size, heads), name='go_ba...  50.9 us
    unnamed x60, local copies, waits for them, and re-layouts  8.99 us

profile of v3, /device:TPU:0, one launch (start us, length us, event | category | flops | bytes accessed | tf_op | source)
XLA Modules:
  0.0 308.7 jit_solution(9319337321553247829)
XLA Ops:
  0.6 0.7 convert_bitcast_fusion
  1.3 0.8 broadcast_in_dim.33.refs_15_.fcol_ref
  2.1 0.6 broadcast_in_dim.34.refs_16_.frow_ref
  2.7 109.0 %front.1 = (bf16[256,1024]{1,0:T(8,128)(2,1)}, f32[256,1024]{1,0:T(8,128)}, bf16[256,1024]{1,0:T(8,128)(2,1)}, f32[256,1024]{1,0:T(8,128)}, f32[1,1024]{1,0:T(1,...) custom-call(bf16[256,1024]{1,0:T(8,128)(2,1)} %refs_0_.1, ...), custom_call_target="tpu_custom_call" | custom-call | tf_op jit(solution)/shard_map/front/pallas_call | solution.py:490
  111.7 50.9 %go_back.1 = (bf16[256,1024]{1,0:T(8,128)(2,1)}, bf16[256,1024]{1,0:T(8,128)(2,1)}, bf16[256,1024]{1,0:T(8,128)(2,1)}, bf16[256,256]{1,0:T(8,128)(2,1)}, bf16[25...) custom-call(bf16[256,1024]{1,0:T(8,128)(2,1)} %get-tuple-element.62.q_ref, ...), custom_call_target="tpu_custom_call" | custom-call | tf_op jit(solution)/shard_map/go_back/pallas_call | solution.py:662
  162.6 1.9 fusion.8
  164.6 0.8 convolution_add_fusion.2
  165.4 0.2 copy-done.2
  165.6 0.7 copy-done.6
  166.4 0.8 convolution_add_fusion.1
  167.2 0.2 copy-done.3
  167.4 0.7 copy-done.4
  168.1 0.8 fusion.9
  168.9 0.2 multiply_reduce_fusion
  169.1 0.1 copy-done.11
  169.2 0.7 fusion.3
  170.0 0.6 reshape.93.refs_13_
  170.6 128.0 %sum_grads.1 = (f32[88,1024]{1,0:T(8,128)}, f32[32,2816]{1,0:T(8,128)}, f32[32,2816]{1,0:T(8,128)}, f32[32,1024]{1,0:T(8,128)}, f32[32,1024]{1,0:T(8,128)}, /*in...) custom-call(bf16[2,1536,256]{2,1,0:T(8,128)(2,1)} %get-tuple-element.85.r, ...), custom_call_target="tpu_custom_call" | custom-call | tf_op jit(solution)/shard_map/sum_grads/pallas_call | solution.py:857
  298.6 0.8 reshape.94
  299.4 0.6 fusion.6
  300.0 0.6 fusion.7
  300.6 1.1 fusion.5
  301.7 0.8 copy.41
  302.5 0.7 copy.42
  303.2 0.7 copy.43
  303.9 0.7 copy.44
  304.5 0.6 copy.45
  305.1 0.7 copy.46
  305.8 0.7 copy.47
  306.4 0.7 copy.48
  307.2 0.7 copy.49
  307.9 0.7 copy.50
  (48 shorter events, 0.1 us)
Async XLA Ops:
  111.7 50.9 %copy-start.5 = (bf16[1024,1024]{1,0:T(8,128)(2,1)S(1)}, bf16[1024,1024]{1,0:T(8,128)(2,1)}, u32[]{:S(2)}) copy-start(bf16[1024,1024]{1,0:T(8,128)(2,1)} %get-tuple-element.76) | copy-start | bytes 6291460
  162.6 2.0 copy-start.1
  162.6 2.0 copy-start.7
  164.6 1.0 copy-start.2
  164.6 1.8 copy-start.6
  166.3 1.0 copy-start.3
  166.4 1.8 copy-start.4
  167.2 1.8 copy-start
  168.1 1.0 copy-start.9
  168.1 1.1 copy-start.11
  168.1 1.1 copy-start.20
  169.2 0.7 copy-start.22
  169.2 0.7 copy-start.23
  169.2 0.7 copy-start.24
  170.6 130.0 %copy-start.8 = (f32[256,1024]{1,0:T(8,128)S(1)}, f32[256,1024]{1,0:T(8,128)}, u32[]{:S(2)}) copy-start(f32[256,1024]{1,0:T(8,128)} %get-tuple-element.61) | copy-start | bytes 3145732
  298.6 3.2 %copy-start.10 = (bf16[256,1024]{1,0:T(8,128)(2,1)S(1)}, bf16[256,1024]{1,0:T(8,128)(2,1)}, u32[]{:S(2)}) copy-start(bf16[256,1024]{1,0:T(8,128)(2,1)} %get-tuple-element.60) | copy-start | bytes 1572868
  300.6 2.0 copy-start.19
  300.6 2.6 copy-start.18
  300.6 3.3 %copy-start.17 = (f32[32,1024]{1,0:T(8,128)S(1)}, f32[32,1024]{1,0:T(8,128)}, u32[]{:S(2)}) copy-start(f32[32,1024]{1,0:T(8,128)} %get-tuple-element.132) | copy-start | bytes 393220
  300.6 3.9 %copy-start.21 = (f32[32,256]{1,0:T(8,128)S(1)}, f32[32,256]{1,0:T(8,128)}, u32[]{:S(2)}) copy-start(f32[32,256]{1,0:T(8,128)} %get-tuple-element.133) | copy-start | bytes 98308
  300.6 4.5 %copy-start.16 = (f32[32,1024]{1,0:T(8,128)S(1)}, f32[32,1024]{1,0:T(8,128)}, u32[]{:S(2)}) copy-start(f32[32,1024]{1,0:T(8,128)} %get-tuple-element.135) | copy-start | bytes 393220
  300.6 5.2 %copy-start.15 = (f32[32,1024]{1,0:T(8,128)S(1)}, f32[32,1024]{1,0:T(8,128)}, u32[]{:S(2)}) copy-start(f32[32,1024]{1,0:T(8,128)} %get-tuple-element.136) | copy-start | bytes 393220
  300.6 5.8 %copy-start.14 = (f32[32,2816]{1,0:T(8,128)S(1)}, f32[32,2816]{1,0:T(8,128)}, u32[]{:S(2)}) copy-start(f32[32,2816]{1,0:T(8,128)} %get-tuple-element.139) | copy-start | bytes 1081348
  301.7 5.5 %copy-start.13 = (f32[32,2816]{1,0:T(8,128)S(1)}, f32[32,2816]{1,0:T(8,128)}, u32[]{:S(2)}) copy-start(f32[32,2816]{1,0:T(8,128)} %get-tuple-element.140) | copy-start | bytes 1081348
  301.7 6.2 %copy-start.12 = (f32[88,1024]{1,0:T(8,128)S(1)}, f32[88,1024]{1,0:T(8,128)}, u32[]{:S(2)}) copy-start(f32[88,1024]{1,0:T(8,128)} %get-tuple-element.141) | copy-start | bytes 1081348

commit v4 on v3

--- a/solution.py
+++ b/solution.py
@@ -138,8 +138,8 @@
         out_ref, first_ref, attn_ref, mdelta_ref, postgain_grad,
         normed_t, merged_t, second_t, hidden_t, gate_delta, up_delta,
         q_ref, k_ref, v_ref, pre_ref, logit_ref,
-        mixed_ref, aff_ref, mixing_ref, weight_ref, inner_ref, state_ref, pass_ref,
-    ), refs = refs[:23], refs[23:]
+        mixed_ref, aff_ref, mixing_ref, weight_ref, inner_ref, state_ref, pass_ref, pass_all,
+    ), refs = refs[:24], refs[24:]
     passed, refs = dict(zip(WEIGHTS[:5], refs[:5])), refs[5:]
     whole, refs = dict(zip(WEIGHTS, refs[:count])), refs[count:]
     (
@@ -343,6 +343,7 @@
     for place in range(size):
         prefix[place] = state.astype(bf16)
         entry = gathered[place].astype(f32)
+        pass_all[place] = gathered[place][:, 2 * head :]
         state = entry[:, 2 * head : 2 * head + 1] * state + entry[:, : 2 * head]
     for d in range(1, size):
         to = others[d - 1]
@@ -483,6 +484,7 @@
         low(n, width), low(n, width), low(n, width), full(n, heads * slots), full(n, width),
         full(n, width), low(heads, n, n), low(heads, n, n), full(n, heads * slots), full(n, heads * slots),
         low(pairs, per + 1, slots, 2 * head), full(pairs * per, slots, 128),
+        low(size, pairs * slots // size, 128),
     ]
     wholes = [low(4 * w.shape[0], w.shape[1]) for w in shards]
     share = pairs * slots // size
@@ -521,133 +523,6 @@
     return got
 
 
-def return_kernel(
-    size, heads, q_ref, k_ref, v_ref, pre_ref, bias_ref, fcol_ref, frow_ref, logit_ref, gain_ref,
-    mixed_ref, aff_ref, mixing_ref, weight_ref, inner_ref, state_ref, pass_ref, delta_ref,
-    q_low, k_low, v_low, forget_low, logit_low, bias_grad, gain_grad,
-    owed, came, going, k_acc, v_acc, dmix, da_acc, doma_acc, send_sem, recv_sem,
-):
-    s, f = lax.axis_index("seq"), lax.axis_index("fsdp")
-    right, left = (lax.rem(s + 1, size), f), (lax.rem(s + size - 1, size), f)
-    greet((left, right))
-    n, width = q_ref.shape
-    head = width // heads
-    slots = pre_ref.shape[1] // heads
-    blocks = n // BLOCK
-    streams = 2
-    per = blocks // streams
-    scale = head ** (-0.5)
-    lower, linked, fresh, ending, unbroken = mask_set(fcol_ref[...], frow_ref[...])
-    z, u, oma, growth, inverse, tail = gate_set(pre_ref[...], bias_ref[...], lower, ending)
-    shrink, kept = inverse * oma, tail * oma
-
-    @pl.when(s == size - 1)
-    def _():
-        came[...] = jnp.zeros_like(came)
-
-    gain_total = jnp.zeros((1, head), f32)
-    for h in range(heads):
-        hs, hd = slice(h * slots, (h + 1) * slots), slice(h * head, (h + 1) * head)
-        mixed, logits, delta = mixed_ref[:, hd], logit_ref[:, hd], delta_ref[:, hd]
-        r = lax.rsqrt(jnp.mean(mixed * mixed, axis=1, keepdims=True) + norm_eps)
-        sig = 1.0 / (1.0 + jnp.exp(-logits))
-        silu = logits * sig
-        unit = mixed * r
-        dy = delta * silu
-        logit_low[:, hd] = (delta * unit * gain_ref[...] * (sig + silu * (1.0 - sig))).astype(bf16)
-        gain_total = gain_total + jnp.sum(dy * unit, axis=0, keepdims=True)
-        dy = dy * gain_ref[...]
-        dmixed = r * (dy - unit * jnp.mean(unit * dy, axis=1, keepdims=True))
-        gr, sh = growth[:, hs], shrink[:, hs].astype(bf16)
-        weights, inner = weight_ref[:, hs], inner_ref[:, hs]
-        aff, mixing = aff_ref[h], mixing_ref[h]
-        qh, kh, vh = q_ref[:, hd], k_ref[:, hd], v_ref[:, hd]
-        do = dmixed.astype(bf16)
-        lifted = (weights * gr).astype(bf16)
-        dm = (dot(do, vh, 1, 1) * linked).astype(bf16)
-        v_acc[:, hd] = dot(mixing, do, 0, 0)
-        fdo = (dmixed * fresh).astype(bf16)
-
-        def states(b, h=h):
-            return state_ref.at[h * streams + b // per, b % per]
-
-        dlift = dot(dm, sh) + jnp.concatenate(
-            [dot(fdo[rows_of(b)], states(b)[:, head:], 1, 1) for b in range(blocks)], axis=0
-        )
-        dsh = dot(dm, lifted, 0, 0)
-        dw = dlift * gr
-        dsc = weights * (dw - jnp.sum(weights * dw, axis=1, keepdims=True))
-        du = dsc * gr
-        du_low = du.astype(bf16)
-        da = (dot(du_low, sh, 1, 1) * (linked * scale)).astype(bf16)
-        dsh = dsh + dot(aff, du_low, 0, 0)
-        fdu = (du * (fresh * scale)).astype(bf16)
-        q_low[:, hd] = (
-            dot(da, kh)
-            + jnp.concatenate(
-                [dot(fdu[rows_of(b)], states(b)[:, :head]) for b in range(blocks)], axis=0
-            )
-        ).astype(bf16)
-        k_acc[:, hd] = dot(da, qh, 0, 0)
-        for b in range(blocks):
-            at = (h * streams + b // per) * per + b % per
-            owed[at, :, :head] = dot(fdu[rows_of(b)], qh[rows_of(b)], 0, 0)
-            owed[at, :, head:] = dot(lifted[rows_of(b)], fdo[rows_of(b)], 0, 0)
-        da_acc[:, hs] = lifted.astype(f32) * dlift + du_low.astype(f32) * inner - dsh * sh.astype(f32)
-        doma_acc[:, hs] = dsh * inverse[:, hs]
-    gain_grad[...] = gain_total
-    sends = []
-    for pair in range(heads * streams):
-        copy = remote(going.at[pair], came.at[pair], (send_sem, recv_sem), pair, left)
-
-        @pl.when(s < size - 1)
-        def _(copy=copy):
-            copy.wait_recv()
-
-        state = came[pair].astype(f32)
-        for b in reversed(range(per)):
-            at = pair * per + b
-            before = owed[at] + pass_ref[at][:, :1] * state
-            owed[at] = state
-            state = before
-        going[pair] = state.astype(bf16)
-
-        @pl.when(s > 0)
-        def _(copy=copy):
-            copy.start()
-
-        sends.append(copy)
-    row = lax.broadcasted_iota(jnp.int32, (BLOCK, 1), 0)
-    for h in range(heads):
-        hs, hd = slice(h * slots, (h + 1) * slots), slice(h * head, (h + 1) * head)
-        for b in range(blocks):
-            rb = rows_of(b)
-            pair = h * streams + b // per
-            at = pair * per + b % per
-            leaving = owed[at]
-            low = leaving.astype(bf16)
-            part = kept[rb, hs].astype(bf16)
-            dkept = dot(k_ref[rb, hd], low[:, :head], 1, 1) + dot(v_ref[rb, hd], low[:, head:], 1, 1)
-            k_low[rb, hd] = (k_acc[rb, hd] + dot(part, low[:, :head])).astype(bf16)
-            v_low[rb, hd] = (v_acc[rb, hd] + dot(part, low[:, head:])).astype(bf16)
-            held = jnp.sum(low.astype(f32) * state_ref[pair, b % per + 1].astype(f32), axis=1, keepdims=True)
-            held_row = to_row(held)
-            da_acc[rb, hs] = (
-                da_acc[rb, hs] - dkept * part.astype(f32) + jnp.where(row == BLOCK - 1, held_row, 0.0)
-            )
-            doma_acc[rb, hs] = doma_acc[rb, hs] + dkept * tail[rb, hs]
-    dg = dot(lower, da_acc[...], 0, 0, count=3) - doma_acc[...] * (1.0 - oma)
-    sig = jnp.where(z >= 0.0, u / (1.0 + u), 1.0 / (1.0 + u))
-    dpre = dg * sig * 0.125
-    forget_low[...] = dpre.astype(bf16)
-    bias_grad[...] = jnp.sum(dpre, axis=0, keepdims=True)
-    for copy in sends:
-
-        @pl.when(s > 0)
-        def _(copy=copy):
-            copy.wait_send()
-
-
 def to_row(col):
     n = col.shape[0]
     i = lax.broadcasted_iota(jnp.int32, (n, n), 0)
@@ -655,40 +530,9 @@
     return jnp.sum(jnp.where(i == j, jnp.broadcast_to(col, (n, n)), 0.0), axis=0, keepdims=True)
 
 
-def go_back(size, heads, q, k, v, pre, bias, fcol, frow, logits, gain, kept, delta):
-    n, width = q.shape
-    head, slots = width // heads, pre.shape[1] // heads
-    pairs, per = heads * 2, n // BLOCK // 2
-    return pl.pallas_call(
-        functools.partial(return_kernel, size, heads),
-        name="go_back",
-        out_shape=[
-            jax.ShapeDtypeStruct((n, width), bf16),
-            jax.ShapeDtypeStruct((n, width), bf16),
-            jax.ShapeDtypeStruct((n, width), bf16),
-            jax.ShapeDtypeStruct(pre.shape, bf16),
-            jax.ShapeDtypeStruct((n, width), bf16),
-            jax.ShapeDtypeStruct((1, pre.shape[1]), f32),
-            jax.ShapeDtypeStruct((1, head), f32),
-        ],
-        in_specs=[in_vmem()] * 17,
-        out_specs=[in_vmem()] * 7,
-        scratch_shapes=[
-            VMEM((pairs * per, slots, 2 * head), f32),
-            VMEM((pairs, slots, 2 * head), bf16),
-            VMEM((pairs, slots, 2 * head), bf16),
-            VMEM((n, width), f32),
-            VMEM((n, width), f32),
-            VMEM((8, 128), f32),
-            VMEM(pre.shape, f32),
-            VMEM(pre.shape, f32),
-            pltpu.SemaphoreType.DMA((pairs,)),
-            pltpu.SemaphoreType.DMA((pairs,)),
-        ],
-        compiler_params=pltpu.CompilerParams(
-            collective_id=3, has_side_effects=True, vmem_limit_bytes=LIMIT
-        ),
-    )(q, k, v, pre, bias, fcol, frow, logits, gain, *kept, delta)
+LEAST, SHALLOW, DEEP = 4.0, 8.0, 10.0
+STRIPS = 3
+BACK_LIMIT = 63 * 2**20
 
 
 def cut(columns, flip):
@@ -705,65 +549,156 @@
     return out
 
 
-def sum_kernel(plan, n_left, n_right, *refs):
-    lefts, refs = refs[:n_left], refs[n_left:]
-    rights, refs = refs[:n_right], refs[n_right:]
-    vec_in, refs = refs[0], refs[1:]
-    outs, refs = refs[: len(plan)], refs[len(plan) :]
-    vec_out, refs = refs[0], refs[1:]
-    left_all, refs = refs[:n_left], refs[n_left:]
-    right_all, refs = refs[:n_right], refs[n_right:]
-    chunks = [(g,) + c for g, p in enumerate(plan) for c in p[5]]
+def in_order(chunks, path, held_back, least, shallow, deep):
+    now, free = 0.0, dict.fromkeys(("x", "y", "z", "zz"), 0.0)
+    came, done, coming, out = {}, set(), [], []
+    path, left = list(path), list(range(len(chunks)))
+    rate, delay = 0.045, 2.0
+
+    def leave(c, stage):
+        rows, width, order = chunks[c][1], chunks[c][3], chunks[c][4]
+        link = (("y", "z", "x", "zz"), ("x", "z", "y", "zz"))[order][stage]
+        size = 16 * rows * width * 2 / 1e6 / 2 ** (stage + 1)
+        free[link] = max(now, free[link]) + size / rate * (2 if stage == 3 else 1)
+        coming.append((free[link] + delay, c, stage))
+
+    while left or path or coming:
+        here = sorted(a for a in coming if a[0] <= now)
+        open_ = [c for c in left if held_back.get(chunks[c][0], None) in done or chunks[c][0] not in held_back]
+        depth = deep if "second hop" in done else shallow
+        queue = free[("y", "x")[chunks[open_[0]][4]]] - now if open_ else 0.0
+        ready = path and came.get(path[0][2], 0.0 if path[0][2] is None else 1e9) <= now
+        if here:
+            _, c, stage = here[0]
+            coming.remove(here[0])
+            now += 0.1 + 0.1 * chunks[c][1] / 32 * chunks[c][3] / TILE / 2**stage
+            out.append(("advance", c, stage))
+            if stage < 3:
+                leave(c, stage + 1)
+        elif ready and not (open_ and queue < least):
+            name, time, _, starts, takes = path.pop(0)
+            now += time
+            done.add(name)
+            out.append(("path", name, None))
+            if starts:
+                came[starts] = now + takes
+        elif open_ and queue < depth:
+            c = open_[0]
+            left.remove(c)
+            now += 0.1 + 0.3 * chunks[c][1] / 32 * chunks[c][3] / TILE
+            out.append(("produce", c, None))
+            leave(c, 0)
+        else:
+            later = [a[0] for a in coming]
+            if path and path[0][2] in came:
+                later.append(came[path[0][2]])
+            if open_:
+                later.append(now + queue - depth)
+            now = max(now + 0.05, min(later))
+    return out
+
+
+FORM = (("cotan", 0), ("gate", 1), ("up", 1), ("attn", 2), ("outgate", 3), ("query", 3), ("key", 3), ("value", 3), ("forget", 3))
+SAVED = ("q", "k", "v", "pre", "logits", "mixed", "aff", "mixing", "weights", "inner", "state", "pass", "mdelta", "pass_all")
+
+
+def back_kernel(size, heads, plan, *refs):
+    def take(count):
+        nonlocal refs
+        got, refs = refs[:count], refs[count:]
+        return got
+
+    lefts, rights, saved = take(4), take(4), dict(zip(SAVED, take(len(SAVED))))
+    weights, (first_in, tokens_in) = take(5), take(2)
+    bias_ref, fcol_ref, frow_ref, head_gain, pre_gain, postgain_ref = take(6)
+    outs, (vec_out, input_grad) = take(9), take(2)
+    left_all, right_all = take(4), take(9)
+    have_ref = dict(zip(SAVED, take(len(SAVED))))
+    chunks = [(g, p[2]) + c for g, p in enumerate(plan) for c in p[4]]
     nc = len(chunks)
-    sums, refs = refs[:nc], refs[nc:]
-    landed = []
-    for _ in range(4):
-        landed.append(refs[:nc])
-        refs = refs[nc:]
-    vec_acc, vec_got, local, in_send, in_recv, st_send, st_recv, v_send, v_recv = refs
+    sums = take(nc)
+    landed = [take(nc) for _ in range(4)]
+    owed, da_acc, doma_acc, strip, going, gathered, prefix, came, vec_acc, vec_got = take(10)
+    loads, in_local, in_send, in_recv, strip_sem, first_sem = take(6)
+    hop_send, hop_recv, st_send, st_recv, v_send, v_recv = take(6)
+    q_ref, k_ref, v_ref = have_ref["q"], have_ref["k"], have_ref["v"]
+    logit_ref, mixed_ref, mdelta_ref = have_ref["logits"], have_ref["mixed"], have_ref["mdelta"]
+    state_ref, pass_ref = have_ref["state"], have_ref["pass"]
+
     s, f = lax.axis_index("seq"), lax.axis_index("fsdp")
     core, y = lax.rem(f, 2), f // 2
     x, z_low, z_high = lax.rem(s, 2), lax.rem(s // 2, 2), lax.rem(s // 4, 2)
     sib, far, nx, nz, nzz = (s, f ^ 1), (s, f ^ 2), (s ^ 1, f), (s ^ 2, f), (s ^ 4, f)
-    greet([sib, far, nx, nz, nzz])
+    others = [(lax.rem(s + d, size), f) for d in range(1, size)]
+    greet([sib, far] + others)
     started = []
 
     def go(copy):
         copy.start()
         started.append(copy)
 
-    tokens = rights[0].shape[0]
+    n, width = q_ref.shape
+    head = width // heads
+    slots = bias_ref.shape[1] // heads
+    blocks = n // BLOCK
+    streams = 2
+    per = blocks // streams
+    pairs = heads * streams
+    scale = head ** (-0.5)
+    share = pairs * slots // size
+
     waiting = {}
 
-    def exchange(kind, i):
-        index = i if kind == 0 else n_left + i
-        if (kind, i) in waiting:
-            return
-        if kind == 0:
-            src_own, src_far = lefts[i].at[core], lefts[i].at[1 - core]
-            dst_own, dst_far = left_all[i].at[:, pl.ds(0, tokens)], left_all[i].at[:, pl.ds(tokens, tokens)]
-        else:
-            src_own = src_far = rights[i]
-            dst_own, dst_far = right_all[i].at[pl.ds(0, tokens)], right_all[i].at[pl.ds(tokens, tokens)]
-        keep = pltpu.make_async_copy(src_own, dst_own, local.at[index])
+    def fetch_left(i):
+        keep = pltpu.make_async_copy(lefts[i].at[core], left_all[i].at[:, pl.ds(0, n)], in_local.at[i])
         keep.start()
-        copy = remote(src_far, dst_far, (in_send, in_recv), index, sib)
+        copy = remote(lefts[i].at[1 - core], left_all[i].at[:, pl.ds(n, n)], (in_send, in_recv), i, sib)
         go(copy)
-        waiting[kind, i] = [keep, copy]
+        waiting["left", i] = [keep, copy]
+
+    def fetch_right(i):
+        own, other = right_all[i].at[pl.ds(0, n)], right_all[i].at[pl.ds(n, n)]
+        keep = None
+        src = own
+        if i < 4:
+            src = rights[i]
+            keep = pltpu.make_async_copy(src, own, in_local.at[4 + i])
+            keep.start()
+        copy = remote(src, other, (in_send, in_recv), 4 + i, sib)
+        go(copy)
+        waiting["right", i] = [keep, copy]
 
     def have(kind, i):
         pair = waiting[kind, i]
         if pair:
-            pair[0].wait()
+            if pair[0] is not None:
+                pair[0].wait()
             pair[1].wait_recv()
             waiting[kind, i] = None
 
-    for left, right, *_ in plan[:2]:
-        exchange(0, left)
-        exchange(1, right)
+    fetch_left(0)
+    fetch_right(0)
+    loading = []
+    for i, name in enumerate(SAVED):
+        copy = pltpu.make_async_copy(saved[name], have_ref[name], loads.at[i])
+        copy.start()
+        loading.append(copy)
+    for i in (1, 2, 3):
+        fetch_right(i)
+    for i in (1, 2, 3):
+        fetch_left(i)
+
+    strips = [(w, t * TILE) for w in range(5) for t in range(weights[w].shape[1] // TILE)]
+
+    def strip_copy(i):
+        w, at = strips[i]
+        return pltpu.make_async_copy(weights[w].at[:, pl.ds(at, TILE)], strip.at[i % STRIPS], strip_sem.at[i % STRIPS])
+
+    for i in range(STRIPS):
+        strip_copy(i).start()
 
     def route(c):
-        if chunks[c][3]:
+        if chunks[c][4]:
             return (x, z_low, y, z_high), (nx, nz, far, nzz)
         return (y, z_low, x, z_high), (far, nz, nx, nzz)
 
@@ -773,20 +708,17 @@
         return remote(sums[c].at[at], landed[stage][c], (st_send, st_recv), (stage, c), partners[stage])
 
     def produce(c):
-        g, start, width, order = chunks[c]
-        left, right, columns, rows, kept, _ = plan[g]
-        have(0, left)
-        have(1, right)
-        for after in plan[g + 1 : g + 3]:
-            exchange(0, after[0])
-            exchange(1, after[1])
-        tile = min(TILE, width)
-
-        def body(i, carry):
+        g, rows, start, wide, order = chunks[c]
+        left = plan[g][0]
+        have("left", left)
+        have("right", g)
+        tile = min(TILE, wide)
+
+        def turn(i, carry):
             at = pl.multiple_of(start + i * tile, 128)
             to = pl.multiple_of(i * tile, 128)
             got = jnp.dot(
-                left_all[left][...], right_all[right][:, pl.ds(at, tile)], preferred_element_type=f32
+                left_all[left][...], right_all[g][:, pl.ds(at, tile)], preferred_element_type=f32
             ).astype(bf16)
             for group in range(16):
                 zh, zl, xx, yy = (group >> 3) & 1, (group >> 2) & 1, (group >> 1) & 1, group & 1
@@ -794,17 +726,16 @@
                 sums[c][*place, :, pl.ds(to, tile)] = got[group * rows : (group + 1) * rows]
             return carry
 
-        lax.fori_loop(0, width // tile, body, 0)
+        lax.fori_loop(0, wide // tile, turn, 0)
         go(stage_copy(c, 0))
 
     def advance(c, stage):
         stage_copy(c, stage).wait_recv()
         bits, _ = route(c)
         if stage == 3:
-            g, start, width, _ = chunks[c]
-            kept = plan[g][4]
+            g, rows, start, wide, _ = chunks[c]
             total = sums[c][bits].astype(f32) + landed[3][c][...].astype(f32)
-            outs[g][:, start : start + width] = total[:kept]
+            outs[g][:, start : start + wide] = total[: plan[g][3]]
             return
         for rest in range(1 << (3 - stage)):
             tail = tuple((rest >> k) & 1 for k in reversed(range(3 - stage)))
@@ -812,69 +743,265 @@
             sums[c][at] = (sums[c][at].astype(f32) + landed[stage][c][tail].astype(f32)).astype(bf16)
         go(stage_copy(c, stage + 1))
 
+    keep = {}
+
+    def begin():
+        for copy in loading:
+            copy.wait()
+        lower, linked, fresh, ending, unbroken = mask_set(fcol_ref[...], frow_ref[...])
+        z, u, oma, growth, inverse, tail = gate_set(have_ref["pre"][...], bias_ref[...], lower, ending)
+        keep.update(lower=lower, linked=linked, fresh=fresh, z=z, u=u, oma=oma, growth=growth)
+        keep.update(inverse=inverse, tail=tail, shrink=inverse * oma, kept=tail * oma)
+        keep["gain"] = jnp.zeros((1, head), f32)
+
+    def states(h, b):
+        return state_ref.at[h * streams + b // per, b % per]
+
+    def one_head(h):
+        linked, fresh, growth, shrink = keep["linked"], keep["fresh"], keep["growth"], keep["shrink"]
+        hs, hd = slice(h * slots, (h + 1) * slots), slice(h * head, (h + 1) * head)
+        mixed, logits, delta = mixed_ref[:, hd], logit_ref[:, hd], mdelta_ref[:, hd]
+        r = lax.rsqrt(jnp.mean(mixed * mixed, axis=1, keepdims=True) + norm_eps)
+        sig = sigmoid(logits)
+        silu = logits * sig
+        unit = mixed * r
+        dy = delta * silu
+        right_all[4][0:n, hd] = (delta * unit * head_gain[...] * (sig + silu * (1.0 - sig))).astype(bf16)
+        keep["gain"] = keep["gain"] + jnp.sum(dy * unit, axis=0, keepdims=True)
+        dy = dy * head_gain[...]
+        dmixed = r * (dy - unit * jnp.mean(unit * dy, axis=1, keepdims=True))
+        gr, sh = growth[:, hs], shrink[:, hs].astype(bf16)
+        weigh, inner = have_ref["weights"][:, hs], have_ref["inner"][:, hs]
+        aff, mixing = have_ref["aff"][h], have_ref["mixing"][h]
+        qh, kh, vh = q_ref[:, hd], k_ref[:, hd], v_ref[:, hd]
+        do = dmixed.astype(bf16)
+        lifted = (weigh * gr).astype(bf16)
+        dm = (dot(do, vh, 1, 1) * linked).astype(bf16)
+        mixed_ref[:, hd] = dot(mixing, do, 0, 0)
+        fdo = (dmixed * fresh).astype(bf16)
+        dlift = dot(dm, sh) + jnp.concatenate(
+            [dot(fdo[rows_of(b)], states(h, b)[:, head:], 1, 1) for b in range(blocks)], axis=0
+        )
+        dsh = dot(dm, lifted, 0, 0)
+        dw = dlift * gr
+        dsc = weigh * (dw - jnp.sum(weigh * dw, axis=1, keepdims=True))
+        du = dsc * gr
+        du_low = du.astype(bf16)
+        da = (dot(du_low, sh, 1, 1) * (linked * scale)).astype(bf16)
+        dsh = dsh + dot(aff, du_low, 0, 0)
+        fdu = (du * (fresh * scale)).astype(bf16)
+        right_all[5][0:n, hd] = (
+            dot(da, kh)
+            + jnp.concatenate([dot(fdu[rows_of(b)], states(h, b)[:, :head]) for b in range(blocks)], axis=0)
+        ).astype(bf16)
+        mdelta_ref[:, hd] = dot(da, qh, 0, 0)
+        for stream in range(streams):
+            pair = h * streams + stream
+            total = None
+            for b in reversed(range(stream * per, (stream + 1) * per)):
+                at = pair * per + b % per
+                own_k = dot(fdu[rows_of(b)], qh[rows_of(b)], 0, 0)
+                own_v = dot(lifted[rows_of(b)], fdo[rows_of(b)], 0, 0)
+                owed[at, :, :head] = own_k.astype(bf16)
+                owed[at, :, head:] = own_v.astype(bf16)
+                if total is not None:
+                    factor = pass_ref[at][:, :1]
+                    own_k, own_v = own_k + factor * total[0], own_v + factor * total[1]
+                total = (own_k, own_v)
+            at = slice(pair * slots, (pair + 1) * slots)
+            going[at, :head] = total[0].astype(bf16)
+            going[at, head:] = total[1].astype(bf16)
+        da_acc[:, hs] = lifted.astype(f32) * dlift + du_low.astype(f32) * inner - dsh * sh.astype(f32)
+        doma_acc[:, hs] = dsh * keep["inverse"][:, hs]
+
+    def rows_for(place):
+        return pl.ds(pl.multiple_of(place * share, 16), share)
+
+    sources = [lax.rem(s + size - d, size) for d in range(1, size)]
+
+    def first_hop():
+        for d in range(1, size):
+            to = others[d - 1]
+            go(remote(going.at[rows_for(to[0])], gathered.at[s], (hop_send, hop_recv), (0, d - 1), to))
+        gathered[s] = going[rows_for(s)]
+        fetch_right(4)
+        fetch_right(5)
+
+    def second_hop():
+        for d in range(1, size):
+            part = gathered.at[sources[d - 1]]
+            remote(part, part, (hop_send, hop_recv), (0, d - 1), sib).wait_recv()
+        state = jnp.zeros((share, 2 * head), f32)
+        for place in reversed(range(size)):
+            prefix[place] = state.astype(bf16)
+            state = have_ref["pass_all"][place][:, :1].astype(f32) * state + gathered[place].astype(f32)
+        for d in range(1, size):
+            to = others[d - 1]
+            go(remote(prefix.at[to[0]], came.at[rows_for(s)], (hop_send, hop_recv), (1, d - 1), to))
+        came[rows_for(s)] = prefix[s]
+
+    def last_hop():
+        for d in range(1, size):
+            part = came.at[rows_for(sources[d - 1])]
+            remote(part, part, (hop_send, hop_recv), (1, d - 1), sib).wait_recv()
+
+    def end_head(h):
+        kept, tail = keep["kept"], keep["tail"]
+        row = lax.broadcasted_iota(jnp.int32, (BLOCK, 1), 0)
+        hs, hd = slice(h * slots, (h + 1) * slots), slice(h * head, (h + 1) * head)
+        for stream in range(streams):
+            pair = h * streams + stream
+            leaving = came[pair * slots : (pair + 1) * slots].astype(f32)
+            for i in reversed(range(per)):
+                at, rb = pair * per + i, rows_of(stream * per + i)
+                low = leaving.astype(bf16)
+                part = kept[rb, hs].astype(bf16)
+                dkept = dot(k_ref[rb, hd], low[:, :head], 1, 1) + dot(v_ref[rb, hd], low[:, head:], 1, 1)
+                right_all[6][rb, hd] = (mdelta_ref[rb, hd] + dot(part, low[:, :head])).astype(bf16)
+                right_all[7][rb, hd] = (mixed_ref[rb, hd] + dot(part, low[:, head:])).astype(bf16)
+                held = jnp.sum(low.astype(f32) * state_ref[pair, i + 1].astype(f32), axis=1, keepdims=True)
+                da_acc[rb, hs] = (
+                    da_acc[rb, hs] - dkept * part.astype(f32) + jnp.where(row == BLOCK - 1, to_row(held), 0.0)
+                )
+                doma_acc[rb, hs] = doma_acc[rb, hs] + dkept * tail[rb, hs]
+                if i > 0:
+                    leaving = owed[at].astype(f32) + pass_ref[at][:, :1] * leaving
+
+    def end_gates():
+        fetch_right(6)
+        fetch_right(7)
+        z, u = keep["z"], keep["u"]
+        dg = dot(keep["lower"], da_acc[...], 0, 0, count=3) - doma_acc[...] * (1.0 - keep["oma"])
+        sig = jnp.where(z >= 0.0, u / (1.0 + u), 1.0 / (1.0 + u))
+        dpre = dg * sig * 0.125
+        right_all[8][0:n] = dpre.astype(bf16)
+        fetch_right(8)
+        pltpu.make_async_copy(first_in, mdelta_ref, first_sem.at[0]).start()
+        pltpu.make_async_copy(tokens_in, q_ref, first_sem.at[1]).start()
+        vec_acc[0] = jnp.zeros(vec_acc.shape[1:], f32)
+        vec_acc[0, 1:2, : dpre.shape[1]] = jnp.sum(dpre, axis=0, keepdims=True)
+        vec_acc[0, 2:3, :head] = keep["gain"]
+        vec_acc[0, 3:4, :] = postgain_ref[...]
+
+    def strip_step(i):
+        strip_copy(i).wait()
+        w, at = strips[i]
+        term = dot(right_all[(6, 7, 8, 5, 4)[w]][0:n, at : at + TILE], strip[i % STRIPS], 1, 1)
+        logit_ref[...] = term if i == 0 else logit_ref[...] + term
+        if i + STRIPS < len(strips):
+            strip_copy(i + STRIPS).start()
+
+    def end_norm():
+        pltpu.make_async_copy(first_in, mdelta_ref, first_sem.at[0]).wait()
+        pltpu.make_async_copy(tokens_in, q_ref, first_sem.at[1]).wait()
+        inputs = q_ref[...].astype(f32)
+        r = lax.rsqrt(jnp.mean(inputs * inputs, axis=1, keepdims=True) + norm_eps)
+        unit = inputs * r
+        delta = logit_ref[...]
+        vec_acc[0, 0:1, :] = jnp.sum(delta * unit, axis=0, keepdims=True)
+        delta = delta * pre_gain[...]
+        input_grad[...] = (
+            mdelta_ref[...] + r * (delta - unit * jnp.mean(unit * delta, axis=1, keepdims=True))
+        ).astype(bf16)
+        go(v_copy(0))
+
     def v_copy(i):
         return remote(vec_acc.at[i], vec_got.at[i], (v_send, v_recv), i, (sib, far, nx, nz, nzz)[i])
 
-    def vector(step):
-        if step == 0:
-            vec_acc[0] = vec_in[...]
+    def vector(i):
+        v_copy(i).wait_recv()
+        total = vec_acc[i] + vec_got[i]
+        if i == 4:
+            vec_out[...] = total
+            return
+        vec_acc[i + 1] = total
+        go(v_copy(i + 1))
+
+    steps = {"begin": begin}
+    path = [("begin", 2.0, None, None, 0)]
+    for h in range(heads):
+        steps["head", h] = functools.partial(one_head, h)
+        path.append((("head", h), 3.0, None, None, 0))
+    steps.update({"first hop": first_hop, "second hop": second_hop, "last hop": last_hop})
+    path.append(("first hop", 0.5, None, "first", 12.0))
+    path.append(("second hop", 1.0, "first", "second", 12.0))
+    path.append(("last hop", 0.1, "second", None, 0))
+    for h in range(heads):
+        steps["end", h] = functools.partial(end_head, h)
+        path.append((("end", h), 1.2, None, None, 0))
+    steps["gates"] = end_gates
+    path.append(("gates", 1.0, None, None, 0))
+    for i in range(len(strips)):
+        steps["strip", i] = functools.partial(strip_step, i)
+        path.append((("strip", i), 0.4, None, None, 0))
+    steps["norm"] = end_norm
+    path.append(("norm", 1.5, None, ("vector", 0), 3.0))
+    for i in range(5):
+        steps["vector", i] = functools.partial(vector, i)
+        path.append((("vector", i), 0.1, ("vector", i), ("vector", i + 1), 4.0))
+    held_back = {4: "first hop", 5: "first hop", 6: "gates", 7: "gates", 8: "gates"}
+    for what, which, stage in in_order(chunks, path, held_back, LEAST, SHALLOW, DEEP):
+        if what == "path":
+            steps[which]()
+        elif what == "produce":
+            produce(which)
         else:
-            v_copy(step - 1).wait_recv()
-            total = vec_acc[step - 1] + vec_got[step - 1]
-            if step == 5:
-                vec_out[...] = total
-                return
-            vec_acc[step] = total
-        go(v_copy(step))
-
-    lag = 3
-    steps = nc + 4 * lag
-    for t in range(steps):
-        if t < nc:
-            produce(t)
-        for stage in range(4):
-            c = t - (stage + 1) * lag
-            if 0 <= c < nc:
-                advance(c, stage)
-        if steps - 7 <= t < steps - 1:
-            vector(t - (steps - 7))
+            advance(which, stage)
     for copy in started:
         copy.wait_send()
 
 
-def sum_grads(plan, lefts, rights, vectors):
-    tokens = rights[0].shape[0]
-    chunks = [(p[3],) + c for p in plan for c in p[5]]
+def back(size, heads, plan, lefts, rights, saved, weights, first, tokens, bias, fcol, frow, head_gain, pre_gain, postgain):
+    n, width = saved["q"].shape
+    head, slots = width // heads, bias.shape[1] // heads
+    pairs, per = heads * 2, n // BLOCK // 2
+    share = pairs * slots // size
+    chunks = [(p[2],) + c for p in plan for c in p[4]]
     nc = len(chunks)
     dma = pltpu.SemaphoreType.DMA
-    n_in = len(lefts) + len(rights)
-    scratch = [VMEM((a.shape[1], 2 * tokens), bf16) for a in lefts]
-    scratch += [VMEM((2 * tokens, b.shape[1]), bf16) for b in rights]
+    saved = [saved[name] for name in SAVED]
+    scratch = [VMEM((a.shape[1], 2 * n), bf16) for a in lefts]
+    scratch += [VMEM((2 * n, p[1]), bf16) for p in plan]
+    scratch += [VMEM(a.shape, a.dtype) for a in saved]
     for lead in ((2, 2, 2, 2), (2, 2, 2), (2, 2), (2,), ()):
         scratch += [VMEM(lead + (r, w), bf16) for r, _, w, _ in chunks]
-    scratch += [VMEM((5,) + vectors.shape, f32)] * 2
-    scratch += [dma((n_in,))] * 3 + [dma((4, nc))] * 2 + [dma((5,))] * 2
+    scratch += [
+        VMEM((pairs * per, slots, 2 * head), bf16),
+        VMEM((n, heads * slots), f32),
+        VMEM((n, heads * slots), f32),
+        VMEM((STRIPS, width, TILE), bf16),
+        VMEM((pairs * slots, 2 * head), bf16),
+        VMEM((size, share, 2 * head), bf16),
+        VMEM((size, share, 2 * head), bf16),
+        VMEM((pairs * slots, 2 * head), bf16),
+        VMEM((5, 8, width), f32),
+        VMEM((5, 8, width), f32),
+        dma((len(SAVED),)),
+        dma((8,)),
+        dma((13,)),
+        dma((13,)),
+        dma((STRIPS,)),
+        dma((2,)),
+        dma((2, size - 1)),
+        dma((2, size - 1)),
+        dma((4, nc)),
+        dma((4, nc)),
+        dma((5,)),
+        dma((5,)),
+    ]
     out = pl.pallas_call(
-        functools.partial(sum_kernel, plan, len(lefts), len(rights)),
-        name="sum_grads",
-        out_shape=[jax.ShapeDtypeStruct((p[4], p[2]), f32) for p in plan]
-        + [jax.ShapeDtypeStruct(vectors.shape, f32)],
-        in_specs=[in_place()] * n_in + [in_vmem()],
-        out_specs=[in_vmem()] * (len(plan) + 1),
+        functools.partial(back_kernel, size, heads, plan),
+        name="back",
+        out_shape=[jax.ShapeDtypeStruct((p[3], p[1]), f32) for p in plan]
+        + [jax.ShapeDtypeStruct((8, width), f32), jax.ShapeDtypeStruct((n, width), bf16)],
+        in_specs=[in_place()] * (8 + len(saved) + 7) + [in_vmem()] * 6,
+        out_specs=[in_vmem()] * (len(plan) + 2),
         scratch_shapes=scratch,
         compiler_params=pltpu.CompilerParams(
-            collective_id=4, has_side_effects=True, vmem_limit_bytes=LIMIT
+            collective_id=2, has_side_effects=True, vmem_limit_bytes=BACK_LIMIT
         ),
-    )(*lefts, *rights, vectors)
-    return out[:-1], out[-1]
-
-
-def rms_norm(values, gain):
-    return values * lax.rsqrt(jnp.mean(values * values, axis=-1, keepdims=True) + norm_eps) * gain
-
-
-def back_dot(left, right):
-    return lax.dot_general(left, right, (((1,), (1,)), ((), ())), preferred_element_type=f32)
+    )(*lefts, *rights, *saved, *weights, first, tokens, bias, fcol, frow, head_gain, pre_gain, postgain)
+    return out[: len(plan)], out[-2], out[-1]
 
 
 def by_owner(a, hi, lo):
@@ -901,7 +1028,8 @@
         "query": query_weight, "key": key_weight, "value": value_weight, "forget": forget_weight,
         "outgate": outgate_weight, "output": output_weight, "gate": gate_weight, "up": up_weight, "down": down_weight,
     }
-    cotan = cotangent.reshape(n, width)
+    ff = gate_weight.shape[1]
+    flat, cotan = tokens.reshape(n, width), cotangent.reshape(n, width)
     flags = resets.reshape(n).astype(f32)
     fcol = jnp.broadcast_to(flags[:, None], (n, 128))
     frow = jnp.broadcast_to(flags[None], (8, n))
@@ -909,42 +1037,29 @@
     (
         block_output, first_delta, attn_delta, merged_delta, postgain_grad,
         normed_t, merged_t, second_t, hidden_t, gate_delta, up_delta,
-        q, k, v, pre, logits, *kept, wk, wv, wf, wq, wg,
+        q, k, v, pre, logits, mixed, aff, mixing, weights, inner, state, passed, pass_all, *wholes,
     ) = front(
-        size, heads, hi == 1, shards, tokens.reshape(n, width), cotan, pre_gain[None], post_gain[None],
+        size, heads, hi == 1, shards, flat, cotan, pre_gain[None], post_gain[None],
         gain, bias, fcol, frow,
     )
-    q_low, k_low, v_low, forget_low, logit_low, bias_grad, headgain_grad = go_back(
-        size, heads, q, k, v, pre, bias, fcol, frow, logits, gain, kept, merged_delta
-    )
-    normed_delta = (
-        back_dot(q_low, wq)
-        + back_dot(k_low, wk)
-        + back_dot(v_low, wv)
-        + back_dot(forget_low, wf)
-        + back_dot(logit_low, wg)
-    )
-    inputs = tokens.reshape(n, width).astype(f32)
-    normed_full, norm_back = jax.vjp(rms_norm, inputs, pre_gain)
-    input_delta, pregain_grad = norm_back(normed_delta)
-    input_grad = (first_delta + input_delta).astype(bf16)
-
     lefts = [hidden_t, second_t, merged_t, normed_t]
     if hi > 1:
         lefts = [by_owner(a, hi, lo) for a in lefts]
-    rights = [cotan, gate_delta, up_delta, attn_delta, logit_low, q_low, k_low, v_low, forget_low]
-    which = (0, 1, 1, 2, 3, 3, 3, 3, 3)
-    features = (gate_delta.shape[1],) + (width,) * 8
+    rights = [cotan, gate_delta, up_delta, attn_delta]
+    columns = (width, ff, ff, width, width, width, width, width, bias.shape[1])
     plan = []
-    for i, (left, right) in enumerate(zip(which, rights)):
-        kept_rows = features[i] // (lo * 4)
-        columns = right.shape[1]
-        plan.append((left, i, columns, -(-kept_rows // 16) * 16, kept_rows, tuple(cut(columns, i % 2))))
-    sizes = (width, bias.shape[1], head, width)
-    vectors = jnp.concatenate([pregain_grad, bias_grad[0], headgain_grad[0], postgain_grad[0]])
-    total = vectors.shape[0]
-    vectors = jnp.pad(vectors, (0, -total % 1024)).reshape(8, -1)
-    grads, vectors = sum_grads(tuple(plan), lefts, rights, vectors)
+    for i, (name, left) in enumerate(FORM):
+        kept_rows = (ff if i == 0 else width) // (lo * 4)
+        plan.append((left, columns[i], -(-kept_rows // 16) * 16, kept_rows, tuple(cut(columns[i], i % 2))))
+    saved = dict(
+        q=q, k=k, v=v, pre=pre, logits=logits, mixed=mixed, aff=aff, mixing=mixing, weights=weights, inner=inner,
+        state=state, mdelta=merged_delta, pass_all=pass_all,
+    )
+    saved["pass"] = passed
+    grads, vectors, input_grad = back(
+        size, heads, tuple(plan), lefts, rights, saved, wholes, first_delta, flat, bias, fcol, frow, gain,
+        pre_gain[None], postgain_grad,
+    )
     if hi > 1:
         alike = [[a * lo + b for a in range(hi)] for b in range(lo)]
         grads = [
@@ -953,9 +1068,7 @@
         ]
         vectors = lax.psum(vectors, "seq", axis_index_groups=alike)
     down_grad, gate_grad, up_grad, output_grad, outgate_grad, query_grad, key_grad, value_grad, forget_grad = grads
-    vectors = vectors.reshape(-1)
-    ends = [sum(sizes[: i + 1]) for i in range(4)]
-    pregain, bias_total, headgain, postgain = [vectors[e - w : e] for e, w in zip(ends, sizes)]
+    pregain, bias_total, headgain, postgain = vectors[0], vectors[1, : bias.shape[1]], vectors[2, :head], vectors[3]
     shape = tokens.shape
     return (
         block_output.reshape(shape), input_grad.reshape(shape), pregain, query_grad, key_grad, value_grad,

time: 310 us -> 277 us (0.89)
  Pallas kernels: 288 us -> 262 us
  matrix products: 4.99 us -> 0 us
    pallas_call x2 -> x1, Pallas kernels: 179 us -> 153 us  [back(): pl.pallas_call(functools.partial(back_kernel, size, heads, plan), name='b...]
    dot_general x5 -> x0, matrix products: 4.99 us -> none  [back_dot(): lax.dot_general(left, right, (((1,), (1,)), ((), ())), preferred_element_...]
    unnamed x60 -> x31, local copies, waits for them, and re-layouts: 8.99 us -> 8.85 us
where the time goes in v4:
time: 277 us
  Pallas kernels  262 us (95%)
  local copies, waits for them, and re-layouts  13 us (5%)
    pallas_call x1, Pallas kernels, back(): pl.pallas_call(functools.partial(back_kernel, size, heads, plan), name='b...  153 us
    pallas_call x1, Pallas kernels, front(): pl.pallas_call(functools.partial(front_kernel, size, heads, grouped), nam...  109 us
    unnamed x31, local copies, waits for them, and re-layouts  8.85 us

profile of v4, /device:TPU:0, one launch (start us, length us, event | category | flops | bytes accessed | tf_op | source)
XLA Modules:
  0.0 276.8 jit_solution(6610441519346829180)
XLA Ops:
  0.6 0.7 convert_bitcast_fusion
  1.3 0.6 broadcast_in_dim.30.refs_16_.refs_31_
  1.9 0.8 broadcast_in_dim.29.refs_15_.refs_30_
  2.7 109.1 %front.1 = (bf16[256,1024]{1,0:T(8,128)(2,1)}, f32[256,1024]{1,0:T(8,128)}, bf16[256,1024]{1,0:T(8,128)(2,1)}, f32[256,1024]{1,0:T(8,128)}, f32[1,1024]{1,0:T(1,...) custom-call(bf16[256,1024]{1,0:T(8,128)(2,1)} %refs_0_.1, ...), custom_call_target="tpu_custom_call" | custom-call | tf_op jit(solution)/shard_map/front/pallas_call | solution.py:492
  111.8 0.0 copy-start
  111.8 153.3 %back.1 = (f32[88,1024]{1,0:T(8,128)}, f32[32,2816]{1,0:T(8,128)}, f32[32,2816]{1,0:T(8,128)}, f32[32,1024]{1,0:T(8,128)}, f32[32,1024]{1,0:T(8,128)}, /*index=5...) custom-call(bf16[2,1536,256]{2,1,0:T(8,128)(2,1)} %get-tuple-element, ...), custom_call_target="tpu_custom_call" | custom-call | tf_op jit(solution)/shard_map/back/pallas_call | solution.py:992
  265.2 0.0 copy-start.8
  265.2 0.0 copy-start.7
  265.2 0.0 copy-start.6
  265.2 0.0 copy-start.9
  265.2 0.0 copy-start.5
  265.2 1.4 fusion.1
  266.6 1.4 fusion
  268.0 0.0 copy-done
  268.0 0.8 copy.42
  268.8 1.9 copy.43
  270.7 0.0 copy-done.8
  270.7 0.7 copy.44
  271.4 0.0 copy-done.7
  271.4 0.7 copy.45
  272.0 0.0 copy-done.6
  272.0 0.7 copy.46
  272.7 0.0 copy-done.9
  272.7 0.6 copy.47
  273.3 0.0 copy-done.5
  273.3 0.7 copy.48
  274.0 0.0 copy-done.4
  274.0 0.7 copy.49
  274.6 0.0 copy-done.3
  274.6 0.7 copy.50
  275.4 0.7 copy.51
  276.1 0.7 copy.52
  (6 shorter events, 0.0 us)
Async XLA Ops:
  111.8 156.2 %copy-start = (bf16[256,1024]{1,0:T(8,128)(2,1)S(1)}, bf16[256,1024]{1,0:T(8,128)(2,1)}, u32[]{:S(2)}) copy-start(bf16[256,1024]{1,0:T(8,128)(2,1)} %get-tuple-element.55) | copy-start | bytes 1572868
  265.2 5.6 %copy-start.8 = (f32[32,1024]{1,0:T(8,128)S(1)}, f32[32,1024]{1,0:T(8,128)}, u32[]{:S(2)}) copy-start(f32[32,1024]{1,0:T(8,128)} %get-tuple-element.117) | copy-start | bytes 393220
  265.2 6.2 %copy-start.7 = (f32[32,1024]{1,0:T(8,128)S(1)}, f32[32,1024]{1,0:T(8,128)}, u32[]{:S(2)}) copy-start(f32[32,1024]{1,0:T(8,128)} %get-tuple-element.118) | copy-start | bytes 393220
  265.2 6.9 %copy-start.6 = (f32[32,1024]{1,0:T(8,128)S(1)}, f32[32,1024]{1,0:T(8,128)}, u32[]{:S(2)}) copy-start(f32[32,1024]{1,0:T(8,128)} %get-tuple-element.119) | copy-start | bytes 393220
  265.2 7.5 %copy-start.9 = (f32[32,256]{1,0:T(8,128)S(1)}, f32[32,256]{1,0:T(8,128)}, u32[]{:S(2)}) copy-start(f32[32,256]{1,0:T(8,128)} %get-tuple-element.120) | copy-start | bytes 98308
  265.2 8.1 %copy-start.5 = (f32[32,1024]{1,0:T(8,128)S(1)}, f32[32,1024]{1,0:T(8,128)}, u32[]{:S(2)}) copy-start(f32[32,1024]{1,0:T(8,128)} %get-tuple-element.122) | copy-start | bytes 393220
  268.0 6.0 %copy-start.4 = (f32[32,1024]{1,0:T(8,128)S(1)}, f32[32,1024]{1,0:T(8,128)}, u32[]{:S(2)}) copy-start(f32[32,1024]{1,0:T(8,128)} %get-tuple-element.123) | copy-start | bytes 393220
  268.0 6.6 %copy-start.3 = (f32[32,2816]{1,0:T(8,128)S(1)}, f32[32,2816]{1,0:T(8,128)}, u32[]{:S(2)}) copy-start(f32[32,2816]{1,0:T(8,128)} %get-tuple-element.126) | copy-start | bytes 1081348
  268.8 6.6 %copy-start.2 = (f32[32,2816]{1,0:T(8,128)S(1)}, f32[32,2816]{1,0:T(8,128)}, u32[]{:S(2)}) copy-start(f32[32,2816]{1,0:T(8,128)} %get-tuple-element.127) | copy-start | bytes 1081348
  270.7 5.4 %copy-start.1 = (f32[88,1024]{1,0:T(8,128)S(1)}, f32[88,1024]{1,0:T(8,128)}, u32[]{:S(2)}) copy-start(f32[88,1024]{1,0:T(8,128)} %get-tuple-element.128) | copy-start | bytes 1081348

commit v5 on v4

--- a/solution.py
+++ b/solution.py
@@ -72,15 +72,17 @@
     return jnp.sum(jnp.where(i == j, jnp.broadcast_to(row, (n, n)), 0.0), axis=1, keepdims=True)
 
 
-def mask_set(flags_col, flags_row):
-    n = flags_col.shape[0]
+def mask_set(flags):
+    row = jnp.concatenate([flags[i : i + 1].astype(f32) for i in range(flags.shape[0])], axis=1)
+    n = row.shape[1]
+    flags_row = jnp.broadcast_to(row, (8, n))
     i = lax.broadcasted_iota(jnp.int32, (n, n), 0)
     j = lax.broadcasted_iota(jnp.int32, (n, n), 1)
     same = (i // BLOCK) == (j // BLOCK)
     lower = jnp.where(same & (i >= j), 1.0, 0.0)
     block = jnp.where(same, 1.0, 0.0)
-    seen_col = dot(lower, flags_col)[:, :1]
-    all_col = dot(block, flags_col)[:, :1]
+    seen_col = dot(lower, flags_row, 1, 1)[:, :1]
+    all_col = dot(block, flags_row, 1, 1)[:, :1]
     seen_row = dot(flags_row, lower, 1, 1)[:1, :]
     linked = jnp.where(seen_col == seen_row, lower, 0.0)
     fresh = jnp.where(seen_col == 0.0, 1.0, 0.0)
@@ -127,13 +129,13 @@
 
 
 WEIGHTS = ("key", "value", "forget", "query", "outgate", "output", "gate", "up", "down")
-TWICE = ("gate", "up")
+TWICE = ("gate", "up", "down")
 
 
 def front_kernel(size, heads, grouped, *refs):
     count = len(WEIGHTS)
     shards, refs = dict(zip(WEIGHTS, refs[:count])), refs[count:]
-    (tok_ref, cot_ref, pre_gain, post_gain, head_gain, bias_ref, fcol_ref, frow_ref), refs = refs[:8], refs[8:]
+    (tok_ref, cot_ref, pre_gain, post_gain, head_gain, bias_ref, flag_ref), refs = refs[:7], refs[7:]
     (
         out_ref, first_ref, attn_ref, mdelta_ref, postgain_grad,
         normed_t, merged_t, second_t, hidden_t, gate_delta, up_delta,
@@ -288,7 +290,7 @@
     for m, to_ref in (("key", k_ref), ("value", v_ref), ("forget", pre_ref)):
         ready(m)
         project(m, to_ref)
-    lower, linked, fresh, ending, unbroken = mask_set(fcol_ref[...], frow_ref[...])
+    lower, linked, fresh, ending, unbroken = mask_set(flag_ref[...])
     z, u, oma, growth, inverse, tail = gate_set(pre_ref[...], bias_ref[...], lower, ending)
     shrink, kept = inverse * oma, tail * oma
     for h in range(heads):
@@ -458,7 +460,7 @@
         copy.wait_send()
 
 
-def front(size, heads, grouped, shards, tokens, cotan, pre_gain, post_gain, head_gain, bias, fcol, frow):
+def front(size, heads, grouped, shards, tokens, cotan, pre_gain, post_gain, head_gain, bias, flags):
     n, width = tokens.shape
     head, slots = width // heads, bias.shape[1] // heads
     pairs, per = heads * 2, n // BLOCK // 2
@@ -493,7 +495,7 @@
         functools.partial(front_kernel, size, heads, grouped),
         name="front",
         out_shape=outs + wholes[:5],
-        in_specs=[in_place()] * count + [in_vmem()] * 8,
+        in_specs=[in_place()] * count + [in_vmem()] * 7,
         out_specs=[in_vmem()] * len(outs) + [in_place()] * 5,
         scratch_shapes=[VMEM(w.shape, bf16) for w in wholes]
         + [
@@ -519,7 +521,7 @@
         compiler_params=pltpu.CompilerParams(
             collective_id=1, has_side_effects=True, vmem_limit_bytes=LIMIT
         ),
-    )(*shards, tokens, cotan, pre_gain, post_gain, head_gain, bias, fcol, frow)
+    )(*shards, tokens, cotan, pre_gain, post_gain, head_gain, bias, flags)
     return got
 
 
@@ -535,18 +537,33 @@
 BACK_LIMIT = 63 * 2**20
 
 
-def cut(columns, flip):
-    tiles = columns // TILE
-    if tiles <= 1:
-        half = columns // 2
-        return [(0, half, flip), (half, half, 1 - flip)]
-    pieces = 4 if tiles <= 4 else 6
-    out, start = [], 0
-    for i in range(pieces):
-        count = tiles // pieces + (1 if i < tiles % pieces else 0)
-        out.append((start, count * TILE, (i + flip) % 2))
-        start += count * TILE
-    return out
+ROUTES = (("y", "z", "x", "zz"), ("x", "z", "y", "zz"), ("y", "x", "z", "zz"), ("x", "y", "z", "zz"))
+STATES = {"x": 1.15, "y": 0.0, "z": 1.75}
+
+
+def cut(sizes):
+    load, plan, last = dict(STATES), [], 1
+    for columns, rows in sizes:
+        tiles = columns // TILE
+        pieces = min(4, 2 * tiles) if tiles <= 4 else 6
+        width = columns // pieces if tiles <= 1 else TILE
+        out, start = [], 0
+        for i in range(pieces):
+            count = 1 if tiles <= 1 else tiles // pieces + (1 if i < tiles % pieces else 0)
+            size = 2 * 16 * rows * width * count * 2 / 1e6
+
+            def after(route):
+                new = dict(load)
+                for stage, link in enumerate(ROUTES[route]):
+                    new["z" if link == "zz" else link] += size / 2 ** (stage + 1)
+                return new
+
+            route = min((1 - last, 3 - last), key=lambda r: sum(v**4 for v in after(r).values()))
+            load, last = after(route), route % 2
+            out.append((start, width * count, route))
+            start += width * count
+        plan.append(tuple(out))
+    return plan
 
 
 def in_order(chunks, path, held_back, least, shallow, deep):
@@ -557,7 +574,7 @@
 
     def leave(c, stage):
         rows, width, order = chunks[c][1], chunks[c][3], chunks[c][4]
-        link = (("y", "z", "x", "zz"), ("x", "z", "y", "zz"))[order][stage]
+        link = ROUTES[order][stage]
         size = 16 * rows * width * 2 / 1e6 / 2 ** (stage + 1)
         free[link] = max(now, free[link]) + size / rate * (2 if stage == 3 else 1)
         coming.append((free[link] + delay, c, stage))
@@ -566,7 +583,7 @@
         here = sorted(a for a in coming if a[0] <= now)
         open_ = [c for c in left if held_back.get(chunks[c][0], None) in done or chunks[c][0] not in held_back]
         depth = deep if "second hop" in done else shallow
-        queue = free[("y", "x")[chunks[open_[0]][4]]] - now if open_ else 0.0
+        queue = free[ROUTES[chunks[open_[0]][4]][0]] - now if open_ else 0.0
         ready = path and came.get(path[0][2], 0.0 if path[0][2] is None else 1e9) <= now
         if here:
             _, c, stage = here[0]
@@ -610,7 +627,7 @@
 
     lefts, rights, saved = take(4), take(4), dict(zip(SAVED, take(len(SAVED))))
     weights, (first_in, tokens_in) = take(5), take(2)
-    bias_ref, fcol_ref, frow_ref, head_gain, pre_gain, postgain_ref = take(6)
+    bias_ref, flag_ref, head_gain, pre_gain, postgain_ref = take(5)
     outs, (vec_out, input_grad) = take(9), take(2)
     left_all, right_all = take(4), take(9)
     have_ref = dict(zip(SAVED, take(len(SAVED))))
@@ -698,9 +715,9 @@
         strip_copy(i).start()
 
     def route(c):
-        if chunks[c][4]:
-            return (x, z_low, y, z_high), (nx, nz, far, nzz)
-        return (y, z_low, x, z_high), (far, nz, nx, nzz)
+        names = ROUTES[chunks[c][4]]
+        places, partners = dict(x=x, y=y, z=z_low, zz=z_high), dict(x=nx, y=far, z=nz, zz=nzz)
+        return tuple(places[i] for i in names), tuple(partners[i] for i in names)
 
     def stage_copy(c, stage):
         bits, partners = route(c)
@@ -721,8 +738,8 @@
                 left_all[left][...], right_all[g][:, pl.ds(at, tile)], preferred_element_type=f32
             ).astype(bf16)
             for group in range(16):
-                zh, zl, xx, yy = (group >> 3) & 1, (group >> 2) & 1, (group >> 1) & 1, group & 1
-                place = (xx, zl, yy, zh) if order else (yy, zl, xx, zh)
+                bits = dict(zz=group >> 3 & 1, z=group >> 2 & 1, x=group >> 1 & 1, y=group & 1)
+                place = tuple(bits[i] for i in ROUTES[order])
                 sums[c][*place, :, pl.ds(to, tile)] = got[group * rows : (group + 1) * rows]
             return carry
 
@@ -748,7 +765,7 @@
     def begin():
         for copy in loading:
             copy.wait()
-        lower, linked, fresh, ending, unbroken = mask_set(fcol_ref[...], frow_ref[...])
+        lower, linked, fresh, ending, unbroken = mask_set(flag_ref[...])
         z, u, oma, growth, inverse, tail = gate_set(have_ref["pre"][...], bias_ref[...], lower, ending)
         keep.update(lower=lower, linked=linked, fresh=fresh, z=z, u=u, oma=oma, growth=growth)
         keep.update(inverse=inverse, tail=tail, shrink=inverse * oma, kept=tail * oma)
@@ -951,7 +968,7 @@
         copy.wait_send()
 
 
-def back(size, heads, plan, lefts, rights, saved, weights, first, tokens, bias, fcol, frow, head_gain, pre_gain, postgain):
+def back(size, heads, plan, lefts, rights, saved, weights, first, tokens, bias, flags, head_gain, pre_gain, postgain):
     n, width = saved["q"].shape
     head, slots = width // heads, bias.shape[1] // heads
     pairs, per = heads * 2, n // BLOCK // 2
@@ -994,14 +1011,35 @@
         name="back",
         out_shape=[jax.ShapeDtypeStruct((p[3], p[1]), f32) for p in plan]
         + [jax.ShapeDtypeStruct((8, width), f32), jax.ShapeDtypeStruct((n, width), bf16)],
-        in_specs=[in_place()] * (8 + len(saved) + 7) + [in_vmem()] * 6,
+        in_specs=[in_place()] * (8 + len(saved) + 7) + [in_vmem()] * 5,
         out_specs=[in_vmem()] * (len(plan) + 2),
         scratch_shapes=scratch,
         compiler_params=pltpu.CompilerParams(
             collective_id=2, has_side_effects=True, vmem_limit_bytes=BACK_LIMIT
         ),
-    )(*lefts, *rights, *saved, *weights, first, tokens, bias, fcol, frow, head_gain, pre_gain, postgain)
+    )(*lefts, *rights, *saved, *weights, first, tokens, bias, flags, head_gain, pre_gain, postgain)
     return out[: len(plan)], out[-2], out[-1]
+
+
+def finish_kernel(count, *refs):
+    vectors, outs = refs[count], refs[count + 1 :]
+    for i in range(count):
+        outs[i][...] = refs[i][...]
+    for i, out in enumerate(outs[count:]):
+        out[...] = vectors[i, : out.shape[0]]
+
+
+def finish(arrays, vectors, sizes):
+    count = len(arrays)
+    return pl.pallas_call(
+        functools.partial(finish_kernel, count),
+        name="finish",
+        out_shape=[jax.ShapeDtypeStruct(a.shape, a.dtype) for a in arrays]
+        + [jax.ShapeDtypeStruct((size,), f32) for size in sizes],
+        in_specs=[in_vmem()] * (count + 1),
+        out_specs=[in_vmem()] * (count + len(sizes)),
+        compiler_params=pltpu.CompilerParams(vmem_limit_bytes=LIMIT),
+    )(*arrays, vectors)
 
 
 def by_owner(a, hi, lo):
@@ -1030,9 +1068,6 @@
     }
     ff = gate_weight.shape[1]
     flat, cotan = tokens.reshape(n, width), cotangent.reshape(n, width)
-    flags = resets.reshape(n).astype(f32)
-    fcol = jnp.broadcast_to(flags[:, None], (n, 128))
-    frow = jnp.broadcast_to(flags[None], (8, n))
     bias, gain = forget_bias[None], head_gain[None]
     (
         block_output, first_delta, attn_delta, merged_delta, postgain_grad,
@@ -1040,24 +1075,24 @@
         q, k, v, pre, logits, mixed, aff, mixing, weights, inner, state, passed, pass_all, *wholes,
     ) = front(
         size, heads, hi == 1, shards, flat, cotan, pre_gain[None], post_gain[None],
-        gain, bias, fcol, frow,
+        gain, bias, resets,
     )
     lefts = [hidden_t, second_t, merged_t, normed_t]
     if hi > 1:
         lefts = [by_owner(a, hi, lo) for a in lefts]
     rights = [cotan, gate_delta, up_delta, attn_delta]
     columns = (width, ff, ff, width, width, width, width, width, bias.shape[1])
-    plan = []
-    for i, (name, left) in enumerate(FORM):
-        kept_rows = (ff if i == 0 else width) // (lo * 4)
-        plan.append((left, columns[i], -(-kept_rows // 16) * 16, kept_rows, tuple(cut(columns[i], i % 2))))
+    kept_rows = [(ff if i == 0 else width) // (lo * 4) for i in range(len(FORM))]
+    padded = [-(-r // 16) * 16 for r in kept_rows]
+    pieces = cut(tuple(zip(columns, padded)))
+    plan = [(left, columns[i], padded[i], kept_rows[i], pieces[i]) for i, (_, left) in enumerate(FORM)]
     saved = dict(
         q=q, k=k, v=v, pre=pre, logits=logits, mixed=mixed, aff=aff, mixing=mixing, weights=weights, inner=inner,
         state=state, mdelta=merged_delta, pass_all=pass_all,
     )
     saved["pass"] = passed
     grads, vectors, input_grad = back(
-        size, heads, tuple(plan), lefts, rights, saved, wholes, first_delta, flat, bias, fcol, frow, gain,
+        size, heads, tuple(plan), lefts, rights, saved, wholes, first_delta, flat, bias, resets, gain,
         pre_gain[None], postgain_grad,
     )
     if hi > 1:
@@ -1068,11 +1103,17 @@
         ]
         vectors = lax.psum(vectors, "seq", axis_index_groups=alike)
     down_grad, gate_grad, up_grad, output_grad, outgate_grad, query_grad, key_grad, value_grad, forget_grad = grads
-    pregain, bias_total, headgain, postgain = vectors[0], vectors[1, : bias.shape[1]], vectors[2, :head], vectors[3]
     shape = tokens.shape
+    got = finish(
+        (
+            block_output, input_grad, query_grad, key_grad, value_grad, forget_grad, outgate_grad, output_grad,
+            gate_grad, up_grad, down_grad,
+        ), vectors, (width, bias.shape[1], head, width),
+    )
+    pregain, bias_total, headgain, postgain = got[11:]
     return (
-        block_output.reshape(shape), input_grad.reshape(shape), pregain, query_grad, key_grad, value_grad,
-        forget_grad, bias_total, outgate_grad, output_grad, headgain, postgain, gate_grad, up_grad, down_grad,
+        got[0].reshape(shape), got[1].reshape(shape), pregain, *got[2:6], bias_total, *got[6:8], headgain,
+        postgain, *got[8:11],
     )
 
 

time: 277 us -> 258 us (0.931)
  local copies, waits for them, and re-layouts: 13 us -> 0 us
  Pallas kernels: 262 us -> 257 us
    unnamed x31 -> x0, local copies, waits for them, and re-layouts: 8.85 us -> none
    pallas_call x1, Pallas kernels: 109 us -> 105 us  [front(): pl.pallas_call(functools.partial(front_kernel, size, heads, grouped), nam...]
    pallas_call x1, Pallas kernels: 153 us -> 149 us  [back(): pl.pallas_call(functools.partial(back_kernel, size, heads, plan), name='b...]
    pallas_call x0 -> x1, Pallas kernels: none -> 3.35 us  [finish(): pl.pallas_call(functools.partial(finish_kernel, count), name='finish', ou...]
    slice x2 -> x0, local copies, waits for them, and re-layouts: 2.79 us -> none  [the longest x1 1.44 us: body(): vectors[3]]
where the time goes in v5:
time: 258 us
  Pallas kernels  257 us (100%)
    pallas_call x1, Pallas kernels, back(): pl.pallas_call(functools.partial(back_kernel, size, heads, plan), name='b...  149 us
    pallas_call x1, Pallas kernels, front(): pl.pallas_call(functools.partial(front_kernel, size, heads, grouped), nam...  105 us

profile of v5, /device:TPU:0, one launch (start us, length us, event | category | flops | bytes accessed | tf_op | source)
XLA Modules:
  0.0 258.0 jit_solution(15769639284361089385)
XLA Ops:
  0.6 104.6 %front.1 = (bf16[256,1024]{1,0:T(8,128)(2,1)}, f32[256,1024]{1,0:T(8,128)}, bf16[256,1024]{1,0:T(8,128)(2,1)}, f32[256,1024]{1,0:T(8,128)}, f32[1,1024]{1,0:T(1,...) custom-call(bf16[256,1024]{1,0:T(8,128)(2,1)} %refs_0_.1, ...), custom_call_target="tpu_custom_call" | custom-call | tf_op jit(solution)/shard_map/front/pallas_call | solution.py:494
  105.3 149.2 %back.1 = (f32[88,1024]{1,0:T(8,128)}, f32[32,2816]{1,0:T(8,128)}, f32[32,2816]{1,0:T(8,128)}, f32[32,1024]{1,0:T(8,128)}, f32[32,1024]{1,0:T(8,128)}, /*index=5...) custom-call(bf16[2,1536,256]{2,1,0:T(8,128)(2,1)} %get-tuple-element, ...), custom_call_target="tpu_custom_call" | custom-call | tf_op jit(solution)/shard_map/back/pallas_call | solution.py:1009
  254.5 3.4 %finish.1 = (bf16[256,1024]{1,0:T(8,128)(2,1)}, bf16[256,1024]{1,0:T(8,128)(2,1)}, f32[32,1024]{1,0:T(8,128)}, f32[32,1024]{1,0:T(8,128)}, f32[32,1024]{1,0:T(8,...) custom-call(bf16[256,1024]{1,0:T(8,128)(2,1)} %get-tuple-element.70., ...), custom_call_target="tpu_custom_call" | custom-call | tf_op jit(solution)/shard_map/finish/pallas_call | solution.py:1034

commit v6 on v5

--- a/solution.py
+++ b/solution.py
@@ -129,25 +129,36 @@
 
 
 WEIGHTS = ("key", "value", "forget", "query", "outgate", "output", "gate", "up", "down")
-TWICE = ("gate", "up", "down")
+TWICE = ("output", "gate", "up", "down", "rest")
+PARTS = WEIGHTS + ("rest",)
+
+
+RESULTS = (
+    "block", "first", "attn", "mdelta", "postgain", "normed_t", "merged_t", "second_t", "hidden_t", "gate_delta",
+    "up_delta", "q", "k", "v", "pre", "logits", "mixed", "aff", "mixing", "weights", "inner", "state", "pass", "pass_all",
+)
+SHARED = ("normed_t", "merged_t", "second_t", "hidden_t")
 
 
 def front_kernel(size, heads, grouped, *refs):
     count = len(WEIGHTS)
     shards, refs = dict(zip(WEIGHTS, refs[:count])), refs[count:]
     (tok_ref, cot_ref, pre_gain, post_gain, head_gain, bias_ref, flag_ref), refs = refs[:7], refs[7:]
+    results, refs = dict(zip(RESULTS, refs[: len(RESULTS)])), refs[len(RESULTS) :]
+    passed, refs = dict(zip(WEIGHTS[:5], refs[:5])), refs[5:]
+    held, refs = refs[: len(RESULTS)], refs[len(RESULTS) :]
     (
         out_ref, first_ref, attn_ref, mdelta_ref, postgain_grad,
         normed_t, merged_t, second_t, hidden_t, gate_delta, up_delta,
         q_ref, k_ref, v_ref, pre_ref, logit_ref,
         mixed_ref, aff_ref, mixing_ref, weight_ref, inner_ref, state_ref, pass_ref, pass_all,
-    ), refs = refs[:24], refs[24:]
-    passed, refs = dict(zip(WEIGHTS[:5], refs[:5])), refs[5:]
+    ) = held
+    held = dict(zip(RESULTS, held))
     whole, refs = dict(zip(WEIGHTS, refs[:count])), refs[count:]
     (
         normed, merged, one_ref, second, block_acc, delta_acc, flat_t,
         ends, going, gathered, prefix, came,
-        local, send_sem, recv_sem, away, st_send, st_recv,
+        local, send_sem, recv_sem, away, st_send, st_recv, out_sem, share_send, share_recv,
     ) = refs
     sems = (send_sem, recv_sem)
     s, f = lax.axis_index("seq"), lax.axis_index("fsdp")
@@ -163,23 +174,47 @@
         copy.start()
         started.append(copy)
 
+    leaving = []
+
+    def emit(*names):
+        n = tok_ref.shape[0]
+        for name in names:
+            source, to, i = held[name], results[name], RESULTS.index(name)
+            if grouped and name in SHARED:
+                far_half = to.at[:, pl.ds(n, n)]
+                core = lax.rem(f, 2)
+                j = SHARED.index(name)
+                copy = remote(source.at[1 - core], far_half, (share_send, share_recv), j, sib)
+                copy.start()
+                leaving.append(copy)
+                source, to = source.at[core], to.at[:, pl.ds(0, n)]
+            copy = pltpu.make_async_copy(source, to, out_sem.at[i])
+            copy.start()
+            leaving.append(copy)
+
+    spot = {m: (m, 0, shards[m].shape[0]) for m in WEIGHTS}
+    rows = shards["down"].shape[0]
+    lead = rows // 2 // 64 * 64
+    spot["down"], spot["rest"] = ("down", 0, lead), ("down", lead, rows - lead)
+
     def piece(m, owner, start, length):
-        rows = shards[m].shape[0]
-        return whole[m].at[pl.ds(pl.multiple_of(owner * rows + start, 16), length)]
+        name, first, _ = spot[m]
+        rows = shards[name].shape[0]
+        return whole[name].at[pl.ds(pl.multiple_of(owner * rows + first + start, 16), length)]
 
     def quarter(m, owner, which, half=None):
-        rows = shards[m].shape[0] // 4
+        rows = spot[m][2] // 4
         first = (rows // 2 + 15) // 16 * 16
         start, length = (0, rows) if half is None else ((0, first), (first, rows - first))[half]
         return piece(m, owner, which * rows + start, length)
 
     def eighth(m, owner, bit, half):
-        rows = shards[m].shape[0] // 2
+        rows = spot[m][2] // 2
         return piece(m, owner, bit * rows + half * (rows // 2), rows // 2)
 
     def mine(m, owner):
         if m in TWICE:
-            rows = shards[m].shape[0] // 2
+            rows = spot[m][2] // 2
             return piece(m, owner, kind_bit * rows, rows)
         return quarter(m, owner, q)
 
@@ -190,64 +225,72 @@
         return eighth(m, owner, 1 - kind_bit, 1) if m in TWICE else quarter(m, owner, q ^ 2)
 
     def send(kind, m, part, partner):
-        go(remote(part, part, sems, (kind, WEIGHTS.index(m)), partner))
+        go(remote(part, part, sems, (kind, PARTS.index(m)), partner))
 
     def arrived(kind, m, part):
-        remote(part, part, sems, (kind, WEIGHTS.index(m)), sib).wait_recv()
+        remote(part, part, sems, (kind, PARTS.index(m)), sib).wait_recv()
+
+    for i, m in enumerate(PARTS):
+        name, first, rows = spot[m]
+        if m in TWICE:
+            src = shards[name].at[pl.ds(pl.multiple_of(first + kind_bit * (rows // 2), 16), rows // 2)]
+        else:
+            src = shards[name].at[pl.ds(pl.multiple_of(first + q * (rows // 4), 16), rows // 4)]
+        go(remote(src, mine(m, f), sems, (1, i), far))
+
+    def own_rows(m, owner):
+        rows = shards[m].shape[0]
+        return whole[m].at[pl.ds(pl.multiple_of(owner * rows, 16), rows)]
 
     own = {}
     for i, m in enumerate(WEIGHTS):
-        rows = shards[m].shape[0]
+        go(remote(shards[m], own_rows(m, f), sems, (0, i), sib))
+        own[m] = pltpu.make_async_copy(shards[m], own_rows(m, f), local.at[i])
+        own[m].start()
+
+    def pass_first(m):
+        part = mine(m, fy)
+        arrived(1, m, part)
         if m in TWICE:
-            src = shards[m].at[pl.ds(pl.multiple_of(kind_bit * (rows // 2), 16), rows // 2)]
+            send(2, m, eighth(m, fy, kind_bit, 0), nx)
+            send(3, m, eighth(m, fy, kind_bit, 1), nz)
         else:
-            src = shards[m].at[pl.ds(pl.multiple_of(q * (rows // 4), 16), rows // 4)]
-        go(remote(src, mine(m, f), sems, (1, i), far))
-    for i, m in enumerate(WEIGHTS):
-        rows = shards[m].shape[0]
-        go(remote(shards[m], piece(m, f, 0, rows), sems, (0, i), sib))
-        own[m] = pltpu.make_async_copy(shards[m], piece(m, f, 0, rows), local.at[i])
-        own[m].start()
+            send(2, m, part, nx)
+            send(3, m, part, nz)
+        send(6, m, part, sib)
+
+    def pass_second(m):
+        arrived(2, m, from_x(m, fy))
+        if m not in TWICE:
+            send(4, m, quarter(m, fy, q ^ 1, 0), nz)
+        send(7, m, from_x(m, fy), sib)
+        arrived(3, m, from_z(m, fy))
+        if m not in TWICE:
+            send(5, m, quarter(m, fy, q ^ 2, 1), nx)
+        send(8, m, from_z(m, fy), sib)
+
+    def pass_third(m):
+        if m not in TWICE:
+            for kind in (4, 5):
+                part = quarter(m, fy, q ^ 3, kind - 4)
+                arrived(kind, m, part)
+                send(kind + 5, m, part, sib)
 
     def pump(step):
-        if step < count:
-            m = WEIGHTS[step]
-            part = mine(m, fy)
-            arrived(1, m, part)
-            if m in TWICE:
-                send(2, m, eighth(m, fy, kind_bit, 0), nx)
-                send(3, m, eighth(m, fy, kind_bit, 1), nz)
-            else:
-                send(2, m, part, nx)
-                send(3, m, part, nz)
-            send(6, m, part, sib)
-        if 0 <= step - 1 < count:
-            m = WEIGHTS[step - 1]
-            arrived(2, m, from_x(m, fy))
-            if m not in TWICE:
-                send(4, m, quarter(m, fy, q ^ 1, 0), nz)
-            send(7, m, from_x(m, fy), sib)
-            arrived(3, m, from_z(m, fy))
-            if m not in TWICE:
-                send(5, m, quarter(m, fy, q ^ 2, 1), nx)
-            send(8, m, from_z(m, fy), sib)
-        if 0 <= step - 2 < count:
-            m = WEIGHTS[step - 2]
-            if m not in TWICE:
-                for kind in (4, 5):
-                    part = quarter(m, fy, q ^ 3, kind - 4)
-                    arrived(kind, m, part)
-                    send(kind + 5, m, part, sib)
+        for late, stage in enumerate((pass_first, pass_second, pass_third)):
+            if 0 <= step - late < len(PARTS):
+                stage(PARTS[step - late])
 
     def ready(m):
         own[m].wait()
-        arrived(0, m, piece(m, f ^ 1, 0, shards[m].shape[0]))
-        arrived(6, m, mine(m, fs))
-        arrived(7, m, from_x(m, fs))
-        arrived(8, m, from_z(m, fs))
-        if m not in TWICE:
-            arrived(9, m, quarter(m, fs, q ^ 3, 0))
-            arrived(10, m, quarter(m, fs, q ^ 3, 1))
+        arrived(0, m, own_rows(m, f ^ 1))
+        for part in ("down", "rest") if m == "down" else (m,):
+            arrived(6, part, mine(part, fs))
+            arrived(7, part, from_x(part, fs))
+            arrived(8, part, from_z(part, fs))
+            if part not in TWICE:
+                arrived(9, part, quarter(part, fs, q ^ 3, 0))
+                arrived(10, part, quarter(part, fs, q ^ 3, 1))
 
     n, width = tok_ref.shape
     head = width // heads
@@ -285,11 +328,13 @@
     scaled = unit * pre_gain[...]
     normed[...] = scaled.astype(bf16)
     turn_over(scaled.T, normed_t, width // 32, width // 32)
+    emit("normed_t")
     for step in range(5):
         pump(step)
     for m, to_ref in (("key", k_ref), ("value", v_ref), ("forget", pre_ref)):
         ready(m)
         project(m, to_ref)
+    emit("k", "v", "pre")
     lower, linked, fresh, ending, unbroken = mask_set(flag_ref[...])
     z, u, oma, growth, inverse, tail = gate_set(pre_ref[...], bias_ref[...], lower, ending)
     shrink, kept = inverse * oma, tail * oma
@@ -334,6 +379,7 @@
     for m, to_ref in (("query", q_ref), ("outgate", logit_ref)):
         ready(m)
         project(m, to_ref)
+    emit("q", "logits", "pass")
     for i, m in enumerate(WEIGHTS[:5]):
         copy = pltpu.make_async_copy(whole[m], passed[m], away.at[i])
         copy.start()
@@ -351,14 +397,15 @@
         to = others[d - 1]
         go(remote(prefix.at[to[0]], came.at[rows_for(s)], (st_send, st_recv), (1, d - 1), to))
     came[rows_for(s)] = prefix[s]
+    emit("pass_all")
     pump(7)
     for h in range(heads):
         hd = slice(h * head, (h + 1) * head)
         aff_ref[h] = (dot(q_ref[:, hd], k_ref[:, hd], 1, 1) * (linked * scale)).astype(bf16)
+    emit("aff")
     for d in range(1, size):
         part = came.at[rows_for(first_hop[d - 1])]
         remote(part, part, (st_send, st_recv), (1, d - 1), sib).wait_recv()
-    pump(8)
     for h in range(heads):
         hs, hd = slice(h * slots, (h + 1) * slots), slice(h * head, (h + 1) * head)
         for stream in range(streams):
@@ -400,6 +447,9 @@
         logits = logit_ref[:, hd]
         delta_acc[:, hd] = mixed * r * head_gain[...] * (logits * sigmoid(logits))
         merged[:, hd] = delta_acc[:, hd].astype(bf16)
+    emit("mixed", "mixing", "weights", "inner", "state")
+    pass_first("down")
+    pass_second("up")
     ready("output")
 
     def join(at):
@@ -407,39 +457,50 @@
 
     across(width, join)
     turn_over(delta_acc[...].T, merged_t, width // 32, width // 32)
+    emit("merged_t")
     one = one_ref[...]
     scaled = one * lax.rsqrt(jnp.mean(one * one, axis=1, keepdims=True) + norm_eps) * post_gain[...]
     second[...] = scaled.astype(bf16)
     turn_over(scaled.T, second_t, width // 32, width // 32)
-    pump(9)
-    pump(10)
+    emit("second_t")
+    pass_first("rest")
     ready("gate")
     ready("up")
-    ready("down")
     block_acc[...] = one
     delta_acc[...] = jnp.zeros_like(delta_acc)
+
+    def open_tile(i, carry):
+        at = pl.ds(pl.multiple_of(i * TILE, TILE), TILE)
+        gate_vals, up_vals = dot(second[...], whole["gate"][:, at]), dot(second[...], whole["up"][:, at])
+        sig = sigmoid(gate_vals)
+        silu = gate_vals * sig
+        flat_t[at] = (silu * up_vals).T
+        up_delta[:, at] = silu.astype(bf16)
+        gate_delta[:, at] = (up_vals * (sig + silu * (1.0 - sig))).astype(bf16)
+        return carry
 
     def unit_tile(i, carry):
         at = pl.ds(pl.multiple_of(i * TILE, TILE), TILE)
         w_gate, w_up, w_down = whole["gate"][:, at], whole["up"][:, at], whole["down"][at]
-        gate_vals, up_vals = dot(second[...], w_gate), dot(second[...], w_up)
-        sig = sigmoid(gate_vals)
-        silu = gate_vals * sig
-        full = silu * up_vals
-        flat_t[at] = full.T
         hidden_delta = dot(cot_ref[...], w_down, 1, 1)
-        d_up = (hidden_delta * silu).astype(bf16)
-        d_gate = (hidden_delta * up_vals * (sig + silu * (1.0 - sig))).astype(bf16)
+        d_up = (hidden_delta * up_delta[:, at].astype(f32)).astype(bf16)
+        d_gate = (hidden_delta * gate_delta[:, at].astype(f32)).astype(bf16)
         gate_delta[:, at] = d_gate
         up_delta[:, at] = d_up
-        block_acc[...] += dot(full, w_down)
+        block_acc[...] += dot(flat_t[at].astype(bf16), w_down, 0, 0)
         delta_acc[...] += dot(d_gate, w_gate, 1, 1) + dot(d_up, w_up, 1, 1)
         return carry
 
-    ff = whole["down"].shape[0]
+    ff = whole["gate"].shape[1]
+    lax.fori_loop(0, ff // TILE, open_tile, 0)
+    turn_over(flat_t, hidden_t, ff // 32, -(-(ff // 32) // 16) * 16)
+    emit("hidden_t")
+    pass_second("down")
+    pass_second("rest")
+    ready("down")
     lax.fori_loop(0, ff // TILE, unit_tile, 0)
     out_ref[...] = block_acc[...].astype(bf16)
-    turn_over(flat_t, hidden_t, ff // 32, -(-(ff // 32) // 16) * 16)
+    emit("block", "gate_delta", "up_delta")
     one = one_ref[...]
     r = lax.rsqrt(jnp.mean(one * one, axis=1, keepdims=True) + norm_eps)
     unit = one * r
@@ -449,11 +510,15 @@
     first = cot_ref[...].astype(f32) + r * (delta - unit * jnp.mean(unit * delta, axis=1, keepdims=True))
     first_ref[...] = first
     attn_ref[...] = first.astype(bf16)
+    emit("postgain", "first", "attn")
 
     def split(at):
         mdelta_ref[:, at] = dot(attn_ref[...], whole["output"][at], 1, 1)
 
     across(width, split)
+    emit("mdelta")
+    for copy in leaving:
+        copy.wait()
     for m in WEIGHTS[:5]:
         own[m].wait()
     for copy in started:
@@ -470,8 +535,7 @@
     padded = -(-(ff // 32) // 16) * 512
 
     def turned(rows, grouped_rows):
-        shape = (2, grouped_rows // 2, n) if grouped else (rows, n)
-        return jax.ShapeDtypeStruct(shape, bf16)
+        return low(grouped_rows // 2, 2 * n) if grouped else low(rows, n)
 
     def low(*shape):
         return jax.ShapeDtypeStruct(shape, bf16)
@@ -489,6 +553,9 @@
         low(size, pairs * slots // size, 128),
     ]
     wholes = [low(4 * w.shape[0], w.shape[1]) for w in shards]
+    keeps = [
+        (2, o.shape[0], n) if grouped and name in SHARED else o.shape for name, o in zip(RESULTS, outs)
+    ]
     share = pairs * slots // size
     dma = pltpu.SemaphoreType.DMA
     got = pl.pallas_call(
@@ -496,8 +563,9 @@
         name="front",
         out_shape=outs + wholes[:5],
         in_specs=[in_place()] * count + [in_vmem()] * 7,
-        out_specs=[in_vmem()] * len(outs) + [in_place()] * 5,
-        scratch_shapes=[VMEM(w.shape, bf16) for w in wholes]
+        out_specs=[in_place()] * (len(outs) + 5),
+        scratch_shapes=[VMEM(shape, o.dtype) for shape, o in zip(keeps, outs)]
+        + [VMEM(w.shape, bf16) for w in wholes]
         + [
             VMEM((n, width), bf16),
             VMEM((n, width), bf16),
@@ -512,11 +580,14 @@
             VMEM((size, share, 2 * head), bf16),
             VMEM((pairs * slots, 2 * head), bf16),
             dma((count,)),
-            dma((11, count)),
-            dma((11, count)),
+            dma((11, len(PARTS))),
+            dma((11, len(PARTS))),
             dma((5,)),
             dma((2, size - 1)),
             dma((2, size - 1)),
+            dma((len(RESULTS),)),
+            dma((len(SHARED),)),
+            dma((len(SHARED),)),
         ],
         compiler_params=pltpu.CompilerParams(
             collective_id=1, has_side_effects=True, vmem_limit_bytes=LIMIT
@@ -667,6 +738,11 @@
     waiting = {}
 
     def fetch_left(i):
+        if len(lefts[i].shape) == 2:
+            keep = pltpu.make_async_copy(lefts[i], left_all[i], in_local.at[i])
+            keep.start()
+            waiting["left", i] = [keep, None]
+            return
         keep = pltpu.make_async_copy(lefts[i].at[core], left_all[i].at[:, pl.ds(0, n)], in_local.at[i])
         keep.start()
         copy = remote(lefts[i].at[1 - core], left_all[i].at[:, pl.ds(n, n)], (in_send, in_recv), i, sib)
@@ -690,7 +766,8 @@
         if pair:
             if pair[0] is not None:
                 pair[0].wait()
-            pair[1].wait_recv()
+            if pair[1] is not None:
+                pair[1].wait_recv()
             waiting[kind, i] = None
 
     fetch_left(0)
@@ -977,7 +1054,7 @@
     nc = len(chunks)
     dma = pltpu.SemaphoreType.DMA
     saved = [saved[name] for name in SAVED]
-    scratch = [VMEM((a.shape[1], 2 * n), bf16) for a in lefts]
+    scratch = [VMEM((a.shape[-2], 2 * n), bf16) for a in lefts]
     scratch += [VMEM((2 * n, p[1]), bf16) for p in plan]
     scratch += [VMEM(a.shape, a.dtype) for a in saved]
     for lead in ((2, 2, 2, 2), (2, 2, 2), (2, 2), (2,), ()):

time: 258 us -> 252 us (0.977)
  Pallas kernels: 257 us -> 251 us
    pallas_call x1, Pallas kernels: 105 us -> 98.1 us  [front(): pl.pallas_call(functools.partial(front_kernel, size, heads, grouped), nam...]
where the time goes in v6:
time: 252 us
  Pallas kernels  251 us (100%)
    pallas_call x1, Pallas kernels, back(): pl.pallas_call(functools.partial(back_kernel, size, heads, plan), name='b...  150 us
    pallas_call x1, Pallas kernels, front(): pl.pallas_call(functools.partial(front_kernel, size, heads, grouped), nam...  98.1 us

profile of v6, /device:TPU:0, one launch (start us, length us, event | category | flops | bytes accessed | tf_op | source)
XLA Modules:
  0.0 251.9 jit_solution(11584464179595031082)
XLA Ops:
  0.6 98.1 %front.1 = (bf16[256,1024]{1,0:T(8,128)(2,1)}, f32[256,1024]{1,0:T(8,128)}, bf16[256,1024]{1,0:T(8,128)(2,1)}, f32[256,1024]{1,0:T(8,128)}, f32[1,1024]{1,0:T(1,...) custom-call(bf16[256,1024]{1,0:T(8,128)(2,1)} %refs_0_.1, ...), custom_call_target="tpu_custom_call" | custom-call | tf_op jit(solution)/shard_map/front/pallas_call | solution.py:561
  98.8 149.6 %back.1 = (f32[88,1024]{1,0:T(8,128)}, f32[32,2816]{1,0:T(8,128)}, f32[32,2816]{1,0:T(8,128)}, f32[32,1024]{1,0:T(8,128)}, f32[32,1024]{1,0:T(8,128)}, /*index=5...) custom-call(bf16[1536,512]{1,0:T(8,128)(2,1)} %get-tuple-element.71., ...), custom_call_target="tpu_custom_call" | custom-call | tf_op jit(solution)/shard_map/back/pallas_call | solution.py:1086
  248.4 3.4 %finish.1 = (bf16[256,1024]{1,0:T(8,128)(2,1)}, bf16[256,1024]{1,0:T(8,128)(2,1)}, f32[32,1024]{1,0:T(8,128)}, f32[32,1024]{1,0:T(8,128)}, f32[32,1024]{1,0:T(8,...) custom-call(bf16[256,1024]{1,0:T(8,128)(2,1)} %get-tuple-element.70., ...), custom_call_target="tpu_custom_call" | custom-call | tf_op jit(solution)/shard_map/finish/pallas_call | solution.py:1111

commit v7 on v6

--- a/solution.py
+++ b/solution.py
@@ -133,27 +133,22 @@
 PARTS = WEIGHTS + ("rest",)
 
 
-RESULTS = (
-    "block", "first", "attn", "mdelta", "postgain", "normed_t", "merged_t", "second_t", "hidden_t", "gate_delta",
-    "up_delta", "q", "k", "v", "pre", "logits", "mixed", "aff", "mixing", "weights", "inner", "state", "pass", "pass_all",
-)
-SHARED = ("normed_t", "merged_t", "second_t", "hidden_t")
+RESULTS, SHARED = 24, (5, 6, 7, 8)
 
 
 def front_kernel(size, heads, grouped, *refs):
     count = len(WEIGHTS)
     shards, refs = dict(zip(WEIGHTS, refs[:count])), refs[count:]
     (tok_ref, cot_ref, pre_gain, post_gain, head_gain, bias_ref, flag_ref), refs = refs[:7], refs[7:]
-    results, refs = dict(zip(RESULTS, refs[: len(RESULTS)])), refs[len(RESULTS) :]
+    results, refs = refs[:RESULTS], refs[RESULTS:]
     passed, refs = dict(zip(WEIGHTS[:5], refs[:5])), refs[5:]
-    held, refs = refs[: len(RESULTS)], refs[len(RESULTS) :]
+    held, refs = refs[:RESULTS], refs[RESULTS:]
     (
         out_ref, first_ref, attn_ref, mdelta_ref, postgain_grad,
         normed_t, merged_t, second_t, hidden_t, gate_delta, up_delta,
         q_ref, k_ref, v_ref, pre_ref, logit_ref,
         mixed_ref, aff_ref, mixing_ref, weight_ref, inner_ref, state_ref, pass_ref, pass_all,
     ) = held
-    held = dict(zip(RESULTS, held))
     whole, refs = dict(zip(WEIGHTS, refs[:count])), refs[count:]
     (
         normed, merged, one_ref, second, block_acc, delta_acc, flat_t,
@@ -176,14 +171,15 @@
 
     leaving = []
 
-    def emit(*names):
+    def emit(*sources):
         n = tok_ref.shape[0]
-        for name in names:
-            source, to, i = held[name], results[name], RESULTS.index(name)
-            if grouped and name in SHARED:
+        for source in sources:
+            i = next(k for k, ref in enumerate(held) if ref is source)
+            to = results[i]
+            if grouped and i in SHARED:
                 far_half = to.at[:, pl.ds(n, n)]
                 core = lax.rem(f, 2)
-                j = SHARED.index(name)
+                j = SHARED.index(i)
                 copy = remote(source.at[1 - core], far_half, (share_send, share_recv), j, sib)
                 copy.start()
                 leaving.append(copy)
@@ -328,13 +324,13 @@
     scaled = unit * pre_gain[...]
     normed[...] = scaled.astype(bf16)
     turn_over(scaled.T, normed_t, width // 32, width // 32)
-    emit("normed_t")
+    emit(normed_t)
     for step in range(5):
         pump(step)
     for m, to_ref in (("key", k_ref), ("value", v_ref), ("forget", pre_ref)):
         ready(m)
         project(m, to_ref)
-    emit("k", "v", "pre")
+    emit(k_ref, v_ref, pre_ref)
     lower, linked, fresh, ending, unbroken = mask_set(flag_ref[...])
     z, u, oma, growth, inverse, tail = gate_set(pre_ref[...], bias_ref[...], lower, ending)
     shrink, kept = inverse * oma, tail * oma
@@ -379,7 +375,7 @@
     for m, to_ref in (("query", q_ref), ("outgate", logit_ref)):
         ready(m)
         project(m, to_ref)
-    emit("q", "logits", "pass")
+    emit(q_ref, logit_ref, pass_ref)
     for i, m in enumerate(WEIGHTS[:5]):
         copy = pltpu.make_async_copy(whole[m], passed[m], away.at[i])
         copy.start()
@@ -397,12 +393,12 @@
         to = others[d - 1]
         go(remote(prefix.at[to[0]], came.at[rows_for(s)], (st_send, st_recv), (1, d - 1), to))
     came[rows_for(s)] = prefix[s]
-    emit("pass_all")
+    emit(pass_all)
     pump(7)
     for h in range(heads):
         hd = slice(h * head, (h + 1) * head)
         aff_ref[h] = (dot(q_ref[:, hd], k_ref[:, hd], 1, 1) * (linked * scale)).astype(bf16)
-    emit("aff")
+    emit(aff_ref)
     for d in range(1, size):
         part = came.at[rows_for(first_hop[d - 1])]
         remote(part, part, (st_send, st_recv), (1, d - 1), sib).wait_recv()
@@ -447,7 +443,7 @@
         logits = logit_ref[:, hd]
         delta_acc[:, hd] = mixed * r * head_gain[...] * (logits * sigmoid(logits))
         merged[:, hd] = delta_acc[:, hd].astype(bf16)
-    emit("mixed", "mixing", "weights", "inner", "state")
+    emit(mixed_ref, mixing_ref, weight_ref, inner_ref, state_ref)
     pass_first("down")
     pass_second("up")
     ready("output")
@@ -457,12 +453,12 @@
 
     across(width, join)
     turn_over(delta_acc[...].T, merged_t, width // 32, width // 32)
-    emit("merged_t")
+    emit(merged_t)
     one = one_ref[...]
     scaled = one * lax.rsqrt(jnp.mean(one * one, axis=1, keepdims=True) + norm_eps) * post_gain[...]
     second[...] = scaled.astype(bf16)
     turn_over(scaled.T, second_t, width // 32, width // 32)
-    emit("second_t")
+    emit(second_t)
     pass_first("rest")
     ready("gate")
     ready("up")
@@ -494,13 +490,13 @@
     ff = whole["gate"].shape[1]
     lax.fori_loop(0, ff // TILE, open_tile, 0)
     turn_over(flat_t, hidden_t, ff // 32, -(-(ff // 32) // 16) * 16)
-    emit("hidden_t")
+    emit(hidden_t)
     pass_second("down")
     pass_second("rest")
     ready("down")
     lax.fori_loop(0, ff // TILE, unit_tile, 0)
     out_ref[...] = block_acc[...].astype(bf16)
-    emit("block", "gate_delta", "up_delta")
+    emit(out_ref, gate_delta, up_delta)
     one = one_ref[...]
     r = lax.rsqrt(jnp.mean(one * one, axis=1, keepdims=True) + norm_eps)
     unit = one * r
@@ -510,13 +506,13 @@
     first = cot_ref[...].astype(f32) + r * (delta - unit * jnp.mean(unit * delta, axis=1, keepdims=True))
     first_ref[...] = first
     attn_ref[...] = first.astype(bf16)
-    emit("postgain", "first", "attn")
+    emit(postgain_grad, first_ref, attn_ref)
 
     def split(at):
         mdelta_ref[:, at] = dot(attn_ref[...], whole["output"][at], 1, 1)
 
     across(width, split)
-    emit("mdelta")
+    emit(mdelta_ref)
     for copy in leaving:
         copy.wait()
     for m in WEIGHTS[:5]:
@@ -554,7 +550,7 @@
     ]
     wholes = [low(4 * w.shape[0], w.shape[1]) for w in shards]
     keeps = [
-        (2, o.shape[0], n) if grouped and name in SHARED else o.shape for name, o in zip(RESULTS, outs)
+        (2, o.shape[0], n) if grouped and i in SHARED else o.shape for i, o in enumerate(outs)
     ]
     share = pairs * slots // size
     dma = pltpu.SemaphoreType.DMA
@@ -585,7 +581,7 @@
             dma((5,)),
             dma((2, size - 1)),
             dma((2, size - 1)),
-            dma((len(RESULTS),)),
+            dma((RESULTS,)),
             dma((len(SHARED),)),
             dma((len(SHARED),)),
         ],
@@ -603,7 +599,7 @@
     return jnp.sum(jnp.where(i == j, jnp.broadcast_to(col, (n, n)), 0.0), axis=0, keepdims=True)
 
 
-LEAST, SHALLOW, DEEP = 4.0, 8.0, 10.0
+LEAST, SHALLOW, DEEP = 4.0, 8.0, 12.0
 STRIPS = 3
 BACK_LIMIT = 63 * 2**20
 
@@ -641,7 +637,7 @@
     now, free = 0.0, dict.fromkeys(("x", "y", "z", "zz"), 0.0)
     came, done, coming, out = {}, set(), [], []
     path, left = list(path), list(range(len(chunks)))
-    rate, delay = 0.045, 2.0
+    rate, delay = 0.04, 4.0
 
     def leave(c, stage):
         rows, width, order = chunks[c][1], chunks[c][3], chunks[c][4]

time: 252 us -> 251 us (level)
  no operation moved by 1% of the time
where the time goes in v7:
time: 251 us; the launch traced here: 250 us
  Pallas kernels  249 us (99%)
    pallas_call x1, Pallas kernels, back(): pl.pallas_call(functools.partial(back_kernel, size, heads, plan), name='b...  148 us
    pallas_call x1, Pallas kernels, front(): pl.pallas_call(functools.partial(front_kernel, size, heads, grouped), nam...  98.1 us

profile of v7, /device:TPU:0, one launch (start us, length us, event | category | flops | bytes accessed | tf_op | source)
XLA Modules:
  0.0 250.2 jit_solution(15382443718114678501)
XLA Ops:
  0.6 98.1 %front.1 = (bf16[256,1024]{1,0:T(8,128)(2,1)}, f32[256,1024]{1,0:T(8,128)}, bf16[256,1024]{1,0:T(8,128)(2,1)}, f32[256,1024]{1,0:T(8,128)}, f32[1,1024]{1,0:T(1,...) custom-call(bf16[256,1024]{1,0:T(8,128)(2,1)} %refs_0_.1, ...), custom_call_target="tpu_custom_call" | custom-call | tf_op jit(solution)/shard_map/front/pallas_call | solution.py:557
  98.8 147.9 %back.1 = (f32[88,1024]{1,0:T(8,128)}, f32[32,2816]{1,0:T(8,128)}, f32[32,2816]{1,0:T(8,128)}, f32[32,1024]{1,0:T(8,128)}, f32[32,1024]{1,0:T(8,128)}, /*index=5...) custom-call(bf16[1536,512]{1,0:T(8,128)(2,1)} %get-tuple-element.71., ...), custom_call_target="tpu_custom_call" | custom-call | tf_op jit(solution)/shard_map/back/pallas_call | solution.py:1082
  246.7 3.4 %finish.1 = (bf16[256,1024]{1,0:T(8,128)(2,1)}, bf16[256,1024]{1,0:T(8,128)(2,1)}, f32[32,1024]{1,0:T(8,128)}, f32[32,1024]{1,0:T(8,128)}, f32[32,1024]{1,0:T(8,...) custom-call(bf16[256,1024]{1,0:T(8,128)(2,1)} %get-tuple-element.70., ...), custom_call_target="tpu_custom_call" | custom-call | tf_op jit(solution)/shard_map/finish/pallas_call | solution.py:1107

commit v8 on v7

--- a/solution.py
+++ b/solution.py
@@ -605,7 +605,7 @@
 
 
 ROUTES = (("y", "z", "x", "zz"), ("x", "z", "y", "zz"), ("y", "x", "z", "zz"), ("x", "y", "z", "zz"))
-STATES = {"x": 1.15, "y": 0.0, "z": 1.75}
+STATES = {"x": 1.15, "y": 0.0, "z": 0.5}
 
 
 def cut(sizes):

time: 251 us -> 248 us (0.988)
  no operation moved by 1% of the time
where the time goes in v8:
time: 248 us
  Pallas kernels  247 us (100%)
    pallas_call x1, Pallas kernels, back(): pl.pallas_call(functools.partial(back_kernel, size, heads, plan), name='b...  146 us
    pallas_call x1, Pallas kernels, front(): pl.pallas_call(functools.partial(front_kernel, size, heads, grouped), nam...  98.1 us

profile of v8, /device:TPU:0, one launch (start us, length us, event | category | flops | bytes accessed | tf_op | source)
XLA Modules:
  0.0 247.9 jit_solution(13982192332403292076)
XLA Ops:
  0.6 98.1 %front.1 = (bf16[256,1024]{1,0:T(8,128)(2,1)}, f32[256,1024]{1,0:T(8,128)}, bf16[256,1024]{1,0:T(8,128)(2,1)}, f32[256,1024]{1,0:T(8,128)}, f32[1,1024]{1,0:T(1,...) custom-call(bf16[256,1024]{1,0:T(8,128)(2,1)} %refs_0_.1, ...), custom_call_target="tpu_custom_call" | custom-call | tf_op jit(solution)/shard_map/front/pallas_call | solution.py:557
  98.8 145.6 %back.1 = (f32[88,1024]{1,0:T(8,128)}, f32[32,2816]{1,0:T(8,128)}, f32[32,2816]{1,0:T(8,128)}, f32[32,1024]{1,0:T(8,128)}, f32[32,1024]{1,0:T(8,128)}, /*index=5...) custom-call(bf16[1536,512]{1,0:T(8,128)(2,1)} %get-tuple-element.71., ...), custom_call_target="tpu_custom_call" | custom-call | tf_op jit(solution)/shard_map/back/pallas_call | solution.py:1082
  244.4 3.4 %finish.1 = (bf16[256,1024]{1,0:T(8,128)(2,1)}, bf16[256,1024]{1,0:T(8,128)(2,1)}, f32[32,1024]{1,0:T(8,128)}, f32[32,1024]{1,0:T(8,128)}, f32[32,1024]{1,0:T(8,...) custom-call(bf16[256,1024]{1,0:T(8,128)(2,1)} %get-tuple-element.70., ...), custom_call_target="tpu_custom_call" | custom-call | tf_op jit(solution)/shard_map/finish/pallas_call | solution.py:1107
